TPU v7x, 512 devices: a whole 4x4x16 slice. The times are simulated.
512 devices in a mesh: dp: 16 (over x, y_lo, core), mp: 32 (over z, y_hi).
Axes of the slice: x: 4, y: 4 (y_hi: 2, y_lo: 2; y = y_hi * 2 + y_lo), z: 16, core: 2. Of those that a mesh axis runs over, the one named last changes fastest.
Arguments:
- tokens: bfloat16 [4096, 3072], P('dp'), may hold values from -6 to 6
- layer_norm_gain: float32 [3072], replicated, may hold values from 0.5 to 1.5
- w_qkv: bfloat16 [3072, 12288], P('dp', 'mp'), may hold values from -0.109375 to 0.109375
- q_gain: float32 [32, 128], P('mp'), may hold values from 0.5 to 1.5
- k_gain: float32 [32, 128], P('mp'), may hold values from 0.5 to 1.5
- ctx_grad: bfloat16 [4096, 4096], P('dp', 'mp'), may hold values from -12 to 12
Outputs:
- context: bfloat16 [4096, 4096], P('dp', 'mp')
- input_gradient_rows: bfloat16 [4096, 3072], P('dp', 'mp')
- layer_norm_gain_gradient: float32 [3072], P('mp')
- w_grad: bfloat16 [3072, 12288], P('dp', 'mp')
- q_gain_grad: float32 [32, 128], P('mp')
- k_gain_grad: float32 [32, 128], P('mp')
All inputs are finite; a program needn't handle non-finite values.
Results may differ from a plain program's by a relative error of at most 0.025.
Values may be sent and summed in bfloat16 or wider, within the bound.
No kernel may reach another device: no remote copies, remote signals or barrier semaphores. Data moves between devices by JAX's collectives and lax.ppermute only.
A program may use at most 64 MiB of HBM per device.

v0:
```python
import jax
import jax.numpy as jnp
from jax import lax
from jax.sharding import PartitionSpec as P

PATCHES = 256


def head_norm(raw):
    centered_input = raw - jnp.mean(raw, axis=-1, keepdims=True)
    inverse_deviation = lax.rsqrt(
        jnp.mean(centered_input * centered_input, axis=-1, keepdims=True) + 1e-06
    )
    return (centered_input * inverse_deviation, inverse_deviation)


def norm_backward_pass(grad_hat, normal, inverse_deviation):
    first = jnp.mean(grad_hat, axis=-1, keepdims=True)
    second = jnp.mean(grad_hat * normal, axis=-1, keepdims=True)
    return (grad_hat - first - normal * second) * inverse_deviation


def attend(query_raw, key_raw, value_raw, grad, q_gain, k_gain):
    head_size = query_raw.shape[-1]
    scale = head_size ** (-0.5)
    qhat, q_inv = head_norm(query_raw)
    khat, k_inv = head_norm(key_raw)
    q_norm = (qhat * q_gain).astype(jnp.bfloat16)
    k_norm = (khat * k_gain).astype(jnp.bfloat16)
    value = value_raw.astype(jnp.bfloat16)
    scores = (
        jnp.einsum("...qhd,...khd->...hqk", q_norm, k_norm, preferred_element_type=jnp.float32)
        * scale
    )
    expo = jnp.exp(scores)
    probs = expo / jnp.sum(expo, axis=-1, keepdims=True)
    probs_b = probs.astype(jnp.bfloat16)
    context = jnp.einsum(
        "...hqk,...khd->...qhd", probs_b, value, preferred_element_type=jnp.float32
    ).astype(jnp.bfloat16)
    dprob = jnp.einsum("...qhd,...khd->...hqk", grad, value, preferred_element_type=jnp.float32)
    dvalue = jnp.einsum(
        "...hqk,...qhd->...khd", probs_b, grad, preferred_element_type=jnp.float32
    ).astype(jnp.bfloat16)
    dscore = (probs * (dprob - jnp.sum(probs * dprob, axis=-1, keepdims=True)) * scale).astype(
        jnp.bfloat16
    )
    dqn = jnp.einsum("...hqk,...khd->...qhd", dscore, k_norm, preferred_element_type=jnp.float32)
    dkn = jnp.einsum("...hqk,...qhd->...khd", dscore, q_norm, preferred_element_type=jnp.float32)
    lead = tuple(range(dqn.ndim - 2))
    q_part = jnp.sum(dqn * qhat, axis=lead)
    k_part = jnp.sum(dkn * khat, axis=lead)
    dquery = norm_backward_pass(dqn * q_gain, qhat, q_inv).astype(jnp.bfloat16)
    dkey = norm_backward_pass(dkn * k_gain, khat, k_inv).astype(jnp.bfloat16)
    return (context, dquery, dkey, dvalue, q_part, k_part)


def per_device(tokens, layer_norm_gain, w_qkv, q_gain, k_gain, ctx_grad):
    tok_rows, feature_width = tokens.shape
    heads_here, head_size = q_gain.shape
    images = tok_rows // PATCHES
    columns = w_qkv.shape[1]
    x_float = tokens.astype(jnp.float32)
    centered_input = x_float - jnp.mean(x_float, axis=-1, keepdims=True)
    inverse_deviation = lax.rsqrt(
        jnp.mean(centered_input * centered_input, axis=-1, keepdims=True) + 1e-06
    )
    standardized_input = centered_input * inverse_deviation
    normed_input = (standardized_input * layer_norm_gain).astype(jnp.bfloat16)
    full_cols = lax.all_gather(w_qkv, "dp", axis=0, tiled=True)
    qkv = jnp.dot(normed_input, full_cols, preferred_element_type=jnp.float32)
    qkv = qkv.reshape(images, PATCHES, heads_here, 3, head_size)
    grads = ctx_grad.reshape(images, PATCHES, heads_here, head_size)
    context, dquery, dkey, dvalue, q_part, k_part = attend(
        qkv[:, :, :, 0], qkv[:, :, :, 1], qkv[:, :, :, 2], grads, q_gain, k_gain
    )
    context = context.reshape(tok_rows, heads_here * head_size)
    dqkv = jnp.stack([dquery, dkey, dvalue], axis=3).reshape(tok_rows, columns)
    w_grad = lax.psum_scatter(
        lax.dot_general(
            normed_input, dqkv, (((0,), (0,)), ((), ())), preferred_element_type=jnp.float32
        ).astype(jnp.bfloat16),
        "dp",
        scatter_dimension=0,
        tiled=True,
    )
    partial_in = lax.dot_general(
        dqkv, full_cols, (((1,), (1,)), ((), ())), preferred_element_type=jnp.float32
    )
    normed_gradient_share = lax.psum_scatter(
        partial_in.astype(jnp.bfloat16), "mp", scatter_dimension=1, tiled=True
    ).astype(jnp.float32)
    local_share = normed_gradient_share.shape[1]
    leading_column = lax.axis_index("mp") * local_share
    standardized_share = lax.dynamic_slice_in_dim(
        standardized_input, leading_column, local_share, 1
    )
    gain_share = lax.dynamic_slice_in_dim(layer_norm_gain, leading_column, local_share, 0)
    scaled_input = normed_gradient_share * gain_share
    plain_gradient_sum, cross_term_sum = lax.psum(
        (
            jnp.sum(scaled_input, axis=-1, keepdims=True),
            jnp.sum(scaled_input * standardized_share, axis=-1, keepdims=True),
        ),
        "mp",
    )
    gain_portion = jnp.sum(normed_gradient_share * standardized_share, axis=0)
    layer_norm_gain_gradient, q_gain_grad, k_gain_grad = lax.psum(
        (gain_portion, q_part, k_part), "dp"
    )
    input_gradient_rows = (
        (
            scaled_input
            - plain_gradient_sum / feature_width
            - standardized_share * (cross_term_sum / feature_width)
        )
        * inverse_deviation
    ).astype(jnp.bfloat16)
    return (
        context,
        input_gradient_rows,
        layer_norm_gain_gradient,
        w_grad,
        q_gain_grad,
        k_gain_grad,
    )


def solution(mesh):
    placed = (P("dp", None), P(), P("dp", "mp"), P("mp", None), P("mp", None), P("dp", "mp"))
    return jax.shard_map(
        per_device,
        mesh=mesh,
        in_specs=placed,
        out_specs=(
            P("dp", "mp"),
            P("dp", "mp"),
            P("mp"),
            P("dp", "mp"),
            P("mp", None),
            P("mp", None),
        ),
        check_vma=False,
    )
```

profile of v0, /device:TPU:128, one launch (start us, length us, event | category | flops | bytes accessed | tf_op | source)
XLA Modules:
  0.0 838.1 jit_solution(980596884754253209)
XLA Ops:
  7.2 0.0 copy-start
  7.2 0.0 all-gather.2.cloned.1.call-start
  7.2 0.7 all-gather.2.cloned.1.call-update
  7.9 0.0 copy-start.4
  7.9 0.0 reduce-scatter.3.cloned.1.call-start
  8.0 1.7 copy.16
  9.7 0.4 convert_reduce_fusion
  10.1 0.5 fusion.2
  10.6 0.0 copy-start.2
  10.6 0.0 copy-start.3
  10.6 44.5 %all-gather.2.cloned.1.call-done = bf16[3072,384]{1,0:T(8,128)(2,1)} async-done(((bf16[192,384]{1,0:T(8,128)(2,1)}), bf16[3072,384]{1,0:T(8,128)(2,1)}) %all-gather.2.cloned.1.call-update) | async-done | bytes 2359312 | tf_op jit(solution)/shard_map/all_gather | solution.py:70
  55.1 0.0 copy-done.4
  55.1 3.1 fusion.6
  58.2 0.0 copy-start.1
  58.4 0.0 copy-done.2
  58.4 0.0 copy-done.3
  58.4 0.3 fusion.54
  58.7 0.0 copy-done
  58.7 0.2 fusion.5
  59.0 0.2 multiply_reduce_fusion
  59.2 0.1 multiply_convert_fusion.1
  59.3 0.2 convolution_bitcast_fusion.2
  59.5 0.3 multiply_reduce_fusion.1
  59.8 0.1 fusion.29
  60.0 0.0 copy-done.1
  60.0 2.2 convolution_convert_fusion.1
  62.2 0.0 reduce-scatter.3.cloned.1.call-update
  62.2 0.0 reduce-scatter.5.cloned.1.call-start
  62.2 2.5 convolution_convert_fusion
  64.7 0.0 reduce-scatter.5.cloned.1.call-update
  64.8 0.1 dynamic_slice.6
  64.8 2.0 fusion
  66.8 0.2 fusion.4
  67.0 0.7 copy.19
  67.7 658.7 %reduce-scatter.3.cloned.1.call-done = bf16[256,96]{0,1:T(8,128)(2,1)} async-done(((bf16[256,3072]{0,1:T(8,128)(2,1)}), bf16[256,96]{0,1:T(8,128)(2,1)}) %reduce-scatter.3.cloned.1.call-update) | async-done | bytes 49168 | tf_op jit(solution)/shard_map/reduce_scatter | solution.py:90
  726.4 1.1 fusion.28
  727.5 27.7 %all-reduce.1 = (f32[96]{0:T(128)}, f32[1,128]{1,0:T(1,128)}, f32[1,128]{1,0:T(1,128)}) all-reduce(f32[96]{0:T(128)S(1)} %get-tuple-element.18, f32[1,128]{1,0:T(1,128)S(1)} %bitcast.160, f32[1,128]{1,0:T(1,128)S(1)} %bitcast.159), channel_id=1, replica_groups=mesh['dp'=16,'mp'=32] {'dp'}, use_global_device_ids=true, to_apply=%region_18.0 | all-reduce | flops 352 | bytes 2816 | tf_op jit(solution)/shard_map/psum | solution.py:108
  755.2 74.7 %all-reduce = (f32[256,1]{0,1:T(1,128)S(1)}, f32[256,1]{0,1:T(1,128)S(1)}) all-reduce(f32[256,1]{0,1:T(1,128)S(1)} %bitcast.152, f32[256,1]{0,1:T(1,128)S(1)} %bitcast.153), channel_id=1, replica_groups=mesh['dp'=16,'mp'=32] {'mp'}, use_global_device_ids=true, to_apply=%region_16.0 | all-reduce | flops 512 | bytes 4096 | tf_op jit(solution)/shard_map/psum | solution.py:100
  829.9 1.6 fusion.26
  831.6 0.0 reduce-scatter.5.cloned.1.call-done
  (14 shorter events, 0.2 us)
Async XLA Ops:
  7.2 51.6 %copy-start = (bf16[256,128]{1,0:T(8,128)(2,1)S(1)}, bf16[256,128]{1,0:T(8,128)(2,1)}, u32[]{:S(2)}) copy-start(bf16[256,128]{1,0:T(8,128)(2,1)} %param.11) | copy-start | bytes 196612
  7.2 47.9 %all-gather.2.cloned.1.call-start = ((), (), s32[]{:S(2)}) async-start(), calls=%async_computation.2 | async-start | bytes 2506752 | tf_op jit(solution)/shard_map/all_gather | solution.py:70
  7.9 47.2 %copy-start.4 = (f32[3072]{0:T(1024)S(1)}, f32[3072]{0:T(1024)}, u32[]{:S(2)}) copy-start(f32[3072]{0:T(1024)} %param.7) | copy-start | bytes 36868
  7.9 718.5 %reduce-scatter.3.cloned.1.call-start = ((), (), s32[]{:S(2)}) async-start(), calls=%async_computation.3 | async-start | bytes 1622016 | tf_op jit(solution)/shard_map/reduce_scatter | solution.py:90
  10.6 47.8 %copy-start.2 = (f32[1,128]{1,0:T(1,128)S(1)}, f32[1,128]{1,0:T(1,128)}, u32[]{:S(2)}) copy-start(f32[1,128]{1,0:T(1,128)} %param.10) | copy-start | bytes 1540
  10.6 47.8 %copy-start.3 = (f32[1,128]{1,0:T(1,128)S(1)}, f32[1,128]{1,0:T(1,128)}, u32[]{:S(2)}) copy-start(f32[1,128]{1,0:T(1,128)} %param.9) | copy-start | bytes 1540
  58.2 1.8 copy-start.1
  62.2 769.4 %reduce-scatter.5.cloned.1.call-start = ((), (), s32[]{:S(2)}) async-start(), calls=%async_computation.4 | async-start | bytes 2506752 | tf_op jit(solution)/shard_map/reduce_scatter | solution.py:79
Sparse Core Ops, SparseCore 0:
  10.2 44.9 all-gather.1
  62.3 664.0 reduce-scatter.2
  729.8 70.5 reduce-scatter.4
where the time goes:
time: 839 us; the launch traced here: 838 us
  waiting for transfers between devices  704 us (84%)
  blocking collectives  102 us (12%)
  between operations  13.9 us (2%)
  matrix products  9.23 us (1%)
    reduce_scatter x1, waiting for transfers between devices, per_device(): lax.psum_scatter(partial_in.astype(jnp.bfloat16), 'mp', scatter_dimension...  659 us
    psum x1, blocking collectives, per_device(): lax.psum((jnp.sum(scaled_input, axis=-1, keepdims=True), jnp.sum(scaled_i...  74.7 us
    all_gather x1, waiting for transfers between devices, per_device(): full_cols = lax.all_gather(w_qkv, 'dp', axis=0, tiled=True)  44.5 us
    psum x1, blocking collectives, per_device(): lax.psum((gain_portion, q_part, k_part), 'dp')  27.7 us
  transfers between devices with their start and end apart: 3, of which 2 were waited for; matrix products, arithmetic and copies ran while one was open for 1% of the time, Pallas kernels for 0%

commit v1 on v0

v1 whole, which is shorter than its diff:
```python
import jax
import jax.numpy as jnp
from jax import lax
from jax.sharding import PartitionSpec as P

BF = jnp.bfloat16
F32 = jnp.float32
PATCHES = 256
DP, MP = "dp", "mp"
NX, NYL, NC = 4, 2, 2
NZ, NYH = 16, 2

CORE_SWAP = [(i, i ^ 1) for i in range(NX * NYL * NC)]
SAME_CORE = [[2 * i + c for i in range(NX * NYL)] for c in range(NC)]
YHI_SWAP = [(j, j ^ 1) for j in range(NZ * NYH)]
SAME_YHI = [[2 * z + y for z in range(NZ)] for y in range(NYH)]


def head_norm(raw):
    centered = raw - jnp.mean(raw, axis=-1, keepdims=True)
    inverse = lax.rsqrt(jnp.mean(centered * centered, axis=-1, keepdims=True) + 1e-06)
    return centered * inverse, inverse


def norm_backward_pass(grad_hat, normal, inverse):
    first = jnp.mean(grad_hat, axis=-1, keepdims=True)
    second = jnp.mean(grad_hat * normal, axis=-1, keepdims=True)
    return (grad_hat - first - normal * second) * inverse


def dot(a, b, ca, cb):
    return lax.dot_general(a, b, (((ca,), (cb,)), ((), ())), preferred_element_type=F32)


def attend(raw, grad, q_gain, k_gain):
    hd = q_gain.shape[-1]
    scale = hd ** (-0.5)
    qhat, q_inv = head_norm(raw[:, :hd])
    khat, k_inv = head_norm(raw[:, hd : 2 * hd])
    value = raw[:, 2 * hd :].astype(BF)
    q_norm = (qhat * q_gain).astype(BF)
    k_norm = (khat * k_gain).astype(BF)
    expo = jnp.exp(dot(q_norm, k_norm, 1, 1) * scale)
    probs = expo / jnp.sum(expo, axis=-1, keepdims=True)
    probs_b = probs.astype(BF)
    context = dot(probs_b, value, 1, 0).astype(BF)
    dprob = dot(grad, value, 1, 1)
    dvalue = dot(probs_b, grad, 0, 0).astype(BF)
    dscore = (probs * (dprob - jnp.sum(probs * dprob, axis=-1, keepdims=True)) * scale).astype(BF)
    dqn = dot(dscore, k_norm, 1, 0)
    dkn = dot(dscore, q_norm, 0, 0)
    q_part = jnp.sum(dqn * qhat, axis=0, keepdims=True)
    k_part = jnp.sum(dkn * khat, axis=0, keepdims=True)
    dquery = norm_backward_pass(dqn * q_gain, qhat, q_inv).astype(BF)
    dkey = norm_backward_pass(dkn * k_gain, khat, k_inv).astype(BF)
    return context, jnp.concatenate([dquery, dkey, dvalue], axis=1), q_part, k_part


def hi_lo(value):
    hi = value.astype(BF)
    lo = (value - hi.astype(F32)).astype(BF)
    return hi, lo


def per_device(tokens, layer_norm_gain, w_qkv, q_gain, k_gain, ctx_grad):
    rows, width = tokens.shape
    w_rows, columns = w_qkv.shape
    share = width // (NZ * NYH)
    core = lax.axis_index(DP) % 2
    y_hi = lax.axis_index(MP) % 2
    mp = lax.axis_index(MP)

    with jax.named_scope("gather_w"):
        copies = jnp.broadcast_to(w_qkv[None], (NX * NYL, w_rows, columns))
        own = lax.all_to_all(copies, DP, 0, 0, axis_index_groups=SAME_CORE, tiled=True)
        other = lax.ppermute(own, DP, CORE_SWAP)
        full = jnp.stack(
            [jnp.where(core == 0, own, other), jnp.where(core == 0, other, own)], axis=1
        ).reshape(width, columns)

    with jax.named_scope("input_norm"):
        x_float = tokens.astype(F32)
        centered = x_float - jnp.mean(x_float, axis=-1, keepdims=True)
        inverse = lax.rsqrt(jnp.mean(centered * centered, axis=-1, keepdims=True) + 1e-06)
        xhat = centered * inverse
        normed = (xhat * layer_norm_gain).astype(BF)

    with jax.named_scope("attention"):
        qkv = dot(normed, full, 1, 0)
        context, dqkv, q_part, k_part = attend(qkv, ctx_grad, q_gain, k_gain)

    with jax.named_scope("input_gradient_partial"):
        dqkv_f = dqkv.astype(F32)
        weighted = jnp.sum(full.astype(F32) * layer_norm_gain[:, None], axis=0)
        s1 = jnp.sum(dqkv_f * weighted[None, :], axis=1)
        s2 = jnp.sum(dqkv_f * qkv, axis=1)
        by_y = full.reshape(NZ, NYH, share, columns)
        w_keep = jnp.where(y_hi == 0, by_y[:, 0], by_y[:, 1]).reshape(-1, columns)
        w_send = jnp.where(y_hi == 0, by_y[:, 1], by_y[:, 0]).reshape(-1, columns)
        part_send = dot(w_send, dqkv, 1, 1).astype(BF)
        part_keep = dot(w_keep, dqkv, 1, 1)
        h1, l1 = hi_lo(s1)
        h2, l2 = hi_lo(s2)
        sums = jnp.concatenate(
            [jnp.stack([h1, l1, h2, l2]), jnp.zeros((12, rows), BF)], axis=0
        )
        got = lax.ppermute(part_send, MP, YHI_SWAP).astype(F32)
        got_sums = lax.ppermute(sums, MP, YHI_SWAP).astype(F32)
        t1 = s1 + got_sums[0] + got_sums[1]
        t2 = s2 + got_sums[2] + got_sums[3]
        h1, l1 = hi_lo(t1)
        h2, l2 = hi_lo(t2)
        sums = jnp.concatenate(
            [jnp.stack([h1, l1, h2, l2]), jnp.zeros((12, rows), BF)], axis=0
        )
        pair = (part_keep + got).astype(BF).reshape(NZ, share, rows)
        pair = jnp.concatenate([pair, jnp.broadcast_to(sums[None], (NZ, 16, rows))], axis=1)

    with jax.named_scope("w_grad"):
        term = dot(normed, dqkv, 0, 0).astype(BF).reshape(NX * NYL, NC, w_rows, columns)
        term_keep = jnp.where(core == 0, term[:, 0], term[:, 1])
        term_send = jnp.where(core == 0, term[:, 1], term[:, 0])
        term_got = lax.ppermute(term_send, DP, CORE_SWAP)
        chip = (term_keep.astype(F32) + term_got.astype(F32)).astype(BF)
        w_grad = lax.psum_scatter(
            chip.reshape(-1, columns), DP, scatter_dimension=0, tiled=True,
            axis_index_groups=SAME_CORE,
        )

    with jax.named_scope("sum_over_z"):
        parts = lax.all_to_all(pair, MP, 0, 0, axis_index_groups=SAME_YHI, tiled=True)
        total = jnp.sum(parts.astype(F32), axis=0)
        dnormed = total[:share].T
        plain = (total[share] + total[share + 1])[:, None]
        cross = (total[share + 2] + total[share + 3])[:, None]

    with jax.named_scope("input_gradient"):
        start = mp * share
        xhat_share = lax.dynamic_slice_in_dim(xhat, start, share, 1)
        gain_share = lax.dynamic_slice_in_dim(layer_norm_gain, start, share, 0)
        input_gradient_rows = (
            (dnormed * gain_share - plain / width - xhat_share * (cross / width)) * inverse
        ).astype(BF)
        gain_portion = jnp.sum(dnormed * xhat_share, axis=0)

    with jax.named_scope("gain_gradients"):
        small = jnp.concatenate(
            [
                jnp.pad(gain_portion, (0, 128 - share))[None],
                q_part,
                k_part,
                jnp.zeros((5, 128), F32),
            ],
            axis=0,
        )
        copies = jnp.broadcast_to(small[None], (NX * NYL * NC, 8, 128))
        summed = jnp.sum(lax.all_to_all(copies, DP, 0, 0, tiled=True), axis=0)
    return (
        context,
        input_gradient_rows,
        summed[0, :share],
        w_grad,
        summed[1:2],
        summed[2:3],
    )


def solution(mesh):
    placed = (P("dp", None), P(), P("dp", "mp"), P("mp", None), P("mp", None), P("dp", "mp"))
    return jax.shard_map(
        per_device,
        mesh=mesh,
        in_specs=placed,
        out_specs=(
            P("dp", "mp"),
            P("dp", "mp"),
            P("mp"),
            P("dp", "mp"),
            P("mp", None),
            P("mp", None),
        ),
        check_vma=False,
    )
```

time: 839 us -> 154 us (0.18)
  the two profiles are of different devices: /device:TPU:128 before, /device:TPU:33 now
where the time goes in v1:
time: 154 us; the launch traced here: 152 us
  waiting for transfers between devices  42.5 us (28%)
  starting transfers between devices  39.4 us (26%)
  blocking collectives  20.6 us (13%)
  other arithmetic  17.2 us (11%)
  between operations  14.5 us (9%)
  matrix products  9.16 us (6%)
  local copies, waits for them, and re-layouts  8.64 us (6%)
    all_to_all x1, waiting for transfers between devices, per_device(): lax.all_to_all(pair, MP, 0, 0, axis_index_groups=SAME_YHI, tiled=True)  23.9 us
    all_to_all x1, blocking collectives, per_device(): lax.all_to_all(copies, DP, 0, 0, axis_index_groups=SAME_CORE, tiled=True)  20.6 us
    all_to_all x1, starting transfers between devices, per_device(): lax.all_to_all(pair, MP, 0, 0, axis_index_groups=SAME_YHI, tiled=True)  14.7 us
    ppermute x1, waiting for transfers between devices, per_device(): got_sums = lax.ppermute(sums, MP, YHI_SWAP).astype(F32)  10.9 us
    all_to_all x1, starting transfers between devices, per_device(): summed = jnp.sum(lax.all_to_all(copies, DP, 0, 0, tiled=True), axis=0)  10.4 us
    dot_general x10, matrix products, dot(): lax.dot_general(a, b, (((ca,), (cb,)), ((), ())), preferred_element_type=...  9.16 us
    all_to_all x1, waiting for transfers between devices, per_device(): summed = jnp.sum(lax.all_to_all(copies, DP, 0, 0, tiled=True), axis=0)  5.05 us
    ppermute x1, starting transfers between devices, per_device(): got = lax.ppermute(part_send, MP, YHI_SWAP).astype(F32)  4.52 us
  transfers between devices with their start and end apart: 7, of which 4 were waited for; matrix products, arithmetic and copies ran while one was open for 14% of the time, Pallas kernels for 0%

profile of v1, /device:TPU:33, one launch (start us, length us, event | category | flops | bytes accessed | tf_op | source)
XLA Modules:
  0.0 152.0 jit_solution(4642617535108703140)
XLA Ops:
  7.2 0.0 copy-start
  7.2 0.0 copy-start.6
  7.2 1.0 broadcast_in_dim.14
  8.2 20.6 %all_to_all.15 = bf16[8,192,384]{2,1,0:T(8,128)(2,1)S(1)} all-to-all(bf16[8,192,384]{2,1,0:T(8,128)(2,1)S(1)} %broadcast_in_dim.14), channel_id=1, replica_groups={{0,64,128,192,256,320,384,448},{32,96,160,224,288,352,416,480},{1,65,12..., dimensions={0} | all-to-all | bytes 2359296 | tf_op jit(solution)/shard_map/gather_w/all_to_all | solution.py:75
  28.8 4.1 %collective-permute-start = (bf16[8,192,384]{2,1,0:T(8,128)(2,1)S(1)}, bf16[8,192,384]{2,1,0:T(8,128)(2,1)}, u32[]{:S(2)}, u32[]{:S(2)}) collective-permute-start(bf16[8,192,384]{2,1,0:T(8,128)(2,1)S(1)} %all_to_all.15), channel_id=1, source_target_pairs={{0,32},{32,0},{64,96},{96,64},{128,160},{160,128},{192,224},{224,1... | collective-permute-start | bytes 3538952 | tf_op jit(solution)/shard_map/gather_w/ppermute | solution.py:76
  32.9 0.1 mul.208
  33.0 1.7 %copy.33 = bf16[256,3072]{0,1:T(8,128)(2,1)S(1)} copy(bf16[256,3072]{1,0:T(8,128)(2,1)} %param.6) | data formatting | bytes 3145728 | tf_op args[0]
  34.7 0.4 convert_reduce_fusion
  35.2 0.5 fusion.2
  35.7 1.5 select_bitcast_fusion.1
  37.2 0.3 pad_maximum_fusion
  37.5 0.0 copy-start.12
  37.5 0.0 copy-start.15
  37.5 2.0 %fusion.9 = f32[256,384]{1,0:T(8,128)S(1)} fusion(bf16[3072,384]{1,0:T(8,128)(2,1)S(1)} %bitcast.61, f32[3072]{0:T(1024)S(1)} %copy-done.6, f32[256]{0:T(256)S(1)} %add_rsqrt_fusion.2, f32[256]{0:T(256)S(1)} %broadcast_multiply_fusion.6, bf16[256,3072]{0,1:T(8,128)(2,1)S(1)} %copy.33), kind=kOutput, calls=%fused_computation.34 | convolution fusion | flops 607911936 | bytes 4339712 | tf_op jit(solution)/shard_map/attention/dot_general | solution.py:32
  39.5 0.1 slice_reduce_fusion.1
  39.6 0.2 multiply_reduce_fusion.7
  39.9 0.3 fusion.24
  40.3 0.2 convolution_convert_fusion.2
  40.5 0.0 copy-start.4
  40.5 0.2 multiply_reduce_fusion.1
  40.7 0.7 multiply_reduce_fusion
  41.5 0.3 fusion.14
  41.8 0.9 multiply_reduce_fusion.3
  42.7 0.2 broadcast_select_fusion.1
  43.0 0.3 multiply_convert_fusion.5
  43.3 1.5 convolution_convert_fusion.1
  44.8 4.5 %collective-permute-start.1 = (bf16[1536,256]{1,0:T(8,128)(2,1)}, bf16[1536,256]{1,0:T(8,128)(2,1)}, u32[]{:S(2)}, u32[]{:S(2)}) collective-permute-start(bf16[1536,256]{1,0:T(8,128)(2,1)} %convolution_convert_fusion.1), channel_id=1, source_target_pairs={{0,1},{1,0},{2,3},{3,2},{4,5},{5,4},{6,7},{7,6},{8,9},{9,8},{10,11... | collective-permute-start | bytes 2359304 | tf_op jit(solution)/shard_map/input_gradient_partial/ppermute | solution.py:107
  49.4 0.2 fusion.8
  49.5 0.6 convert_element_type.182
  50.1 0.6 convert_element_type.185
  50.7 0.6 subtract_convert_fusion.3
  51.3 0.6 subtract_convert_fusion.2
  51.9 2.6 %concatenate.16 = bf16[16,256]{1,0:T(8,128)(2,1)} concatenate(bf16[1,256]{1,0:T(2,128)(2,1)} %convert_element_type.182, bf16[1,256]{1,0:T(2,128)(2,1)} %subtract_convert_fusion.3, bf16[1,256]{1,0:T(2,128)(2,1)} %convert_element_type.185, bf16[1,256]{1,0:T(2,128)(2,1)} %subtract_convert_fusion.2, bf16[12,256]{1,0:T(8,128)(2,1)S(1)} %broadcast.133), dimensions={0} | concatenate | bytes 16384 | tf_op jit(solution)/shard_map/input_gradient_partial/concatenate | solution.py:104
  54.5 2.2 %collective-permute-start.2 = (bf16[16,256]{1,0:T(8,128)(2,1)}, bf16[16,256]{1,0:T(8,128)(2,1)S(1)}, u32[]{:S(2)}, u32[]{:S(2)}) collective-permute-start(bf16[16,256]{1,0:T(8,128)(2,1)} %concatenate.16), channel_id=1, source_target_pairs={{0,1},{1,0},{2,3},{3,2},{4,5},{5,4},{6,7},{7,6},{8,9},{9,8},{10,11... | collective-permute-start | bytes 24584 | tf_op jit(solution)/shard_map/input_gradient_partial/ppermute | solution.py:108
  56.7 10.9 %collective-permute-done.2 = bf16[16,256]{1,0:T(8,128)(2,1)S(1)} collective-permute-done((bf16[16,256]{1,0:T(8,128)(2,1)}, bf16[16,256]{1,0:T(8,128)(2,1)S(1)}, u32[]{:S(2)}, u32[]{:S(2)}) %collective-permute-start.2) | collective-permute-done | bytes 8224 | tf_op jit(solution)/shard_map/input_gradient_partial/ppermute | solution.py:108
  67.6 0.6 subtract_convert_fusion
  68.3 0.8 concatenate.17
  69.1 1.8 %add_convert_fusion = bf16[1536,256]{1,0:T(8,128)(2,1)S(1)} fusion(bf16[1536,256]{1,0:T(8,128)(2,1)} %collective-permute-done.1, bf16[1536,384]{1,0:T(8,128)(2,1)S(1)} %bitcast.66, bf16[256,128]{1,0:T(8,128)(2,1)} %copy-done.4, bf16[256,128]{1,0:T(8,128)(2,1)} %copy-done.2, bf16[256,128]{1,0:T(8,128)(2,1)S(1)} %get-tuple-element.30), kind=kOutput, calls=%fused_computation.14 | convolution fusion | flops 303759360 | bytes 2949120 | tf_op jit(solution)/shard_map/input_gradient_partial/dot_general | solution.py:32
  70.9 0.0 copy-start.3
  70.9 0.0 copy-start.5
  71.0 1.0 pad_maximum_fusion.1
  72.0 14.7 %all-to-all-start.1 = ((bf16[16,112,256]{2,1,0:T(8,128)(2,1)}), bf16[16,112,256]{2,1,0:T(8,128)(2,1)S(1)}, u32[]{:S(2)}, u32[]{:S(2)}) async-start(bf16[16,112,256]{2,1,0:T(8,128)(2,1)} %pad_maximum_fusion.1), calls=%async_computation.1 | async-start | bytes 1835008 | tf_op jit(solution)/shard_map/sum_over_z/all_to_all | solution.py:131
  86.6 0.0 reduce-scatter.2.cloned.1.call-start
  86.7 1.0 convolution_convert_fusion
  87.8 1.3 fusion.4
  89.1 0.4 copy-done.1
  89.5 3.4 %collective-permute-start.3 = (bf16[8,192,384]{2,1,0:T(8,128)(2,1)}, bf16[8,192,384]{2,1,0:T(8,128)(2,1)}, u32[]{:S(2)}, u32[]{:S(2)}) collective-permute-start(bf16[8,192,384]{2,1,0:T(8,128)(2,1)} %fusion.4), channel_id=1, source_target_pairs={{0,32},{32,0},{64,96},{96,64},{128,160},{160,128},{192,224},{224,1... | collective-permute-start | bytes 3538952 | tf_op jit(solution)/shard_map/w_grad/ppermute | solution.py:123
  92.9 0.1 dynamic_slice.6
  93.0 0.1 pad.8.clone
  93.1 2.6 %collective-permute-done.3 = bf16[8,192,384]{2,1,0:T(8,128)(2,1)} collective-permute-done((bf16[8,192,384]{2,1,0:T(8,128)(2,1)}, bf16[8,192,384]{2,1,0:T(8,128)(2,1)}, u32[]{:S(2)}, u32[]{:S(2)}) %collective-permute-start.3) | collective-permute-done | bytes 1179680 | tf_op jit(solution)/shard_map/w_grad/ppermute | solution.py:123
  95.7 3.5 %fusion.3 = bf16[8,192,384]{2,1,0:T(8,128)(2,1)} fusion(bf16[8,192,384]{2,1,0:T(8,128)(2,1)} %collective-permute-done.3, pred[]{:T(512)S(6)} %eq.7, bf16[8,2,192,384]{3,2,1,0:T(8,128)(2,1)} %bitcast.64), kind=kLoop, calls=%fused_computation.11 | loop fusion | flops 2949120 | bytes 4718593 | tf_op jit(solution)/shard_map/w_grad/convert_element_type | solution.py:124
  99.2 0.0 reduce-scatter.2.cloned.1.call-update
  99.2 0.0 copy-start.16
  99.3 2.0 %fusion = f32[256,3072]{0,1:T(8,128)} fusion(bf16[256,3072]{0,1:T(8,128)(2,1)S(1)} %copy.33, f32[256]{0:T(256)S(1)} %copy-done.9, f32[256]{0:T(256)S(1)} %copy-done.11), kind=kLoop, calls=%fused_computation.4 | loop fusion | flops 2359296 | bytes 4720640 | tf_op jit(solution)/shard_map/input_norm/mul | solution.py:85
  101.2 23.9 %all-to-all-done.1 = bf16[16,112,256]{2,1,0:T(8,128)(2,1)S(1)} async-done(((bf16[16,112,256]{2,1,0:T(8,128)(2,1)}), bf16[16,112,256]{2,1,0:T(8,128)(2,1)S(1)}, u32[]{:S(2)}, u32[]{:S(2)}) %all-to-all-start.1) | async-done | bytes 917536 | tf_op jit(solution)/shard_map/sum_over_z/all_to_all | solution.py:131
  125.1 0.1 convert_reduce_fusion.1
  125.3 1.7 %multiply_reduce_fusion.10 = (f32[96]{0:T(128)S(1)}, bf16[256,96]{0,1:T(8,128)(2,1)}) fusion(f32[112,256]{1,0:T(8,128)S(1)} %convert_reduce_fusion.1, f32[256,3072]{0,1:T(8,128)} %fusion, s32[]{:T(128)S(6)} %select_n.71, f32[256]{0:T(256)S(1)} %copy-done.9, f32[256]{0:T(256)S(1)} %bitcast.80, f32[256]{0:T(256)S(1)} %bitcast.79, f32[96]{0:T(128)S(1)} %dynamic_slice.6), kind=kLoop, calls=%fused_computation.57 | loop fusion | flops 196512 | bytes 249604 | tf_op jit(solution)/shard_map/input_gradient/reduce_sum | solution.py:144
  127.0 0.1 maximum_maximum_fusion
  127.1 0.6 broadcast_in_dim.20
  127.7 10.4 %all-to-all-start.2 = ((f32[16,8,128]{2,1,0:T(8,128)}), f32[16,8,128]{2,1,0:T(8,128)S(1)}, u32[]{:S(2)}, u32[]{:S(2)}) async-start(f32[16,8,128]{2,1,0:T(8,128)} %broadcast_in_dim.20), calls=%async_computation.2 | async-start | bytes 131072 | tf_op jit(solution)/shard_map/gain_gradients/all_to_all | solution.py:157
  138.2 0.9 convolution_convert_fusion.3
  139.0 5.0 %all-to-all-done.2 = f32[16,8,128]{2,1,0:T(8,128)S(1)} async-done(((f32[16,8,128]{2,1,0:T(8,128)}), f32[16,8,128]{2,1,0:T(8,128)S(1)}, u32[]{:S(2)}, u32[]{:S(2)}) %all-to-all-start.2) | async-done | bytes 65568 | tf_op jit(solution)/shard_map/gain_gradients/all_to_all | solution.py:157
  144.1 0.5 slice_bitcast_fusion.1
  144.6 0.5 fusion.23
  (47 shorter events, 0.2 us)
Async XLA Ops:
  7.2 33.1 %copy-start = (bf16[256,128]{1,0:T(8,128)(2,1)S(1)}, bf16[256,128]{1,0:T(8,128)(2,1)}, u32[]{:S(2)}) copy-start(bf16[256,128]{1,0:T(8,128)(2,1)} %param.11) | copy-start | bytes 196612
  7.2 25.7 %copy-start.6 = (f32[3072]{0:T(1024)S(1)}, f32[3072]{0:T(1024)}, u32[]{:S(2)}) copy-start(f32[3072]{0:T(1024)} %param.7) | copy-start | bytes 36868
  28.8 6.9 %collective-permute-start = (bf16[8,192,384]{2,1,0:T(8,128)(2,1)S(1)}, bf16[8,192,384]{2,1,0:T(8,128)(2,1)}, u32[]{:S(2)}, u32[]{:S(2)}) collective-permute-start(bf16[8,192,384]{2,1,0:T(8,128)(2,1)S(1)} %all_to_all.15), channel_id=1, source_target_pairs={{0,32},{32,0},{64,96},{96,64},{128,160},{160,128},{192,224},{224,1... | collective-permute-start | bytes 3538952 | tf_op jit(solution)/shard_map/gather_w/ppermute | solution.py:76
  35.2 2.3 %copy-start.10 = (f32[256]{0:T(256)}, f32[256]{0:T(256)S(1)}, u32[]{:S(2)}) copy-start(f32[256]{0:T(256)S(1)} %broadcast_multiply_fusion.6) | copy-start | bytes 3076
  35.7 1.8 %copy-start.8 = (f32[256]{0:T(256)}, f32[256]{0:T(256)S(1)}, u32[]{:S(2)}) copy-start(f32[256]{0:T(256)S(1)} %add_rsqrt_fusion.2) | copy-start | bytes 3076
  37.5 2.4 %copy-start.12 = (f32[1,128]{1,0:T(1,128)S(1)}, f32[1,128]{1,0:T(1,128)}, u32[]{:S(2)}) copy-start(f32[1,128]{1,0:T(1,128)} %param.9) | copy-start | bytes 1540
  37.5 2.4 %copy-start.15 = (f32[1,128]{1,0:T(1,128)S(1)}, f32[1,128]{1,0:T(1,128)}, u32[]{:S(2)}) copy-start(f32[1,128]{1,0:T(1,128)} %param.10) | copy-start | bytes 1540
  40.3 1.1 copy-start.13
  40.5 8.9 %copy-start.4 = (bf16[256,128]{1,0:T(8,128)(2,1)}, bf16[256,128]{1,0:T(8,128)(2,1)S(1)}, u32[]{:S(2)}) copy-start(bf16[256,128]{1,0:T(8,128)(2,1)S(1)} %convolution_convert_fusion.2) | copy-start | bytes 196612
  43.3 6.1 %copy-start.2 = (bf16[256,128]{1,0:T(8,128)(2,1)}, bf16[256,128]{1,0:T(8,128)(2,1)S(1)}, u32[]{:S(2)}) copy-start(bf16[256,128]{1,0:T(8,128)(2,1)S(1)} %get-tuple-element.31) | copy-start | bytes 196612
  44.8 24.3 %collective-permute-start.1 = (bf16[1536,256]{1,0:T(8,128)(2,1)}, bf16[1536,256]{1,0:T(8,128)(2,1)}, u32[]{:S(2)}, u32[]{:S(2)}) collective-permute-start(bf16[1536,256]{1,0:T(8,128)(2,1)} %convolution_convert_fusion.1), channel_id=1, source_target_pairs={{0,1},{1,0},{2,3},{3,2},{4,5},{5,4},{6,7},{7,6},{8,9},{9,8},{10,11... | collective-permute-start | bytes 2359304 | tf_op jit(solution)/shard_map/input_gradient_partial/ppermute | solution.py:107
  54.5 13.2 %collective-permute-start.2 = (bf16[16,256]{1,0:T(8,128)(2,1)}, bf16[16,256]{1,0:T(8,128)(2,1)S(1)}, u32[]{:S(2)}, u32[]{:S(2)}) collective-permute-start(bf16[16,256]{1,0:T(8,128)(2,1)} %concatenate.16), channel_id=1, source_target_pairs={{0,1},{1,0},{2,3},{3,2},{4,5},{5,4},{6,7},{7,6},{8,9},{9,8},{10,11... | collective-permute-start | bytes 24584 | tf_op jit(solution)/shard_map/input_gradient_partial/ppermute | solution.py:108
  70.9 15.8 %copy-start.3 = (bf16[256,128]{1,0:T(8,128)(2,1)S(1)}, bf16[256,128]{1,0:T(8,128)(2,1)}, u32[]{:S(2)}) copy-start(bf16[256,128]{1,0:T(8,128)(2,1)} %copy-done.2) | copy-start | bytes 196612
  70.9 15.8 %copy-start.5 = (bf16[256,128]{1,0:T(8,128)(2,1)S(1)}, bf16[256,128]{1,0:T(8,128)(2,1)}, u32[]{:S(2)}) copy-start(bf16[256,128]{1,0:T(8,128)(2,1)} %copy-done.4) | copy-start | bytes 196612
  71.0 15.7 %copy-start.7 = (f32[3072]{0:T(1024)S(1)}, f32[3072]{0:T(1024)}, u32[]{:S(2)}) copy-start(f32[3072]{0:T(1024)} %param.7) | copy-start | bytes 36868
  71.0 15.7 %copy-start.9 = (f32[256]{0:T(256)S(1)}, f32[256]{0:T(256)}, u32[]{:S(2)}) copy-start(f32[256]{0:T(256)} %copy-done.8) | copy-start | bytes 3076
  71.0 15.7 %copy-start.11 = (f32[256]{0:T(256)S(1)}, f32[256]{0:T(256)}, u32[]{:S(2)}) copy-start(f32[256]{0:T(256)} %copy-done.10) | copy-start | bytes 3076
  72.0 53.2 %all-to-all-start.1 = ((bf16[16,112,256]{2,1,0:T(8,128)(2,1)}), bf16[16,112,256]{2,1,0:T(8,128)(2,1)S(1)}, u32[]{:S(2)}, u32[]{:S(2)}) async-start(bf16[16,112,256]{2,1,0:T(8,128)(2,1)} %pad_maximum_fusion.1), calls=%async_computation.1 | async-start | bytes 1835008 | tf_op jit(solution)/shard_map/sum_over_z/all_to_all | solution.py:131
  86.6 58.5 %reduce-scatter.2.cloned.1.call-start = ((), (), s32[]{:S(2)}) async-start(), calls=%async_computation.4 | async-start | bytes 1327104 | tf_op jit(solution)/shard_map/w_grad/reduce_scatter | solution.py:125
  87.8 1.8 %copy-start.1 = (bf16[3072,384]{1,0:T(8,128)(2,1)}, bf16[3072,384]{1,0:T(8,128)(2,1)S(1)}, u32[]{:S(2)}) copy-start(bf16[3072,384]{1,0:T(8,128)(2,1)S(1)} %convolution_convert_fusion) | copy-start | bytes 7077892
  89.5 6.2 %collective-permute-start.3 = (bf16[8,192,384]{2,1,0:T(8,128)(2,1)}, bf16[8,192,384]{2,1,0:T(8,128)(2,1)}, u32[]{:S(2)}, u32[]{:S(2)}) collective-permute-start(bf16[8,192,384]{2,1,0:T(8,128)(2,1)} %fusion.4), channel_id=1, source_target_pairs={{0,32},{32,0},{64,96},{96,64},{128,160},{160,128},{192,224},{224,1... | collective-permute-start | bytes 3538952 | tf_op jit(solution)/shard_map/w_grad/ppermute | solution.py:123
  99.2 27.8 %copy-start.16 = (f32[128]{0:T(128)S(1)}, f32[128]{0:T(128)}, u32[]{:S(2)}) copy-start(f32[128]{0:T(128)} %get-tuple-element.6) | copy-start | bytes 1540
  99.2 27.8 %copy-start.17 = (f32[128]{0:T(128)S(1)}, f32[128]{0:T(128)}, u32[]{:S(2)}) copy-start(f32[128]{0:T(128)} %get-tuple-element.11) | copy-start | bytes 1540
  99.3 38.9 %copy-start.14 = (f32[256]{0:T(256)S(1)}, f32[256]{0:T(256)}, u32[]{:S(2)}) copy-start(f32[256]{0:T(256)} %copy-done.13) | copy-start | bytes 3076
  127.7 16.4 %all-to-all-start.2 = ((f32[16,8,128]{2,1,0:T(8,128)}), f32[16,8,128]{2,1,0:T(8,128)S(1)}, u32[]{:S(2)}, u32[]{:S(2)}) async-start(f32[16,8,128]{2,1,0:T(8,128)} %broadcast_in_dim.20), calls=%async_computation.2 | async-start | bytes 131072 | tf_op jit(solution)/shard_map/gain_gradients/all_to_all | solution.py:157
Sparse Core Ops, SparseCore 0:
  99.4 41.8 reduce-scatter.1

commit v2 on v1

--- a/solution.py
+++ b/solution.py
@@ -13,7 +13,13 @@
 CORE_SWAP = [(i, i ^ 1) for i in range(NX * NYL * NC)]
 SAME_CORE = [[2 * i + c for i in range(NX * NYL)] for c in range(NC)]
 YHI_SWAP = [(j, j ^ 1) for j in range(NZ * NYH)]
-SAME_YHI = [[2 * z + y for z in range(NZ)] for y in range(NYH)]
+Z_PAIR = [(2 * z + y, 2 * (z ^ 1) + y) for z in range(NZ) for y in range(NYH)]
+Z_BETWEEN = [
+    (2 * z + y, 2 * ((z + 1 if z % 2 else z - 1) % NZ) + y)
+    for z in range(NZ)
+    for y in range(NYH)
+]
+Z_PARITY = [[2 * (2 * k + p) + y for k in range(NZ // 2)] for p in range(2) for y in range(NYH)]
 
 
 def head_norm(raw):
@@ -62,6 +68,17 @@
     return hi, lo
 
 
+def pack(sums):
+    hi, lo = hi_lo(sums)
+    return jnp.where(lax.broadcasted_iota(jnp.int32, sums.shape, 0) < 2, hi, lo)
+
+
+def unpack(sums, got):
+    got = got.astype(F32)
+    both = got[0:2] + got[2:4]
+    return sums + jnp.concatenate([both] * 8, axis=0)
+
+
 def per_device(tokens, layer_norm_gain, w_qkv, q_gain, k_gain, ctx_grad):
     rows, width = tokens.shape
     w_rows, columns = w_qkv.shape
@@ -69,6 +86,7 @@
     core = lax.axis_index(DP) % 2
     y_hi = lax.axis_index(MP) % 2
     mp = lax.axis_index(MP)
+    parity = (mp // 2) % 2
 
     with jax.named_scope("gather_w"):
         copies = jnp.broadcast_to(w_qkv[None], (NX * NYL, w_rows, columns))
@@ -89,32 +107,33 @@
         qkv = dot(normed, full, 1, 0)
         context, dqkv, q_part, k_part = attend(qkv, ctx_grad, q_gain, k_gain)
 
+    with jax.named_scope("patch_sums"):
+        weighted = jnp.sum(full.astype(F32) * layer_norm_gain[:, None], axis=0, keepdims=True)
+        row = lax.broadcasted_iota(jnp.int32, (16, columns), 0)
+        is_first = ((row == 0) | (row == 2)).astype(F32)
+        is_second = ((row == 1) | (row == 3)).astype(BF)
+        w_hi, w_lo = hi_lo(is_first * weighted)
+        p_hi, p_lo = hi_lo(dqkv.astype(F32) * qkv)
+        sums = (dot(w_hi, dqkv, 1, 1) + dot(w_lo, dqkv, 1, 1)) + (
+            dot(is_second, p_hi, 1, 1) + dot(is_second, p_lo, 1, 1)
+        )
+
     with jax.named_scope("input_gradient_partial"):
-        dqkv_f = dqkv.astype(F32)
-        weighted = jnp.sum(full.astype(F32) * layer_norm_gain[:, None], axis=0)
-        s1 = jnp.sum(dqkv_f * weighted[None, :], axis=1)
-        s2 = jnp.sum(dqkv_f * qkv, axis=1)
-        by_y = full.reshape(NZ, NYH, share, columns)
-        w_keep = jnp.where(y_hi == 0, by_y[:, 0], by_y[:, 1]).reshape(-1, columns)
-        w_send = jnp.where(y_hi == 0, by_y[:, 1], by_y[:, 0]).reshape(-1, columns)
-        part_send = dot(w_send, dqkv, 1, 1).astype(BF)
-        part_keep = dot(w_keep, dqkv, 1, 1)
-        h1, l1 = hi_lo(s1)
-        h2, l2 = hi_lo(s2)
-        sums = jnp.concatenate(
-            [jnp.stack([h1, l1, h2, l2]), jnp.zeros((12, rows), BF)], axis=0
-        )
-        got = lax.ppermute(part_send, MP, YHI_SWAP).astype(F32)
-        got_sums = lax.ppermute(sums, MP, YHI_SWAP).astype(F32)
-        t1 = s1 + got_sums[0] + got_sums[1]
-        t2 = s2 + got_sums[2] + got_sums[3]
-        h1, l1 = hi_lo(t1)
-        h2, l2 = hi_lo(t2)
-        sums = jnp.concatenate(
-            [jnp.stack([h1, l1, h2, l2]), jnp.zeros((12, rows), BF)], axis=0
-        )
-        pair = (part_keep + got).astype(BF).reshape(NZ, share, rows)
-        pair = jnp.concatenate([pair, jnp.broadcast_to(sums[None], (NZ, 16, rows))], axis=1)
+        half = share // 2
+        lane = rows // 2
+        by = full.reshape(NZ // 2, 2, NYH, share, columns)
+        pick = lambda which, at, dim: jnp.where(
+            which == 0, lax.index_in_dim(at, 0, dim, False), lax.index_in_dim(at, 1, dim, False)
+        ).reshape(-1, columns)
+        w_a, w_b = by[:, :, :, :half], by[:, :, :, half:]
+        send_a = dot(pick(1 - y_hi, w_a, 2), dqkv, 1, 1).astype(BF)
+        send_b = dot(pick(1 - parity, w_b, 1), dqkv, 1, 1).astype(BF)
+        send_a = jnp.concatenate([send_a, pack(sums)], axis=0)
+        got_a = lax.ppermute(send_a, MP, YHI_SWAP)
+        got_b0 = lax.ppermute(send_b[:, :lane], MP, Z_PAIR)
+        got_b1 = lax.ppermute(send_b[:, lane:], MP, Z_BETWEEN)
+        keep_a = dot(pick(y_hi, w_a, 2), dqkv, 1, 1)
+        keep_b = dot(pick(parity, w_b, 1), dqkv, 1, 1)
 
     with jax.named_scope("w_grad"):
         term = dot(normed, dqkv, 0, 0).astype(BF).reshape(NX * NYL, NC, w_rows, columns)
@@ -122,26 +141,58 @@
         term_send = jnp.where(core == 0, term[:, 1], term[:, 0])
         term_got = lax.ppermute(term_send, DP, CORE_SWAP)
         chip = (term_keep.astype(F32) + term_got.astype(F32)).astype(BF)
+        chip, got_a, got_b0, got_b1 = lax.optimization_barrier((chip, got_a, got_b0, got_b1))
         w_grad = lax.psum_scatter(
             chip.reshape(-1, columns), DP, scatter_dimension=0, tiled=True,
             axis_index_groups=SAME_CORE,
         )
 
+    with jax.named_scope("sum_over_pairs"):
+        many = (NZ // 2) * 2 * half
+        a = (keep_a + got_a[:many].astype(F32)).reshape(NZ // 2, 2, half, rows)
+        sums = unpack(sums, got_a[many:])
+        b = (keep_b + jnp.concatenate([got_b0, got_b1], axis=1).astype(F32)).reshape(
+            NZ // 2, NYH, half, rows
+        )
+        flat = (NZ // 2 * half, rows)
+        a_send = jnp.where(parity == 0, a[:, 1], a[:, 0]).astype(BF).reshape(flat)
+        b_send = jnp.where(y_hi == 0, b[:, 1], b[:, 0]).astype(BF).reshape(flat)
+        a_keep = jnp.where(parity == 0, a[:, 0], a[:, 1])
+        b_keep = jnp.where(y_hi == 0, b[:, 0], b[:, 1])
+        packed = pack(sums)
+        packed = jnp.concatenate([packed[:, :lane], packed[:, lane:]], axis=0)
+        got_b = lax.ppermute(b_send, MP, YHI_SWAP)
+        got_a0 = lax.ppermute(
+            jnp.concatenate([a_send[:, :lane], packed], axis=0), MP, Z_PAIR
+        )
+        got_a1 = lax.ppermute(a_send[:, lane:], MP, Z_BETWEEN)
+        many = NZ // 2 * half
+        got_sums = jnp.concatenate([got_a0[many : many + 16], got_a0[many + 16 :]], axis=1)
+        sums = unpack(sums, got_sums)
+        got_a = jnp.concatenate([got_a0[:many], got_a1], axis=1)
+        a = (a_keep + got_a.astype(F32).reshape(a_keep.shape)).astype(BF)
+        b = (b_keep + got_b.astype(F32).reshape(b_keep.shape)).astype(BF)
+
     with jax.named_scope("sum_over_z"):
-        parts = lax.all_to_all(pair, MP, 0, 0, axis_index_groups=SAME_YHI, tiled=True)
+        riding = jnp.broadcast_to(pack(sums)[None], (NZ // 2, 16, rows))
+        parts = lax.all_to_all(
+            jnp.concatenate([a, b, riding], axis=1), MP, 0, 0,
+            axis_index_groups=Z_PARITY, tiled=True,
+        )
         total = jnp.sum(parts.astype(F32), axis=0)
-        dnormed = total[:share].T
-        plain = (total[share] + total[share + 1])[:, None]
-        cross = (total[share + 2] + total[share + 3])[:, None]
+        dnormed = total[:share]
+        plain = total[share : share + 1] + total[share + 2 : share + 3]
+        cross = total[share + 1 : share + 2] + total[share + 3 : share + 4]
 
     with jax.named_scope("input_gradient"):
         start = mp * share
-        xhat_share = lax.dynamic_slice_in_dim(xhat, start, share, 1)
+        xhat_share = lax.dynamic_slice_in_dim(xhat, start, share, 1).T
         gain_share = lax.dynamic_slice_in_dim(layer_norm_gain, start, share, 0)
         input_gradient_rows = (
-            (dnormed * gain_share - plain / width - xhat_share * (cross / width)) * inverse
-        ).astype(BF)
-        gain_portion = jnp.sum(dnormed * xhat_share, axis=0)
+            (dnormed * gain_share[:, None] - plain / width - xhat_share * (cross / width))
+            * inverse.T
+        ).T.astype(BF)
+        gain_portion = jnp.sum(dnormed * xhat_share, axis=1)
 
     with jax.named_scope("gain_gradients"):
         small = jnp.concatenate(

time: 154 us -> 159 us (1.032)
  the two profiles are of different devices: /device:TPU:33 before, /device:TPU:16 now
where the time goes in v2:
time: 159 us
  waiting for transfers between devices  49.2 us (31%)
  starting transfers between devices  41.4 us (26%)
  blocking collectives  21.8 us (14%)
  between operations  14.6 us (9%)
  other arithmetic  14.1 us (9%)
  matrix products  8.97 us (6%)
  local copies, waits for them, and re-layouts  8.53 us (5%)
    all_to_all x1, blocking collectives, per_device(): lax.all_to_all(copies, DP, 0, 0, axis_index_groups=SAME_CORE, tiled=True)  21.8 us
    all_to_all x1, waiting for transfers between devices, per_device(): lax.all_to_all(jnp.concatenate([a, b, riding], axis=1), MP, 0, 0, axis_in...  19.9 us
    reduce_scatter x1, waiting for transfers between devices, per_device(): lax.psum_scatter(chip.reshape(-1, columns), DP, scatter_dimension=0, tile...  16.8 us
    ppermute x1, starting transfers between devices, per_device(): got_b1 = lax.ppermute(send_b[:, lane:], MP, Z_BETWEEN)  11.4 us
    dot_general x16, matrix products, dot(): lax.dot_general(a, b, (((ca,), (cb,)), ((), ())), preferred_element_type=...  8.97 us
    all_to_all x1, starting transfers between devices, per_device(): lax.all_to_all(jnp.concatenate([a, b, riding], axis=1), MP, 0, 0, axis_in...  8.66 us
    all_to_all x1, waiting for transfers between devices, per_device(): summed = jnp.sum(lax.all_to_all(copies, DP, 0, 0, tiled=True), axis=0)  5.49 us
    ppermute x1, starting transfers between devices, per_device(): got_b = lax.ppermute(b_send, MP, YHI_SWAP)  4.81 us
  transfers between devices with their start and end apart: 11, of which 7 were waited for; matrix products, arithmetic and copies ran while one was open for 10% of the time, Pallas kernels for 0%

profile of v2, /device:TPU:16, one launch (start us, length us, event | category | flops | bytes accessed | tf_op | source)
XLA Modules:
  0.0 158.6 jit_solution(11778739384043293601)
XLA Ops:
  7.2 1.0 broadcast_in_dim.14
  8.2 21.8 %all_to_all.15 = bf16[8,192,384]{2,1,0:T(8,128)(2,1)S(1)} all-to-all(bf16[8,192,384]{2,1,0:T(8,128)(2,1)S(1)} %broadcast_in_dim.14), channel_id=1, replica_groups={{0,64,128,192,256,320,384,448},{32,96,160,224,288,352,416,480},{1,65,12..., dimensions={0} | all-to-all | bytes 2359296 | tf_op jit(solution)/shard_map/gather_w/all_to_all | solution.py:93
  30.0 1.9 %collective-permute-start = (bf16[8,192,384]{2,1,0:T(8,128)(2,1)S(1)}, bf16[8,192,384]{2,1,0:T(8,128)(2,1)}, u32[]{:S(2)}, u32[]{:S(2)}) collective-permute-start(bf16[8,192,384]{2,1,0:T(8,128)(2,1)S(1)} %all_to_all.15), channel_id=1, source_target_pairs={{0,32},{32,0},{64,96},{96,64},{128,160},{160,128},{192,224},{224,1... | collective-permute-start | bytes 3538952 | tf_op jit(solution)/shard_map/gather_w/ppermute | solution.py:94
  32.0 0.1 mul.210
  32.1 1.7 %copy.39 = bf16[256,3072]{0,1:T(8,128)(2,1)S(1)} copy(bf16[256,3072]{1,0:T(8,128)(2,1)} %param.6) | data formatting | bytes 3145728 | tf_op args[0]
  33.8 0.4 convert_reduce_fusion
  34.3 0.5 fusion.2
  34.7 0.1 collective-permute-done
  34.9 1.5 broadcast_select_fusion.1
  36.4 0.3 pad_maximum_fusion
  36.7 2.0 %fusion.13 = f32[256,384]{1,0:T(8,128)S(1)} fusion(bf16[3072,384]{1,0:T(8,128)(2,1)S(1)} %bitcast.109, f32[3072]{0:T(1024)S(1)} %copy-done.3, f32[256]{0:T(256)S(1)} %add_rsqrt_fusion.2, f32[256]{0:T(256)S(1)} %broadcast_multiply_fusion.6, bf16[256,3072]{0,1:T(8,128)(2,1)S(1)} %copy.39), kind=kOutput, calls=%fused_computation.52 | convolution fusion | flops 607911936 | bytes 4339712 | tf_op jit(solution)/shard_map/attention/dot_general | solution.py:38
  38.7 0.1 slice_reduce_fusion.1
  38.8 0.2 multiply_reduce_fusion.7
  39.1 0.3 fusion.53
  39.5 0.2 convolution_convert_fusion.3
  39.7 0.2 multiply_reduce_fusion.1
  39.9 0.7 multiply_reduce_fusion
  40.6 0.3 fusion.23
  40.9 0.5 multiply_reduce_fusion.3
  41.5 0.3 multiply_convert_fusion.5
  41.9 1.0 convolution_convert_fusion
  42.9 0.2 fusion.26
  43.1 0.2 convolution_add_fusion.2
  43.3 0.2 fusion.11
  43.5 0.2 fusion.4
  43.6 2.3 %collective-permute-start.1 = (bf16[8,192,384]{2,1,0:T(8,128)(2,1)S(1)}, bf16[8,192,384]{2,1,0:T(8,128)(2,1)S(1)}, u32[]{:S(2)}, u32[]{:S(2)}) collective-permute-start(bf16[8,192,384]{2,1,0:T(8,128)(2,1)S(1)} %fusion.4), channel_id=1, source_target_pairs={{0,32},{32,0},{64,96},{96,64},{128,160},{160,128},{192,224},{224,1... | collective-permute-start | bytes 3538952 | tf_op jit(solution)/shard_map/w_grad/ppermute | solution.py:142
  45.9 0.1 pad_maximum_fusion.2
  46.0 0.1 broadcast_select_fusion.5
  46.2 0.2 fusion.27
  46.4 0.4 convolution_convert_fusion.2
  46.8 2.5 %collective-permute-start.2 = (bf16[784,256]{1,0:T(8,128)(2,1)S(1)}, bf16[784,256]{1,0:T(8,128)(2,1)S(1)}, u32[]{:S(2)}, u32[]{:S(2)}) collective-permute-start(bf16[784,256]{1,0:T(8,128)(2,1)S(1)} %pad_maximum_fusion.4), channel_id=1, source_target_pairs={{0,1},{1,0},{2,3},{3,2},{4,5},{5,4},{6,7},{7,6},{8,9},{9,8},{10,11... | collective-permute-start | bytes 1204232 | tf_op jit(solution)/shard_map/input_gradient_partial/ppermute | solution.py:132
  49.3 0.9 broadcast_select_fusion.2
  50.2 0.4 convolution_convert_fusion.1
  50.7 11.4 %collective-permute-start.4 = (bf16[768,128]{1,0:T(8,128)(2,1)S(1)}, bf16[768,128]{1,0:T(8,128)(2,1)S(1)}, u32[]{:S(2)}, u32[]{:S(2)}) collective-permute-start(bf16[768,128]{1,0:T(8,128)(2,1)S(1)} %get-tuple-element.38), channel_id=1, source_target_pairs={{0,30},{1,31},{2,4},{3,5},{4,2},{5,3},{6,8},{7,9},{8,6},{9,7},{10,... | collective-permute-start | bytes 589832 | tf_op jit(solution)/shard_map/input_gradient_partial/ppermute | solution.py:134
  62.1 1.9 %collective-permute-start.3 = (bf16[768,128]{1,0:T(8,128)(2,1)S(1)}, bf16[768,128]{1,0:T(8,128)(2,1)S(1)}, u32[]{:S(2)}, u32[]{:S(2)}) collective-permute-start(bf16[768,128]{1,0:T(8,128)(2,1)S(1)} %get-tuple-element.39), channel_id=1, source_target_pairs={{0,2},{1,3},{2,0},{3,1},{4,6},{5,7},{6,4},{7,5},{8,10},{9,11},{10,... | collective-permute-start | bytes 589832 | tf_op jit(solution)/shard_map/input_gradient_partial/ppermute | solution.py:133
  64.0 1.5 fusion.3
  65.6 1.5 collective-permute-done.4
  67.0 3.4 %collective-permute-done.3 = bf16[768,128]{1,0:T(8,128)(2,1)S(1)} collective-permute-done((bf16[768,128]{1,0:T(8,128)(2,1)S(1)}, bf16[768,128]{1,0:T(8,128)(2,1)S(1)}, u32[]{:S(2)}, u32[]{:S(2)}) %collective-permute-start.3) | collective-permute-done | bytes 196640 | tf_op jit(solution)/shard_map/input_gradient_partial/ppermute | solution.py:133
  70.4 0.7 copy-done.7
  71.1 0.4 convert_add_fusion.1
  71.7 0.7 fusion.49
  72.3 2.2 %collective-permute-start.6 = (bf16[384,128]{1,0:T(8,128)(2,1)}, bf16[384,128]{1,0:T(8,128)(2,1)}, u32[]{:S(2)}, u32[]{:S(2)}) collective-permute-start(bf16[384,128]{1,0:T(8,128)(2,1)} %get-tuple-element.42), channel_id=1, source_target_pairs={{0,30},{1,31},{2,4},{3,5},{4,2},{5,3},{6,8},{7,9},{8,6},{9,7},{10,... | collective-permute-start | bytes 294920 | tf_op jit(solution)/shard_map/sum_over_pairs/ppermute | solution.py:168
  74.5 1.9 %collective-permute-start.5 = (bf16[416,128]{1,0:T(8,128)(2,1)S(1)}, bf16[416,128]{1,0:T(8,128)(2,1)S(1)}, u32[]{:S(2)}, u32[]{:S(2)}) collective-permute-start(bf16[416,128]{1,0:T(8,128)(2,1)S(1)} %pad_maximum_fusion.6), channel_id=1, source_target_pairs={{0,2},{1,3},{2,0},{3,1},{4,6},{5,7},{6,4},{7,5},{8,10},{9,11},{10,... | collective-permute-start | bytes 319496 | tf_op jit(solution)/shard_map/sum_over_pairs/ppermute | solution.py:165
  76.4 1.6 %convolution_add_fusion = f32[768,256]{1,0:T(8,128)S(1)} fusion(bf16[768,384]{1,0:T(8,128)(2,1)} %bitcast.114, bf16[768,128]{1,0:T(8,128)(2,1)} %copy-done.6, bf16[768,128]{1,0:T(8,128)(2,1)} %copy-done.7, bf16[256,128]{1,0:T(8,128)(2,1)S(1)} %convolution_convert_fusion.3, bf16[256,128]{1,0:T(8,128)(2,1)S(1)} %get-tuple-element.41, ...), kind=kOutput, calls=%fused_computation.12 | convolution fusion | flops 152567808 | bytes 1966080 | tf_op jit(solution)/shard_map/input_gradient_partial/dot_general | solution.py:38
  78.1 0.9 copy-done.1
  79.0 4.8 %collective-permute-start.7 = (bf16[384,256]{1,0:T(8,128)(2,1)S(1)}, bf16[384,256]{1,0:T(8,128)(2,1)S(1)}, u32[]{:S(2)}, u32[]{:S(2)}) collective-permute-start(bf16[384,256]{1,0:T(8,128)(2,1)S(1)} %bitcast.118), channel_id=1, source_target_pairs={{0,1},{1,0},{2,3},{3,2},{4,5},{5,4},{6,7},{7,6},{8,9},{9,8},{10,11... | collective-permute-start | bytes 589832 | tf_op jit(solution)/shard_map/sum_over_pairs/ppermute | solution.py:164
  83.8 0.6 copy-done.2
  84.5 0.9 slice.179
  85.4 1.0 fusion.9
  86.5 1.6 collective-permute-done.7
  88.0 1.2 fusion.8
  89.2 0.8 pad_maximum_fusion.3
  90.1 8.7 %all-to-all-start.1 = ((bf16[8,112,256]{2,1,0:T(8,128)(2,1)}), bf16[8,112,256]{2,1,0:T(8,128)(2,1)S(1)}, u32[]{:S(2)}, u32[]{:S(2)}) async-start(bf16[8,112,256]{2,1,0:T(8,128)(2,1)} %pad_maximum_fusion.3), calls=%async_computation.1 | async-start | bytes 917504 | tf_op jit(solution)/shard_map/sum_over_z/all_to_all | solution.py:178
  98.9 0.5 reduce-scatter.2.cloned.1.call-update
  99.4 2.0 %fusion = f32[256,3072]{0,1:T(8,128)} fusion(bf16[256,3072]{0,1:T(8,128)(2,1)S(1)} %copy.39, f32[256]{0:T(256)S(1)} %add_rsqrt_fusion.2, f32[256]{0:T(256)S(1)} %broadcast_multiply_fusion.6), kind=kLoop, calls=%fused_computation.4 | loop fusion | flops 2359296 | bytes 4720640 | tf_op jit(solution)/shard_map/input_norm/mul | solution.py:103
  101.4 19.9 %all-to-all-done.1 = bf16[8,112,256]{2,1,0:T(8,128)(2,1)S(1)} async-done(((bf16[8,112,256]{2,1,0:T(8,128)(2,1)}), bf16[8,112,256]{2,1,0:T(8,128)(2,1)S(1)}, u32[]{:S(2)}, u32[]{:S(2)}) %all-to-all-start.1) | async-done | bytes 458784 | tf_op jit(solution)/shard_map/sum_over_z/all_to_all | solution.py:178
  121.4 1.7 %fusion.19 = (f32[96]{0:T(128)S(1)}, bf16[256,96]{0,1:T(8,128)(2,1)}) fusion(f32[112,256]{1,0:T(8,128)S(1)} %convert_reduce_fusion.1, f32[256,3072]{0,1:T(8,128)} %fusion, s32[]{:T(128)S(6)} %select_n.167, f32[256]{0:T(256)S(1)} %add_rsqrt_fusion.2, f32[256]{0:T(256)S(1)} %bitcast.125, f32[256]{0:T(256)S(1)} %bitcast.124, f32[96]{0:T(128)S(1)} %dynamic_slice.6), kind=kLoop, calls=%fused_computation.80 | loop fusion | flops 196512 | bytes 249604 | tf_op jit(solution)/shard_map/input_gradient/reduce_sum | solution.py:195
  123.2 0.6 broadcast_in_dim.20
  123.8 3.7 %all-to-all-start.2 = ((f32[16,8,128]{2,1,0:T(8,128)}), f32[16,8,128]{2,1,0:T(8,128)S(1)}, u32[]{:S(2)}, u32[]{:S(2)}) async-start(f32[16,8,128]{2,1,0:T(8,128)} %broadcast_in_dim.20), calls=%async_computation.2 | async-start | bytes 131072 | tf_op jit(solution)/shard_map/gain_gradients/all_to_all | solution.py:208
  127.6 0.9 convolution_convert_fusion.4
  128.4 5.5 %all-to-all-done.2 = f32[16,8,128]{2,1,0:T(8,128)S(1)} async-done(((f32[16,8,128]{2,1,0:T(8,128)}), f32[16,8,128]{2,1,0:T(8,128)S(1)}, u32[]{:S(2)}, u32[]{:S(2)}) %all-to-all-start.2) | async-done | bytes 65568 | tf_op jit(solution)/shard_map/gain_gradients/all_to_all | solution.py:208
  134.0 0.5 slice_bitcast_fusion.2
  134.5 0.5 fusion.52
  135.0 16.8 %reduce-scatter.2.cloned.1.call-done = bf16[192,384]{1,0:T(8,128)(2,1)} async-done(((bf16[1536,384]{1,0:T(8,128)(2,1)}), bf16[192,384]{1,0:T(8,128)(2,1)}) %reduce-scatter.2.cloned.1.call-update) | async-done | bytes 147472 | tf_op jit(solution)/shard_map/w_grad/reduce_scatter | solution.py:145
  (53 shorter events, 0.9 us)
Async XLA Ops:
  7.2 32.3 %copy-start = (bf16[256,128]{1,0:T(8,128)(2,1)S(1)}, bf16[256,128]{1,0:T(8,128)(2,1)}, u32[]{:S(2)}) copy-start(bf16[256,128]{1,0:T(8,128)(2,1)} %param.11) | copy-start | bytes 196612
  7.2 24.8 %copy-start.3 = (f32[3072]{0:T(1024)S(1)}, f32[3072]{0:T(1024)}, u32[]{:S(2)}) copy-start(f32[3072]{0:T(1024)} %param.7) | copy-start | bytes 36868
  30.0 4.9 %collective-permute-start = (bf16[8,192,384]{2,1,0:T(8,128)(2,1)S(1)}, bf16[8,192,384]{2,1,0:T(8,128)(2,1)}, u32[]{:S(2)}, u32[]{:S(2)}) collective-permute-start(bf16[8,192,384]{2,1,0:T(8,128)(2,1)S(1)} %all_to_all.15), channel_id=1, source_target_pairs={{0,32},{32,0},{64,96},{96,64},{128,160},{160,128},{192,224},{224,1... | collective-permute-start | bytes 3538952 | tf_op jit(solution)/shard_map/gather_w/ppermute | solution.py:94
  36.7 2.4 %copy-start.4 = (f32[1,128]{1,0:T(1,128)S(1)}, f32[1,128]{1,0:T(1,128)}, u32[]{:S(2)}) copy-start(f32[1,128]{1,0:T(1,128)} %param.9) | copy-start | bytes 1540
  36.7 2.4 %copy-start.5 = (f32[1,128]{1,0:T(1,128)S(1)}, f32[1,128]{1,0:T(1,128)}, u32[]{:S(2)}) copy-start(f32[1,128]{1,0:T(1,128)} %param.10) | copy-start | bytes 1540
  43.6 20.4 %collective-permute-start.1 = (bf16[8,192,384]{2,1,0:T(8,128)(2,1)S(1)}, bf16[8,192,384]{2,1,0:T(8,128)(2,1)S(1)}, u32[]{:S(2)}, u32[]{:S(2)}) collective-permute-start(bf16[8,192,384]{2,1,0:T(8,128)(2,1)S(1)} %fusion.4), channel_id=1, source_target_pairs={{0,32},{32,0},{64,96},{96,64},{128,160},{160,128},{192,224},{224,1... | collective-permute-start | bytes 3538952 | tf_op jit(solution)/shard_map/w_grad/ppermute | solution.py:142
  46.8 23.6 %collective-permute-start.2 = (bf16[784,256]{1,0:T(8,128)(2,1)S(1)}, bf16[784,256]{1,0:T(8,128)(2,1)S(1)}, u32[]{:S(2)}, u32[]{:S(2)}) collective-permute-start(bf16[784,256]{1,0:T(8,128)(2,1)S(1)} %pad_maximum_fusion.4), channel_id=1, source_target_pairs={{0,1},{1,0},{2,3},{3,2},{4,5},{5,4},{6,7},{7,6},{8,9},{9,8},{10,11... | collective-permute-start | bytes 1204232 | tf_op jit(solution)/shard_map/input_gradient_partial/ppermute | solution.py:132
  50.7 16.4 %collective-permute-start.4 = (bf16[768,128]{1,0:T(8,128)(2,1)S(1)}, bf16[768,128]{1,0:T(8,128)(2,1)S(1)}, u32[]{:S(2)}, u32[]{:S(2)}) collective-permute-start(bf16[768,128]{1,0:T(8,128)(2,1)S(1)} %get-tuple-element.38), channel_id=1, source_target_pairs={{0,30},{1,31},{2,4},{3,5},{4,2},{5,3},{6,8},{7,9},{8,6},{9,7},{10,... | collective-permute-start | bytes 589832 | tf_op jit(solution)/shard_map/input_gradient_partial/ppermute | solution.py:134
  62.1 8.3 %collective-permute-start.3 = (bf16[768,128]{1,0:T(8,128)(2,1)S(1)}, bf16[768,128]{1,0:T(8,128)(2,1)S(1)}, u32[]{:S(2)}, u32[]{:S(2)}) collective-permute-start(bf16[768,128]{1,0:T(8,128)(2,1)S(1)} %get-tuple-element.39), channel_id=1, source_target_pairs={{0,2},{1,3},{2,0},{3,1},{4,6},{5,7},{6,4},{7,5},{8,10},{9,11},{10,... | collective-permute-start | bytes 589832 | tf_op jit(solution)/shard_map/input_gradient_partial/ppermute | solution.py:133
  67.0 3.4 %copy-start.6 = (bf16[768,128]{1,0:T(8,128)(2,1)}, bf16[768,128]{1,0:T(8,128)(2,1)S(1)}, u32[]{:S(2)}) copy-start(bf16[768,128]{1,0:T(8,128)(2,1)S(1)} %collective-permute-done.4) | copy-start | bytes 589828
  70.4 0.7 copy-start.7
  72.3 13.1 %collective-permute-start.6 = (bf16[384,128]{1,0:T(8,128)(2,1)}, bf16[384,128]{1,0:T(8,128)(2,1)}, u32[]{:S(2)}, u32[]{:S(2)}) collective-permute-start(bf16[384,128]{1,0:T(8,128)(2,1)} %get-tuple-element.42), channel_id=1, source_target_pairs={{0,30},{1,31},{2,4},{3,5},{4,2},{5,3},{6,8},{7,9},{8,6},{9,7},{10,... | collective-permute-start | bytes 294920 | tf_op jit(solution)/shard_map/sum_over_pairs/ppermute | solution.py:168
  74.5 9.3 %collective-permute-start.5 = (bf16[416,128]{1,0:T(8,128)(2,1)S(1)}, bf16[416,128]{1,0:T(8,128)(2,1)S(1)}, u32[]{:S(2)}, u32[]{:S(2)}) collective-permute-start(bf16[416,128]{1,0:T(8,128)(2,1)S(1)} %pad_maximum_fusion.6), channel_id=1, source_target_pairs={{0,2},{1,3},{2,0},{3,1},{4,6},{5,7},{6,4},{7,5},{8,10},{9,11},{10,... | collective-permute-start | bytes 319496 | tf_op jit(solution)/shard_map/sum_over_pairs/ppermute | solution.py:165
  78.1 0.9 copy-start.1
  79.0 9.1 %collective-permute-start.7 = (bf16[384,256]{1,0:T(8,128)(2,1)S(1)}, bf16[384,256]{1,0:T(8,128)(2,1)S(1)}, u32[]{:S(2)}, u32[]{:S(2)}) collective-permute-start(bf16[384,256]{1,0:T(8,128)(2,1)S(1)} %bitcast.118), channel_id=1, source_target_pairs={{0,1},{1,0},{2,3},{3,2},{4,5},{5,4},{6,7},{7,6},{8,9},{9,8},{10,11... | collective-permute-start | bytes 589832 | tf_op jit(solution)/shard_map/sum_over_pairs/ppermute | solution.py:164
  83.8 0.6 copy-start.2
  90.1 31.3 %all-to-all-start.1 = ((bf16[8,112,256]{2,1,0:T(8,128)(2,1)}), bf16[8,112,256]{2,1,0:T(8,128)(2,1)S(1)}, u32[]{:S(2)}, u32[]{:S(2)}) async-start(bf16[8,112,256]{2,1,0:T(8,128)(2,1)} %pad_maximum_fusion.3), calls=%async_computation.1 | async-start | bytes 917504 | tf_op jit(solution)/shard_map/sum_over_z/all_to_all | solution.py:178
  98.7 53.0 %reduce-scatter.2.cloned.1.call-start = ((), (), s32[]{:S(2)}) async-start(), calls=%async_computation.4 | async-start | bytes 1327104 | tf_op jit(solution)/shard_map/w_grad/reduce_scatter | solution.py:145
  123.8 10.1 %all-to-all-start.2 = ((f32[16,8,128]{2,1,0:T(8,128)}), f32[16,8,128]{2,1,0:T(8,128)S(1)}, u32[]{:S(2)}, u32[]{:S(2)}) async-start(f32[16,8,128]{2,1,0:T(8,128)} %broadcast_in_dim.20), calls=%async_computation.2 | async-start | bytes 131072 | tf_op jit(solution)/shard_map/gain_gradients/all_to_all | solution.py:208
Sparse Core Ops, SparseCore 0:
  102.9 48.7 reduce-scatter.1

commit v3 on v1

--- a/solution.py
+++ b/solution.py
@@ -12,6 +12,11 @@
 
 CORE_SWAP = [(i, i ^ 1) for i in range(NX * NYL * NC)]
 SAME_CORE = [[2 * i + c for i in range(NX * NYL)] for c in range(NC)]
+YLO_SWAP = [(i, i ^ 2) for i in range(NX * NYL * NC)]
+X_STEPS = [
+    [(i, (i + step * NYL * NC) % (NX * NYL * NC)) for i in range(NX * NYL * NC)]
+    for step in range(1, NX)
+]
 YHI_SWAP = [(j, j ^ 1) for j in range(NZ * NYH)]
 SAME_YHI = [[2 * z + y for z in range(NZ)] for y in range(NYH)]
 
@@ -62,13 +67,35 @@
     return hi, lo
 
 
+def pack(sums):
+    hi, lo = hi_lo(sums)
+    row = lax.broadcasted_iota(jnp.int32, sums.shape, 0)
+    rows = jnp.where(row % 4 < 2, hi, lo)
+    return jnp.concatenate([rows, jnp.zeros_like(rows)], axis=0)
+
+
+def unpack(got):
+    got = got.astype(F32)
+    first, second = got[0:2] + got[2:4], got[4:6] + got[6:8]
+    return jnp.concatenate([first, first, second, second], axis=0)
+
+
+def after(value, other):
+    first = other.reshape(-1, other.shape[-1])[:1, :128].astype(F32)
+    zero = jnp.minimum(jnp.abs(first), 0.0)
+    return value + jnp.concatenate([zero] * (value.shape[-1] // 128), axis=1)
+
+
 def per_device(tokens, layer_norm_gain, w_qkv, q_gain, k_gain, ctx_grad):
     rows, width = tokens.shape
     w_rows, columns = w_qkv.shape
     share = width // (NZ * NYH)
     core = lax.axis_index(DP) % 2
+    y_lo = (lax.axis_index(DP) // NC) % NYL
+    x_at = lax.axis_index(DP) // (NYL * NC)
     y_hi = lax.axis_index(MP) % 2
     mp = lax.axis_index(MP)
+    lane = rows // 2
 
     with jax.named_scope("gather_w"):
         copies = jnp.broadcast_to(w_qkv[None], (NX * NYL, w_rows, columns))
@@ -89,59 +116,78 @@
         qkv = dot(normed, full, 1, 0)
         context, dqkv, q_part, k_part = attend(qkv, ctx_grad, q_gain, k_gain)
 
+    with jax.named_scope("patch_sums"):
+        weighted = jnp.sum(full.astype(F32) * layer_norm_gain[:, None], axis=0, keepdims=True)
+        row = lax.broadcasted_iota(jnp.int32, (8, columns), 0)
+        w_hi, w_lo = hi_lo(jnp.where(row % 2 == 0, weighted, 0.0))
+        ones = (row % 2 == 1).astype(BF)
+        p_hi, p_lo = hi_lo(dqkv.astype(F32) * qkv)
+        sums = (dot(w_hi, dqkv, 1, 1) + dot(w_lo, dqkv, 1, 1)) + (
+            dot(ones, p_hi, 1, 1) + dot(ones, p_lo, 1, 1)
+        )
+        sums = jnp.concatenate([sums[:4, :lane], sums[:4, lane:]], axis=0)
+
     with jax.named_scope("input_gradient_partial"):
-        dqkv_f = dqkv.astype(F32)
-        weighted = jnp.sum(full.astype(F32) * layer_norm_gain[:, None], axis=0)
-        s1 = jnp.sum(dqkv_f * weighted[None, :], axis=1)
-        s2 = jnp.sum(dqkv_f * qkv, axis=1)
         by_y = full.reshape(NZ, NYH, share, columns)
         w_keep = jnp.where(y_hi == 0, by_y[:, 0], by_y[:, 1]).reshape(-1, columns)
         w_send = jnp.where(y_hi == 0, by_y[:, 1], by_y[:, 0]).reshape(-1, columns)
-        part_send = dot(w_send, dqkv, 1, 1).astype(BF)
-        part_keep = dot(w_keep, dqkv, 1, 1)
-        h1, l1 = hi_lo(s1)
-        h2, l2 = hi_lo(s2)
-        sums = jnp.concatenate(
-            [jnp.stack([h1, l1, h2, l2]), jnp.zeros((12, rows), BF)], axis=0
-        )
-        got = lax.ppermute(part_send, MP, YHI_SWAP).astype(F32)
-        got_sums = lax.ppermute(sums, MP, YHI_SWAP).astype(F32)
-        t1 = s1 + got_sums[0] + got_sums[1]
-        t2 = s2 + got_sums[2] + got_sums[3]
-        h1, l1 = hi_lo(t1)
-        h2, l2 = hi_lo(t2)
-        sums = jnp.concatenate(
-            [jnp.stack([h1, l1, h2, l2]), jnp.zeros((12, rows), BF)], axis=0
-        )
-        pair = (part_keep + got).astype(BF).reshape(NZ, share, rows)
-        pair = jnp.concatenate([pair, jnp.broadcast_to(sums[None], (NZ, 16, rows))], axis=1)
+        send_a = dot(w_send, dqkv[:lane], 1, 1).astype(BF)
+        got_a = lax.ppermute(send_a, MP, YHI_SWAP)
 
     with jax.named_scope("w_grad"):
-        term = dot(normed, dqkv, 0, 0).astype(BF).reshape(NX * NYL, NC, w_rows, columns)
+        term = after(dot(normed, dqkv, 0, 0), send_a)
+        term = term.astype(BF).reshape(NX * NYL, NC, w_rows, columns)
         term_keep = jnp.where(core == 0, term[:, 0], term[:, 1])
         term_send = jnp.where(core == 0, term[:, 1], term[:, 0])
         term_got = lax.ppermute(term_send, DP, CORE_SWAP)
         chip = (term_keep.astype(F32) + term_got.astype(F32)).astype(BF)
-        w_grad = lax.psum_scatter(
-            chip.reshape(-1, columns), DP, scatter_dimension=0, tiled=True,
-            axis_index_groups=SAME_CORE,
+
+    with jax.named_scope("sum_over_y"):
+        pair_a = dot(w_keep, dqkv[:lane], 1, 1) + got_a.astype(F32)
+        pair_a = after(pair_a, chip).astype(BF).reshape(NZ, share, lane)
+        send_b = after(dot(w_send, dqkv[lane:], 1, 1), pair_a)
+        send_b = jnp.concatenate([send_b.astype(BF), pack(sums)], axis=0)
+        got_b = lax.ppermute(send_b, MP, YHI_SWAP)
+
+    with jax.named_scope("sum_over_y_second"):
+        many = NZ * share
+        pair_b = dot(w_keep, dqkv[lane:], 1, 1) + got_b[:many].astype(F32)
+        pair_b = pair_b.astype(BF)
+        sums = sums + unpack(got_b[many:])
+        riding = jnp.broadcast_to(pack(sums)[None], (NZ, 16, lane))
+        pair_b = jnp.concatenate([pair_b.reshape(NZ, share, lane), riding], axis=1)
+
+    with jax.named_scope("w_grad_chips"):
+        ready = after(chip.astype(F32), send_b).astype(BF).reshape(NX, NYL, w_rows, columns)
+        x_term = lax.dynamic_index_in_dim(ready, x_at, 0, False).astype(F32)
+        for step, pairs in enumerate(X_STEPS, 1):
+            leaves = lax.dynamic_index_in_dim(ready, (x_at + step) % NX, 0, False)
+            x_term = x_term + lax.ppermute(leaves, DP, pairs).astype(F32)
+        x_term = after(x_term, pair_b)
+        leaves = jnp.where(y_lo == 0, x_term[1], x_term[0]).astype(BF)
+        stays = jnp.where(y_lo == 0, x_term[0], x_term[1])
+        w_grad = (stays + lax.ppermute(leaves, DP, YLO_SWAP).astype(F32)).astype(BF)
+
+    with jax.named_scope("sum_over_z"):
+        exchange = lambda pair: lax.all_to_all(
+            pair, MP, 0, 0, axis_index_groups=SAME_YHI, tiled=True
         )
-
-    with jax.named_scope("sum_over_z"):
-        parts = lax.all_to_all(pair, MP, 0, 0, axis_index_groups=SAME_YHI, tiled=True)
-        total = jnp.sum(parts.astype(F32), axis=0)
-        dnormed = total[:share].T
-        plain = (total[share] + total[share + 1])[:, None]
-        cross = (total[share + 2] + total[share + 3])[:, None]
+        sum_a = jnp.sum(exchange(pair_a).astype(F32), axis=0)
+        sum_b = jnp.sum(exchange(pair_b).astype(F32), axis=0)
+        dnormed = jnp.concatenate([sum_a, sum_b[:share]], axis=1)
+        sums = unpack(sum_b[share:])
+        plain = jnp.concatenate([sums[0:1], sums[4:5]], axis=1)
+        cross = jnp.concatenate([sums[1:2], sums[5:6]], axis=1)
 
     with jax.named_scope("input_gradient"):
         start = mp * share
-        xhat_share = lax.dynamic_slice_in_dim(xhat, start, share, 1)
+        xhat_share = lax.dynamic_slice_in_dim(xhat, start, share, 1).T
         gain_share = lax.dynamic_slice_in_dim(layer_norm_gain, start, share, 0)
         input_gradient_rows = (
-            (dnormed * gain_share - plain / width - xhat_share * (cross / width)) * inverse
-        ).astype(BF)
-        gain_portion = jnp.sum(dnormed * xhat_share, axis=0)
+            (dnormed * gain_share[:, None] - plain / width - xhat_share * (cross / width))
+            * inverse.T
+        ).T.astype(BF)
+        gain_portion = jnp.sum(dnormed * xhat_share, axis=1)
 
     with jax.named_scope("gain_gradients"):
         small = jnp.concatenate(

time: 154 us -> 140 us (0.909)
  the two profiles are of different devices: /device:TPU:33 before, /device:TPU:1 now
where the time goes in v3:
time: 140 us; the launch traced here: 139 us
  starting transfers between devices  72.1 us (51%)
  waiting for transfers between devices  35.9 us (26%)
  other arithmetic  14.5 us (10%)
  matrix products  9.52 us (7%)
  local copies, waits for them, and re-layouts  5.92 us (4%)
    all_to_all x2, starting transfers between devices, per_device(): lax.all_to_all(pair, MP, 0, 0, axis_index_groups=SAME_YHI, tiled=True)  27.1 us
    all_to_all x1, waiting for transfers between devices, per_device(): lax.all_to_all(copies, DP, 0, 0, axis_index_groups=SAME_CORE, tiled=True)  11.3 us
    all_to_all x1, starting transfers between devices, per_device(): summed = jnp.sum(lax.all_to_all(copies, DP, 0, 0, tiled=True), axis=0)  9.68 us
    dot_general x16, matrix products, dot(): lax.dot_general(a, b, (((ca,), (cb,)), ((), ())), preferred_element_type=...  9.52 us
    ppermute x3, starting transfers between devices, per_device(): x_term = x_term + lax.ppermute(leaves, DP, pairs).astype(F32)  8.41 us
    ppermute x3, waiting for transfers between devices, per_device(): x_term = x_term + lax.ppermute(leaves, DP, pairs).astype(F32)  6.8 us
    ppermute x1, starting transfers between devices, per_device(): other = lax.ppermute(own, DP, CORE_SWAP)  6.66 us
    ppermute x1, waiting for transfers between devices, per_device(): got_b = lax.ppermute(send_b, MP, YHI_SWAP)  6.24 us
  transfers between devices with their start and end apart: 12, of which 10 were waited for; matrix products, arithmetic and copies ran while one was open for 14% of the time, Pallas kernels for 0%

profile of v3, /device:TPU:1, one launch (start us, length us, event | category | flops | bytes accessed | tf_op | source)
XLA Modules:
  0.0 139.1 jit_solution(18420525532957193755)
XLA Ops:
  0.6 2.1 %broadcast_in_dim.22 = bf16[8,192,384]{2,1,0:T(8,128)(2,1)} broadcast(bf16[192,384]{1,0:T(8,128)(2,1)} %param.8), dimensions={1,2} | broadcast | bytes 1327104 | tf_op jit(solution)/shard_map/gather_w/broadcast_in_dim | solution.py:101
  2.7 6.0 %all-to-all-start = ((bf16[8,192,384]{2,1,0:T(8,128)(2,1)}), bf16[8,192,384]{2,1,0:T(8,128)(2,1)S(1)}, u32[]{:S(2)}, u32[]{:S(2)}) async-start(bf16[8,192,384]{2,1,0:T(8,128)(2,1)} %broadcast_in_dim.22), calls=%async_computation | async-start | bytes 2359296 | tf_op jit(solution)/shard_map/gather_w/all_to_all | solution.py:102
  8.9 1.7 %copy.29 = bf16[256,3072]{0,1:T(8,128)(2,1)S(1)} copy(bf16[256,3072]{1,0:T(8,128)(2,1)} %param.6) | data formatting | bytes 3145728 | tf_op args[0]
  10.8 11.3 %all-to-all-done = bf16[8,192,384]{2,1,0:T(8,128)(2,1)S(1)} async-done(((bf16[8,192,384]{2,1,0:T(8,128)(2,1)}), bf16[8,192,384]{2,1,0:T(8,128)(2,1)S(1)}, u32[]{:S(2)}, u32[]{:S(2)}) %all-to-all-start) | async-done | bytes 1179680 | tf_op jit(solution)/shard_map/gather_w/all_to_all | solution.py:102
  22.1 6.7 %collective-permute-start = (bf16[8,192,384]{2,1,0:T(8,128)(2,1)S(1)}, bf16[8,192,384]{2,1,0:T(8,128)(2,1)S(1)}, u32[]{:S(2)}, u32[]{:S(2)}) collective-permute-start(bf16[8,192,384]{2,1,0:T(8,128)(2,1)S(1)} %all-to-all-done), channel_id=1, source_target_pairs={{0,32},{32,0},{64,96},{96,64},{128,160},{160,128},{192,224},{224,1... | collective-permute-start | bytes 3538952 | tf_op jit(solution)/shard_map/gather_w/ppermute | solution.py:103
  28.8 0.4 convert_reduce_fusion
  29.2 0.5 fusion.2
  29.7 1.5 %collective-permute-done = bf16[8,192,384]{2,1,0:T(8,128)(2,1)S(1)} collective-permute-done((bf16[8,192,384]{2,1,0:T(8,128)(2,1)S(1)}, bf16[8,192,384]{2,1,0:T(8,128)(2,1)S(1)}, u32[]{:S(2)}, u32[]{:S(2)}) %collective-permute-start) | collective-permute-done | bytes 1179680 | tf_op jit(solution)/shard_map/gather_w/ppermute | solution.py:103
  31.2 0.2 select_bitcast_fusion.2
  31.4 0.3 pad_maximum_fusion
  31.7 2.0 %fusion.14 = f32[256,384]{1,0:T(8,128)S(1)} fusion(bf16[3072,384]{1,0:T(8,128)(2,1)S(1)} %bitcast.101, f32[3072]{0:T(1024)S(1)} %copy-done.6, f32[256]{0:T(256)S(1)} %add_rsqrt_fusion.2, f32[256]{0:T(256)S(1)} %broadcast_multiply_fusion.6, bf16[256,3072]{0,1:T(8,128)(2,1)S(1)} %copy.29), kind=kOutput, calls=%fused_computation.52 | convolution fusion | flops 607911936 | bytes 4339712 | tf_op jit(solution)/shard_map/attention/dot_general | solution.py:37
  33.7 0.1 slice_reduce_fusion.1
  33.8 0.2 multiply_reduce_fusion.7
  34.1 0.3 fusion.86
  34.5 0.2 convolution_convert_fusion.1
  34.7 0.2 multiply_reduce_fusion.1
  34.9 0.3 fusion.35
  35.2 0.5 multiply_reduce_fusion.3
  35.8 0.2 broadcast_select_fusion.1
  36.1 0.3 multiply_convert_fusion.5
  36.4 0.5 convolution_convert_fusion
  36.9 5.3 %collective-permute-start.1 = (bf16[1536,128]{1,0:T(8,128)(2,1)S(1)}, bf16[1536,128]{1,0:T(8,128)(2,1)S(1)}, u32[]{:S(2)}, u32[]{:S(2)}) collective-permute-start(bf16[1536,128]{1,0:T(8,128)(2,1)S(1)} %convolution_convert_fusion), channel_id=1, source_target_pairs={{0,1},{1,0},{2,3},{3,2},{4,5},{5,4},{6,7},{7,6},{8,9},{9,8},{10,11... | collective-permute-start | bytes 1179656 | tf_op jit(solution)/shard_map/input_gradient_partial/ppermute | solution.py:135
  42.2 0.7 multiply_reduce_fusion
  42.9 1.7 %add_convert_fusion = bf16[3072,384]{1,0:T(8,128)(2,1)S(1)} fusion(bf16[256,384]{1,0:T(8,128)(2,1)S(1)} %pad_maximum_fusion.2, f32[384]{0:T(512)S(1)} %maximum_reduce_fusion, f32[3072]{0:T(1024)S(1)} %copy-done.6, f32[256]{0:T(256)S(1)} %add_rsqrt_fusion.2, f32[256]{0:T(256)S(1)} %broadcast_multiply_fusion.6, bf16[256,3072]{0,1:T(8,128)(2,1)S(1)} %copy.29), kind=kOutput, calls=%fused_computation.1 | convolution fusion | flops 610271232 | bytes 4144640 | tf_op jit(solution)/shard_map/w_grad/dot_general | solution.py:37
  44.8 2.6 %collective-permute-start.2 = (bf16[8,192,384]{2,1,0:T(8,128)(2,1)S(1)}, bf16[8,192,384]{2,1,0:T(8,128)(2,1)S(1)}, u32[]{:S(2)}, u32[]{:S(2)}) collective-permute-start(bf16[8,192,384]{2,1,0:T(8,128)(2,1)S(1)} %select_bitcast_fusion), channel_id=1, source_target_pairs={{0,32},{32,0},{64,96},{96,64},{128,160},{160,128},{192,224},{224,1... | collective-permute-start | bytes 3538952 | tf_op jit(solution)/shard_map/w_grad/ppermute | solution.py:142
  47.4 0.2 fusion.38
  47.6 0.2 convolution_add_fusion.2
  47.7 0.2 fusion.12
  47.9 0.2 fusion.6
  48.2 1.6 %collective-permute-done.2 = bf16[8,192,384]{2,1,0:T(8,128)(2,1)S(1)} collective-permute-done((bf16[8,192,384]{2,1,0:T(8,128)(2,1)S(1)}, bf16[8,192,384]{2,1,0:T(8,128)(2,1)S(1)}, u32[]{:S(2)}, u32[]{:S(2)}) %collective-permute-start.2) | collective-permute-done | bytes 1179680 | tf_op jit(solution)/shard_map/w_grad/ppermute | solution.py:142
  49.8 0.5 fusion.4
  50.3 1.1 collective-permute-done.1
  51.4 0.5 add_convert_fusion.3
  51.9 1.2 fusion.3
  53.1 15.0 %all-to-all-start.1 = ((bf16[16,96,128]{2,1,0:T(8,128)(2,1)}), bf16[16,96,128]{2,1,0:T(8,128)(2,1)}, u32[]{:S(2)}, u32[]{:S(2)}) async-start(bf16[16,96,128]{2,1,0:T(8,128)(2,1)} %bitcast.108), calls=%async_computation.1 | async-start | bytes 786432 | tf_op jit(solution)/shard_map/sum_over_z/all_to_all | solution.py:172
  68.1 1.3 maximum_maximum_fusion
  69.4 4.5 %collective-permute-start.3 = (bf16[1552,128]{1,0:T(8,128)(2,1)S(1)}, bf16[1552,128]{1,0:T(8,128)(2,1)S(1)}, u32[]{:S(2)}, u32[]{:S(2)}) collective-permute-start(bf16[1552,128]{1,0:T(8,128)(2,1)S(1)} %maximum_maximum_fusion), channel_id=1, source_target_pairs={{0,1},{1,0},{2,3},{3,2},{4,5},{5,4},{6,7},{7,6},{8,9},{9,8},{10,11... | collective-permute-start | bytes 1191944 | tf_op jit(solution)/shard_map/sum_over_y/ppermute | solution.py:150
  73.9 2.0 %fusion = f32[256,3072]{0,1:T(8,128)} fusion(bf16[256,3072]{0,1:T(8,128)(2,1)S(1)} %copy.29, f32[256]{0:T(256)S(1)} %add_rsqrt_fusion.2, f32[256]{0:T(256)S(1)} %broadcast_multiply_fusion.6), kind=kLoop, calls=%fused_computation.4 | loop fusion | flops 2359296 | bytes 4720640 | tf_op jit(solution)/shard_map/input_norm/mul | solution.py:112
  75.9 6.2 %collective-permute-done.3 = bf16[1552,128]{1,0:T(8,128)(2,1)S(1)} collective-permute-done((bf16[1552,128]{1,0:T(8,128)(2,1)S(1)}, bf16[1552,128]{1,0:T(8,128)(2,1)S(1)}, u32[]{:S(2)}, u32[]{:S(2)}) %collective-permute-start.3) | collective-permute-done | bytes 397344 | tf_op jit(solution)/shard_map/sum_over_y/ppermute | solution.py:150
  82.2 0.5 add_convert_fusion.2
  82.7 0.8 pad_maximum_fusion.1
  83.5 2.2 %all-to-all-done.1 = bf16[16,96,128]{2,1,0:T(8,128)(2,1)} async-done(((bf16[16,96,128]{2,1,0:T(8,128)(2,1)}), bf16[16,96,128]{2,1,0:T(8,128)(2,1)}, u32[]{:S(2)}, u32[]{:S(2)}) %all-to-all-start.1) | async-done | bytes 393248 | tf_op jit(solution)/shard_map/sum_over_z/all_to_all | solution.py:172
  85.7 12.1 %all-to-all-start.2 = ((bf16[16,112,128]{2,1,0:T(8,128)(2,1)}), bf16[16,112,128]{2,1,0:T(8,128)(2,1)}, u32[]{:S(2)}, u32[]{:S(2)}) async-start(bf16[16,112,128]{2,1,0:T(8,128)(2,1)} %pad_maximum_fusion.1), calls=%async_computation.2 | async-start | bytes 917504 | tf_op jit(solution)/shard_map/sum_over_z/all_to_all | solution.py:172
  97.8 0.7 fusion.67
  98.5 0.2 add_convert_fusion.1
  98.9 1.9 %collective-permute-start.4 = (bf16[2,192,384]{2,1,0:T(8,128)(2,1)S(1)}, bf16[2,192,384]{2,1,0:T(8,128)(2,1)S(1)}, u32[]{:S(2)}, u32[]{:S(2)}) collective-permute-start(bf16[2,192,384]{2,1,0:T(8,128)(2,1)S(1)} %get-tuple-element.24), channel_id=1, source_target_pairs={{0,128},{32,160},{64,192},{96,224},{128,256},{160,288},{192,320},{... | collective-permute-start | bytes 884744 | tf_op jit(solution)/shard_map/w_grad_chips/ppermute | solution.py:165
  100.8 4.6 %collective-permute-start.6 = (bf16[2,192,384]{2,1,0:T(8,128)(2,1)S(1)}, bf16[2,192,384]{2,1,0:T(8,128)(2,1)S(1)}, u32[]{:S(2)}, u32[]{:S(2)}) collective-permute-start(bf16[2,192,384]{2,1,0:T(8,128)(2,1)S(1)} %get-tuple-element.25), channel_id=1, source_target_pairs={{0,384},{32,416},{64,448},{96,480},{128,0},{160,32},{192,64},{224,... | collective-permute-start | bytes 884744 | tf_op jit(solution)/shard_map/w_grad_chips/ppermute | solution.py:165
  105.4 1.9 %collective-permute-start.5 = (bf16[2,192,384]{2,1,0:T(8,128)(2,1)S(1)}, bf16[2,192,384]{2,1,0:T(8,128)(2,1)S(1)}, u32[]{:S(2)}, u32[]{:S(2)}) collective-permute-start(bf16[2,192,384]{2,1,0:T(8,128)(2,1)S(1)} %get-tuple-element.26), channel_id=1, source_target_pairs={{0,256},{32,288},{64,320},{96,352},{128,384},{160,416},{192,448},{... | collective-permute-start | bytes 884744 | tf_op jit(solution)/shard_map/w_grad_chips/ppermute | solution.py:165
  107.3 0.9 convolution_convert_fusion.2
  108.2 0.7 fusion.65
  108.9 0.4 collective-permute-done.4
  109.3 1.8 %collective-permute-done.6 = bf16[2,192,384]{2,1,0:T(8,128)(2,1)S(1)} collective-permute-done((bf16[2,192,384]{2,1,0:T(8,128)(2,1)S(1)}, bf16[2,192,384]{2,1,0:T(8,128)(2,1)S(1)}, u32[]{:S(2)}, u32[]{:S(2)}) %collective-permute-start.6) | collective-permute-done | bytes 294944 | tf_op jit(solution)/shard_map/w_grad_chips/ppermute | solution.py:165
  111.1 4.6 %collective-permute-done.5 = bf16[2,192,384]{2,1,0:T(8,128)(2,1)S(1)} collective-permute-done((bf16[2,192,384]{2,1,0:T(8,128)(2,1)S(1)}, bf16[2,192,384]{2,1,0:T(8,128)(2,1)S(1)}, u32[]{:S(2)}, u32[]{:S(2)}) %collective-permute-start.5) | collective-permute-done | bytes 294944 | tf_op jit(solution)/shard_map/w_grad_chips/ppermute | solution.py:165
  115.7 0.2 fusion.9
  115.9 1.9 %collective-permute-start.7 = (bf16[192,384]{1,0:T(8,128)(2,1)S(1)}, bf16[192,384]{1,0:T(8,128)(2,1)S(1)}, u32[]{:S(2)}, u32[]{:S(2)}) collective-permute-start(bf16[192,384]{1,0:T(8,128)(2,1)S(1)} %fusion.15), channel_id=1, source_target_pairs={{0,64},{32,96},{64,0},{96,32},{128,192},{160,224},{192,128},{224,1... | collective-permute-start | bytes 442376 | tf_op jit(solution)/shard_map/w_grad_chips/ppermute | solution.py:169
  117.8 1.1 convert_reduce_fusion.2
  118.9 1.1 convert_reduce_fusion.1
  120.1 1.7 %fusion.21 = (f32[96]{0:T(128)S(1)}, bf16[256,96]{0,1:T(8,128)(2,1)}) fusion(f32[256,3072]{0,1:T(8,128)} %fusion, s32[]{:T(128)S(6)} %select_n.165, f32[96,128]{1,0:T(8,128)S(1)} %slice.178, f32[96,128]{1,0:T(8,128)S(1)} %convert_reduce_fusion.2, f32[256]{0:T(256)S(1)} %add_rsqrt_fusion.2, f32[256]{0:T(256)S(1)} %maximum_multiply_fusion.1, ...), kind=kLoop, calls=%fused_computation.81 | loop fusion | flops 221088 | bytes 249604 | tf_op jit(solution)/shard_map/input_gradient/reduce_sum | solution.py:190
  121.9 0.6 broadcast_in_dim.34
  122.5 9.7 %all-to-all-start.3 = ((f32[16,8,128]{2,1,0:T(8,128)}), f32[16,8,128]{2,1,0:T(8,128)S(1)}, u32[]{:S(2)}, u32[]{:S(2)}) async-start(f32[16,8,128]{2,1,0:T(8,128)} %broadcast_in_dim.34), calls=%async_computation.3 | async-start | bytes 131072 | tf_op jit(solution)/shard_map/gain_gradients/all_to_all | solution.py:203
  132.2 0.7 fusion.10
  132.9 5.2 %all-to-all-done.3 = f32[16,8,128]{2,1,0:T(8,128)S(1)} async-done(((f32[16,8,128]{2,1,0:T(8,128)}), f32[16,8,128]{2,1,0:T(8,128)S(1)}, u32[]{:S(2)}, u32[]{:S(2)}) %all-to-all-start.3) | async-done | bytes 65568 | tf_op jit(solution)/shard_map/gain_gradients/all_to_all | solution.py:203
  138.1 0.5 slice_bitcast_fusion.2
  138.6 0.5 fusion.85
  (67 shorter events, 1.2 us)
Async XLA Ops:
  0.6 33.9 %copy-start = (bf16[256,128]{1,0:T(8,128)(2,1)S(1)}, bf16[256,128]{1,0:T(8,128)(2,1)}, u32[]{:S(2)}) copy-start(bf16[256,128]{1,0:T(8,128)(2,1)} %param.11) | copy-start | bytes 196612
  2.7 6.0 %copy-start.6 = (f32[3072]{0:T(1024)S(1)}, f32[3072]{0:T(1024)}, u32[]{:S(2)}) copy-start(f32[3072]{0:T(1024)} %param.7) | copy-start | bytes 36868
  2.7 19.3 %all-to-all-start = ((bf16[8,192,384]{2,1,0:T(8,128)(2,1)}), bf16[8,192,384]{2,1,0:T(8,128)(2,1)S(1)}, u32[]{:S(2)}, u32[]{:S(2)}) async-start(bf16[8,192,384]{2,1,0:T(8,128)(2,1)} %broadcast_in_dim.22), calls=%async_computation | async-start | bytes 2359296 | tf_op jit(solution)/shard_map/gather_w/all_to_all | solution.py:102
  22.1 9.1 %collective-permute-start = (bf16[8,192,384]{2,1,0:T(8,128)(2,1)S(1)}, bf16[8,192,384]{2,1,0:T(8,128)(2,1)S(1)}, u32[]{:S(2)}, u32[]{:S(2)}) collective-permute-start(bf16[8,192,384]{2,1,0:T(8,128)(2,1)S(1)} %all-to-all-done), channel_id=1, source_target_pairs={{0,32},{32,0},{64,96},{96,64},{128,160},{160,128},{192,224},{224,1... | collective-permute-start | bytes 3538952 | tf_op jit(solution)/shard_map/gather_w/ppermute | solution.py:103
  31.7 2.4 %copy-start.7 = (f32[1,128]{1,0:T(1,128)S(1)}, f32[1,128]{1,0:T(1,128)}, u32[]{:S(2)}) copy-start(f32[1,128]{1,0:T(1,128)} %param.9) | copy-start | bytes 1540
  31.7 2.4 %copy-start.8 = (f32[1,128]{1,0:T(1,128)S(1)}, f32[1,128]{1,0:T(1,128)}, u32[]{:S(2)}) copy-start(f32[1,128]{1,0:T(1,128)} %param.10) | copy-start | bytes 1540
  34.5 1.3 copy-start.4
  36.9 14.4 %collective-permute-start.1 = (bf16[1536,128]{1,0:T(8,128)(2,1)S(1)}, bf16[1536,128]{1,0:T(8,128)(2,1)S(1)}, u32[]{:S(2)}, u32[]{:S(2)}) collective-permute-start(bf16[1536,128]{1,0:T(8,128)(2,1)S(1)} %convolution_convert_fusion), channel_id=1, source_target_pairs={{0,1},{1,0},{2,3},{3,2},{4,5},{5,4},{6,7},{7,6},{8,9},{9,8},{10,11... | collective-permute-start | bytes 1179656 | tf_op jit(solution)/shard_map/input_gradient_partial/ppermute | solution.py:135
  44.8 5.0 %collective-permute-start.2 = (bf16[8,192,384]{2,1,0:T(8,128)(2,1)S(1)}, bf16[8,192,384]{2,1,0:T(8,128)(2,1)S(1)}, u32[]{:S(2)}, u32[]{:S(2)}) collective-permute-start(bf16[8,192,384]{2,1,0:T(8,128)(2,1)S(1)} %select_bitcast_fusion), channel_id=1, source_target_pairs={{0,32},{32,0},{64,96},{96,64},{128,160},{160,128},{192,224},{224,1... | collective-permute-start | bytes 3538952 | tf_op jit(solution)/shard_map/w_grad/ppermute | solution.py:142
  50.3 2.8 %copy-start.1 = (bf16[8,192,384]{2,1,0:T(8,128)(2,1)}, bf16[8,192,384]{2,1,0:T(8,128)(2,1)S(1)}, u32[]{:S(2)}) copy-start(bf16[8,192,384]{2,1,0:T(8,128)(2,1)S(1)} %fusion.4) | copy-start | bytes 3538948
  51.9 1.3 copy-start.3
  53.1 32.6 %all-to-all-start.1 = ((bf16[16,96,128]{2,1,0:T(8,128)(2,1)}), bf16[16,96,128]{2,1,0:T(8,128)(2,1)}, u32[]{:S(2)}, u32[]{:S(2)}) async-start(bf16[16,96,128]{2,1,0:T(8,128)(2,1)} %bitcast.108), calls=%async_computation.1 | async-start | bytes 786432 | tf_op jit(solution)/shard_map/sum_over_z/all_to_all | solution.py:172
  69.4 12.7 %collective-permute-start.3 = (bf16[1552,128]{1,0:T(8,128)(2,1)S(1)}, bf16[1552,128]{1,0:T(8,128)(2,1)S(1)}, u32[]{:S(2)}, u32[]{:S(2)}) collective-permute-start(bf16[1552,128]{1,0:T(8,128)(2,1)S(1)} %maximum_maximum_fusion), channel_id=1, source_target_pairs={{0,1},{1,0},{2,3},{3,2},{4,5},{5,4},{6,7},{7,6},{8,9},{9,8},{10,11... | collective-permute-start | bytes 1191944 | tf_op jit(solution)/shard_map/sum_over_y/ppermute | solution.py:150
  82.2 16.3 %copy-start.2 = (bf16[8,192,384]{2,1,0:T(8,128)(2,1)S(1)}, bf16[8,192,384]{2,1,0:T(8,128)(2,1)}, u32[]{:S(2)}) copy-start(bf16[8,192,384]{2,1,0:T(8,128)(2,1)} %copy-done.1) | copy-start | bytes 3538948
  85.7 33.1 %all-to-all-start.2 = ((bf16[16,112,128]{2,1,0:T(8,128)(2,1)}), bf16[16,112,128]{2,1,0:T(8,128)(2,1)}, u32[]{:S(2)}, u32[]{:S(2)}) async-start(bf16[16,112,128]{2,1,0:T(8,128)(2,1)} %pad_maximum_fusion.1), calls=%async_computation.2 | async-start | bytes 917504 | tf_op jit(solution)/shard_map/sum_over_z/all_to_all | solution.py:172
  98.5 8.8 %copy-start.5 = (f32[256,256]{0,1:T(8,128)S(1)}, f32[256,256]{0,1:T(8,128)}, u32[]{:S(2)}) copy-start(f32[256,256]{0,1:T(8,128)} %copy-done.4) | copy-start | bytes 786436
  98.9 10.5 %collective-permute-start.4 = (bf16[2,192,384]{2,1,0:T(8,128)(2,1)S(1)}, bf16[2,192,384]{2,1,0:T(8,128)(2,1)S(1)}, u32[]{:S(2)}, u32[]{:S(2)}) collective-permute-start(bf16[2,192,384]{2,1,0:T(8,128)(2,1)S(1)} %get-tuple-element.24), channel_id=1, source_target_pairs={{0,128},{32,160},{64,192},{96,224},{128,256},{160,288},{192,320},{... | collective-permute-start | bytes 884744 | tf_op jit(solution)/shard_map/w_grad_chips/ppermute | solution.py:165
  100.8 10.3 %collective-permute-start.6 = (bf16[2,192,384]{2,1,0:T(8,128)(2,1)S(1)}, bf16[2,192,384]{2,1,0:T(8,128)(2,1)S(1)}, u32[]{:S(2)}, u32[]{:S(2)}) collective-permute-start(bf16[2,192,384]{2,1,0:T(8,128)(2,1)S(1)} %get-tuple-element.25), channel_id=1, source_target_pairs={{0,384},{32,416},{64,448},{96,480},{128,0},{160,32},{192,64},{224,... | collective-permute-start | bytes 884744 | tf_op jit(solution)/shard_map/w_grad_chips/ppermute | solution.py:165
  105.4 10.3 %collective-permute-start.5 = (bf16[2,192,384]{2,1,0:T(8,128)(2,1)S(1)}, bf16[2,192,384]{2,1,0:T(8,128)(2,1)S(1)}, u32[]{:S(2)}, u32[]{:S(2)}) collective-permute-start(bf16[2,192,384]{2,1,0:T(8,128)(2,1)S(1)} %get-tuple-element.26), channel_id=1, source_target_pairs={{0,256},{32,288},{64,320},{96,352},{128,384},{160,416},{192,448},{... | collective-permute-start | bytes 884744 | tf_op jit(solution)/shard_map/w_grad_chips/ppermute | solution.py:165
  115.9 16.3 %collective-permute-start.7 = (bf16[192,384]{1,0:T(8,128)(2,1)S(1)}, bf16[192,384]{1,0:T(8,128)(2,1)S(1)}, u32[]{:S(2)}, u32[]{:S(2)}) collective-permute-start(bf16[192,384]{1,0:T(8,128)(2,1)S(1)} %fusion.15), channel_id=1, source_target_pairs={{0,64},{32,96},{64,0},{96,32},{128,192},{160,224},{192,128},{224,1... | collective-permute-start | bytes 442376 | tf_op jit(solution)/shard_map/w_grad_chips/ppermute | solution.py:169
  122.5 15.6 %all-to-all-start.3 = ((f32[16,8,128]{2,1,0:T(8,128)}), f32[16,8,128]{2,1,0:T(8,128)S(1)}, u32[]{:S(2)}, u32[]{:S(2)}) async-start(f32[16,8,128]{2,1,0:T(8,128)} %broadcast_in_dim.34), calls=%async_computation.3 | async-start | bytes 131072 | tf_op jit(solution)/shard_map/gain_gradients/all_to_all | solution.py:203

commit v4 on v3

--- a/solution.py
+++ b/solution.py
@@ -17,8 +17,8 @@
     [(i, (i + step * NYL * NC) % (NX * NYL * NC)) for i in range(NX * NYL * NC)]
     for step in range(1, NX)
 ]
-YHI_SWAP = [(j, j ^ 1) for j in range(NZ * NYH)]
-SAME_YHI = [[2 * z + y for z in range(NZ)] for y in range(NYH)]
+NEAR = [[2 * z + j for j in range(2 * NYH)] for z in range(0, NZ, 2)]
+FAR = [[2 * NYH * k + j for k in range(NZ // 2)] for j in range(2 * NYH)]
 
 
 def head_norm(raw):
@@ -93,7 +93,6 @@
     core = lax.axis_index(DP) % 2
     y_lo = (lax.axis_index(DP) // NC) % NYL
     x_at = lax.axis_index(DP) // (NYL * NC)
-    y_hi = lax.axis_index(MP) % 2
     mp = lax.axis_index(MP)
     lane = rows // 2
 
@@ -128,54 +127,47 @@
         sums = jnp.concatenate([sums[:4, :lane], sums[:4, lane:]], axis=0)
 
     with jax.named_scope("input_gradient_partial"):
-        by_y = full.reshape(NZ, NYH, share, columns)
-        w_keep = jnp.where(y_hi == 0, by_y[:, 0], by_y[:, 1]).reshape(-1, columns)
-        w_send = jnp.where(y_hi == 0, by_y[:, 1], by_y[:, 0]).reshape(-1, columns)
-        send_a = dot(w_send, dqkv[:lane], 1, 1).astype(BF)
-        got_a = lax.ppermute(send_a, MP, YHI_SWAP)
+        chunk = 2 * share
+        part = dot(full, dqkv, 1, 1).astype(BF)
+        part = part.reshape(NZ // 2, 2 * NYH, share, 2, lane)
+        part = part.transpose(1, 0, 3, 2, 4).reshape(2 * NYH, NZ // 2 * chunk, lane)
+        riding = jnp.broadcast_to(pack(sums)[None], (2 * NYH, 16, lane))
+        part = jnp.concatenate([part, riding], axis=1)
+        near = lax.all_to_all(part, MP, 0, 0, axis_index_groups=NEAR, tiled=True)
 
     with jax.named_scope("w_grad"):
-        term = after(dot(normed, dqkv, 0, 0), send_a)
+        term = after(dot(normed, dqkv, 0, 0), part)
         term = term.astype(BF).reshape(NX * NYL, NC, w_rows, columns)
         term_keep = jnp.where(core == 0, term[:, 0], term[:, 1])
         term_send = jnp.where(core == 0, term[:, 1], term[:, 0])
         term_got = lax.ppermute(term_send, DP, CORE_SWAP)
         chip = (term_keep.astype(F32) + term_got.astype(F32)).astype(BF)
-
-    with jax.named_scope("sum_over_y"):
-        pair_a = dot(w_keep, dqkv[:lane], 1, 1) + got_a.astype(F32)
-        pair_a = after(pair_a, chip).astype(BF).reshape(NZ, share, lane)
-        send_b = after(dot(w_send, dqkv[lane:], 1, 1), pair_a)
-        send_b = jnp.concatenate([send_b.astype(BF), pack(sums)], axis=0)
-        got_b = lax.ppermute(send_b, MP, YHI_SWAP)
-
-    with jax.named_scope("sum_over_y_second"):
-        many = NZ * share
-        pair_b = dot(w_keep, dqkv[lane:], 1, 1) + got_b[:many].astype(F32)
-        pair_b = pair_b.astype(BF)
-        sums = sums + unpack(got_b[many:])
-        riding = jnp.broadcast_to(pack(sums)[None], (NZ, 16, lane))
-        pair_b = jnp.concatenate([pair_b.reshape(NZ, share, lane), riding], axis=1)
-
-    with jax.named_scope("w_grad_chips"):
-        ready = after(chip.astype(F32), send_b).astype(BF).reshape(NX, NYL, w_rows, columns)
-        x_term = lax.dynamic_index_in_dim(ready, x_at, 0, False).astype(F32)
+        chip = chip.reshape(NX, NYL, w_rows, columns)
+        x_term = lax.dynamic_index_in_dim(chip, x_at, 0, False).astype(F32)
         for step, pairs in enumerate(X_STEPS, 1):
-            leaves = lax.dynamic_index_in_dim(ready, (x_at + step) % NX, 0, False)
+            leaves = lax.dynamic_index_in_dim(chip, (x_at + step) % NX, 0, False)
             x_term = x_term + lax.ppermute(leaves, DP, pairs).astype(F32)
-        x_term = after(x_term, pair_b)
+
+    with jax.named_scope("sum_over_near"):
+        many = NZ // 2 * chunk
+        pair = jnp.sum(near[:, :many].astype(F32), axis=0)
+        pair = after(pair, chip).astype(BF).reshape(NZ // 2, chunk, lane)
+        sums = near[:, many:].astype(F32)
+        sums = unpack(sums[0]) + unpack(sums[1]) + unpack(sums[2]) + unpack(sums[3])
+        riding = jnp.broadcast_to(pack(sums)[None], (NZ // 2, 16, lane))
+        pair = jnp.concatenate([pair, riding], axis=1)
+        far = lax.all_to_all(pair, MP, 0, 0, axis_index_groups=FAR, tiled=True)
+
+    with jax.named_scope("w_grad_y"):
+        x_term = after(x_term, pair)
         leaves = jnp.where(y_lo == 0, x_term[1], x_term[0]).astype(BF)
         stays = jnp.where(y_lo == 0, x_term[0], x_term[1])
         w_grad = (stays + lax.ppermute(leaves, DP, YLO_SWAP).astype(F32)).astype(BF)
 
-    with jax.named_scope("sum_over_z"):
-        exchange = lambda pair: lax.all_to_all(
-            pair, MP, 0, 0, axis_index_groups=SAME_YHI, tiled=True
-        )
-        sum_a = jnp.sum(exchange(pair_a).astype(F32), axis=0)
-        sum_b = jnp.sum(exchange(pair_b).astype(F32), axis=0)
-        dnormed = jnp.concatenate([sum_a, sum_b[:share]], axis=1)
-        sums = unpack(sum_b[share:])
+    with jax.named_scope("sum_over_far"):
+        total = jnp.sum(far.astype(F32), axis=0)
+        dnormed = jnp.concatenate([total[:share], total[share:chunk]], axis=1)
+        sums = unpack(total[chunk:])
         plain = jnp.concatenate([sums[0:1], sums[4:5]], axis=1)
         cross = jnp.concatenate([sums[1:2], sums[5:6]], axis=1)
 

time: 140 us -> 128 us (0.914)
  starting transfers between devices: 72.1 us -> 55.6 us
  local copies, waits for them, and re-layouts: 5.92 us -> 13.4 us
  waiting for transfers between devices: 35.9 us -> 29.5 us
  other arithmetic: 14.5 us -> 16.8 us
    ppermute x2 -> x0, starting transfers between devices: 9.78 us -> none  [the longest x1 5.27 us: per_device(): got_a = lax.ppermute(send_a, MP, YHI_SWAP)]
    ppermute x2 -> x0, waiting for transfers between devices: 7.3 us -> none  [the longest x1 6.24 us: per_device(): got_b = lax.ppermute(send_b, MP, YHI_SWAP)]
    all_to_all x2, starting transfers between devices: 27.1 us -> 19.9 us  [the longest x1 13.9 us: per_device(): far = lax.all_to_all(pair, MP, 0, 0, axis_index_groups=FAR, tiled=True)]
    all_to_all x2, waiting for transfers between devices: 2.19 us -> 5.79 us  [the longest x1 5.79 us: per_device(): near = lax.all_to_all(part, MP, 0, 0, axis_index_groups=NEAR, tiled=True)]
    unnamed x19 -> x61, local copies, waits for them, and re-layouts: 1.75 us -> 4.87 us
    convert_element_type x1, other arithmetic: 0.47 us -> 2.44 us  [per_device(): chip = (term_keep.astype(F32) + term_got.astype(F32)).astype(BF)]
    reshape x0 -> x1, local copies, waits for them, and re-layouts: none -> 1.88 us  [per_device(): part = part.reshape(NZ // 2, 2 * NYH, share, 2, lane)]
    reduce_sum x2, other arithmetic: 2.15 us -> 0.29 us  [the longest x1 0.23 us: per_device(): pair = jnp.sum(near[:, :many].astype(F32), axis=0)]
  transfers between devices with their start and end apart: 12 -> 10, of which waited for: 10 -> 7; matrix products, arithmetic and copies ran while one was open for 14% -> 16% of each run, Pallas kernels for 0% -> 0%
where the time goes in v4:
time: 128 us; the launch traced here: 127 us
  starting transfers between devices  55.6 us (43%)
  waiting for transfers between devices  29.5 us (23%)
  other arithmetic  16.8 us (13%)
  local copies, waits for them, and re-layouts  13.4 us (10%)
  matrix products  10.1 us (8%)
  between operations  1.4 us (1%)
    all_to_all x1, starting transfers between devices, per_device(): far = lax.all_to_all(pair, MP, 0, 0, axis_index_groups=FAR, tiled=True)  13.9 us
    all_to_all x1, waiting for transfers between devices, per_device(): lax.all_to_all(copies, DP, 0, 0, axis_index_groups=SAME_CORE, tiled=True)  10.5 us
    all_to_all x1, starting transfers between devices, per_device(): summed = jnp.sum(lax.all_to_all(copies, DP, 0, 0, tiled=True), axis=0)  10.3 us
    dot_general x13, matrix products, dot(): lax.dot_general(a, b, (((ca,), (cb,)), ((), ())), preferred_element_type=...  10.1 us
    ppermute x3, starting transfers between devices, per_device(): x_term = x_term + lax.ppermute(leaves, DP, pairs).astype(F32)  8.41 us
    ppermute x1, starting transfers between devices, per_device(): other = lax.ppermute(own, DP, CORE_SWAP)  6.66 us
    all_to_all x1, starting transfers between devices, per_device(): near = lax.all_to_all(part, MP, 0, 0, axis_index_groups=NEAR, tiled=True)  5.98 us
    all_to_all x1, starting transfers between devices, per_device(): lax.all_to_all(copies, DP, 0, 0, axis_index_groups=SAME_CORE, tiled=True)  5.86 us
  transfers between devices with their start and end apart: 10, of which 7 were waited for; matrix products, arithmetic and copies ran while one was open for 16% of the time, Pallas kernels for 0%

profile of v4, /device:TPU:1, one launch (start us, length us, event | category | flops | bytes accessed | tf_op | source)
XLA Modules:
  0.0 126.7 jit_solution(4124956573350287084)
XLA Ops:
  0.7 2.1 %broadcast_in_dim.24 = bf16[8,192,384]{2,1,0:T(8,128)(2,1)} broadcast(bf16[192,384]{1,0:T(8,128)(2,1)} %param.8), dimensions={1,2} | broadcast | bytes 1327104 | tf_op jit(solution)/shard_map/gather_w/broadcast_in_dim | solution.py:100
  2.7 5.9 %all-to-all-start = ((bf16[8,192,384]{2,1,0:T(8,128)(2,1)}), bf16[8,192,384]{2,1,0:T(8,128)(2,1)S(1)}, u32[]{:S(2)}, u32[]{:S(2)}) async-start(bf16[8,192,384]{2,1,0:T(8,128)(2,1)} %broadcast_in_dim.24), calls=%async_computation | async-start | bytes 2359296 | tf_op jit(solution)/shard_map/gather_w/all_to_all | solution.py:101
  8.7 1.7 %copy.35 = bf16[256,3072]{0,1:T(8,128)(2,1)S(1)} copy(bf16[256,3072]{1,0:T(8,128)(2,1)} %param.6) | data formatting | bytes 3145728 | tf_op args[0]
  10.4 0.5 broadcast_add_fusion
  10.9 0.5 iota_and_fusion
  11.4 10.5 %all-to-all-done = bf16[8,192,384]{2,1,0:T(8,128)(2,1)S(1)} async-done(((bf16[8,192,384]{2,1,0:T(8,128)(2,1)}), bf16[8,192,384]{2,1,0:T(8,128)(2,1)S(1)}, u32[]{:S(2)}, u32[]{:S(2)}) %all-to-all-start) | async-done | bytes 1179680 | tf_op jit(solution)/shard_map/gather_w/all_to_all | solution.py:101
  21.9 6.7 %collective-permute-start = (bf16[8,192,384]{2,1,0:T(8,128)(2,1)S(1)}, bf16[8,192,384]{2,1,0:T(8,128)(2,1)S(1)}, u32[]{:S(2)}, u32[]{:S(2)}) collective-permute-start(bf16[8,192,384]{2,1,0:T(8,128)(2,1)S(1)} %all-to-all-done), channel_id=1, source_target_pairs={{0,32},{32,0},{64,96},{96,64},{128,160},{160,128},{192,224},{224,1... | collective-permute-start | bytes 3538952 | tf_op jit(solution)/shard_map/gather_w/ppermute | solution.py:102
  28.6 0.5 compare_and_fusion
  29.1 0.4 convert_reduce_fusion
  29.6 0.5 fusion.2
  30.1 1.0 collective-permute-done
  31.1 0.2 select_bitcast_fusion.1
  31.3 0.3 pad_maximum_fusion
  31.6 2.0 %fusion.15 = f32[256,384]{1,0:T(8,128)S(1)} fusion(bf16[3072,384]{1,0:T(8,128)(2,1)S(1)} %bitcast.108, f32[3072]{0:T(1024)S(1)} %copy-done.10, f32[256]{0:T(256)S(1)} %add_rsqrt_fusion.2, f32[256]{0:T(256)S(1)} %broadcast_multiply_fusion.6, bf16[256,3072]{0,1:T(8,128)(2,1)S(1)} %copy.35), kind=kOutput, calls=%fused_computation.47 | convolution fusion | flops 607911936 | bytes 4339712 | tf_op jit(solution)/shard_map/attention/dot_general | solution.py:37
  33.6 0.1 slice_reduce_fusion.1
  33.8 0.2 multiply_reduce_fusion.7
  34.0 0.3 fusion.84
  34.4 0.2 convolution_convert_fusion.1
  34.6 0.2 multiply_reduce_fusion.1
  34.8 0.7 multiply_reduce_fusion
  35.6 0.3 fusion.26
  35.9 1.0 multiply_reduce_fusion.3
  36.9 0.3 multiply_convert_fusion.5
  37.3 0.6 copy-done.6
  37.9 1.0 convolution_convert_fusion
  38.9 1.9 %reshape.190 = bf16[8,4,96,2,128]{4,3,2,1,0:T(2,128)(2,1)} reshape(bf16[3072,256]{1,0:T(8,128)(2,1)S(1)} %convolution_convert_fusion) | data formatting | bytes 3145728 | tf_op jit(solution)/shard_map/input_gradient_partial/reshape | solution.py:132
  40.8 1.8 %copy.40 = bf16[4,8,2,96,128]{4,3,2,1,0:T(8,128)(2,1)S(1)} copy(bf16[4,8,2,96,128]{4,2,3,0,1:T(2,128)(2,1)} %bitcast.114) | data formatting | bytes 3145728 | tf_op jit(solution)/shard_map/input_gradient_partial/transpose | solution.py:133
  42.7 0.2 fusion.13
  42.9 0.2 fusion.29
  43.1 0.2 convolution_add_fusion.1
  43.3 0.2 fusion.7
  43.6 1.3 %pad_maximum_fusion.1 = bf16[4,1552,128]{2,1,0:T(8,128)(2,1)} fusion(bf16[4,16,128]{2,1,0:T(8,128)(2,1)S(1)} %broadcast_in_dim.31, bf16[4,1536,128]{2,1,0:T(8,128)(2,1)S(1)} %bitcast.113), kind=kLoop, calls=%fused_computation.14 | loop fusion | flops 3178496 | bytes 3178496 | tf_op jit(solution)/shard_map/input_gradient_partial/concatenate | solution.py:135
  44.9 6.0 %all-to-all-start.1 = ((bf16[4,1552,128]{2,1,0:T(8,128)(2,1)}), bf16[4,1552,128]{2,1,0:T(8,128)(2,1)S(1)}, u32[]{:S(2)}, u32[]{:S(2)}) async-start(bf16[4,1552,128]{2,1,0:T(8,128)(2,1)} %pad_maximum_fusion.1), calls=%async_computation.1 | async-start | bytes 3178496 | tf_op jit(solution)/shard_map/input_gradient_partial/all_to_all | solution.py:136
  50.9 0.7 fusion.72
  51.6 2.5 %add_convert_fusion = bf16[3072,384]{1,0:T(8,128)(2,1)S(1)} fusion(f32[384]{0:T(512)S(1)} %maximum_reduce_fusion, f32[3072]{0:T(1024)} %param.7, f32[256]{0:T(256)} %copy-done.11, f32[256]{0:T(256)} %copy-done.13, bf16[256,3072]{0,1:T(8,128)(2,1)S(1)} %copy.35, bf16[256,128]{1,0:T(8,128)(2,1)} %copy-done.8, bf16[256,128]{1,0:T(8,128)(2,1)} %copy-done.6, ...), kind=kOutput, calls=%fused_computation | convolution fusion | flops 610861056 | bytes 4144640 | tf_op jit(solution)/shard_map/w_grad/dot_general | solution.py:37
  54.1 1.4 %copy-done.1 = bf16[3072,384]{1,0:T(8,128)(2,1)} copy-done((bf16[3072,384]{1,0:T(8,128)(2,1)}, bf16[3072,384]{1,0:T(8,128)(2,1)S(1)}, u32[]{:S(2)}) %copy-start.1) | copy-done | bytes 2359320
  55.5 1.2 fusion.4
  56.7 2.6 %collective-permute-start.1 = (bf16[8,192,384]{2,1,0:T(8,128)(2,1)}, bf16[8,192,384]{2,1,0:T(8,128)(2,1)}, u32[]{:S(2)}, u32[]{:S(2)}) collective-permute-start(bf16[8,192,384]{2,1,0:T(8,128)(2,1)} %fusion.4), channel_id=1, source_target_pairs={{0,32},{32,0},{64,96},{96,64},{128,160},{160,128},{192,224},{224,1... | collective-permute-start | bytes 3538952 | tf_op jit(solution)/shard_map/w_grad/ppermute | solution.py:143
  59.4 0.8 dynamic_slice.19
  60.2 1.8 %collective-permute-done.1 = bf16[8,192,384]{2,1,0:T(8,128)(2,1)} collective-permute-done((bf16[8,192,384]{2,1,0:T(8,128)(2,1)}, bf16[8,192,384]{2,1,0:T(8,128)(2,1)}, u32[]{:S(2)}, u32[]{:S(2)}) %collective-permute-start.1) | collective-permute-done | bytes 1179680 | tf_op jit(solution)/shard_map/w_grad/ppermute | solution.py:143
  62.0 2.4 %fusion.3 = bf16[8,192,384]{2,1,0:T(8,128)(2,1)S(1)} fusion(bf16[8,192,384]{2,1,0:T(8,128)(2,1)} %collective-permute-done.1, pred[]{:T(512)S(6)} %eq.34, bf16[8,2,192,384]{3,2,1,0:T(8,128)(2,1)} %bitcast.111), kind=kLoop, calls=%fused_computation.12 | loop fusion | flops 2949120 | bytes 4718593 | tf_op jit(solution)/shard_map/w_grad/convert_element_type | solution.py:144
  64.5 1.0 copy-done.2
  65.5 5.8 %all-to-all-done.1 = bf16[4,1552,128]{2,1,0:T(8,128)(2,1)S(1)} async-done(((bf16[4,1552,128]{2,1,0:T(8,128)(2,1)}), bf16[4,1552,128]{2,1,0:T(8,128)(2,1)S(1)}, u32[]{:S(2)}, u32[]{:S(2)}) %all-to-all-start.1) | async-done | bytes 1589280 | tf_op jit(solution)/shard_map/input_gradient_partial/all_to_all | solution.py:136
  71.5 0.2 convert_reduce_fusion.1
  71.8 0.8 pad_maximum_fusion.2
  72.6 13.9 %all-to-all-start.2 = ((bf16[8,208,128]{2,1,0:T(8,128)(2,1)}), bf16[8,208,128]{2,1,0:T(8,128)(2,1)S(1)}, u32[]{:S(2)}, u32[]{:S(2)}) async-start(bf16[8,208,128]{2,1,0:T(8,128)(2,1)} %pad_maximum_fusion.2), calls=%async_computation.2 | async-start | bytes 851968 | tf_op jit(solution)/shard_map/sum_over_near/all_to_all | solution.py:159
  86.5 2.0 %fusion = f32[256,3072]{0,1:T(8,128)} fusion(bf16[256,3072]{0,1:T(8,128)(2,1)S(1)} %copy.35, f32[256]{0:T(256)S(1)} %copy-done.12, f32[256]{0:T(256)S(1)} %copy-done.14), kind=kLoop, calls=%fused_computation.5 | loop fusion | flops 2359296 | bytes 4720640 | tf_op jit(solution)/shard_map/input_norm/mul | solution.py:111
  88.5 0.1 dynamic-slice_bitcast_fusion.2
  88.6 1.9 %collective-permute-start.2 = (bf16[2,192,384]{2,1,0:T(8,128)(2,1)S(1)}, bf16[2,192,384]{2,1,0:T(8,128)(2,1)S(1)}, u32[]{:S(2)}, u32[]{:S(2)}) collective-permute-start(bf16[2,192,384]{2,1,0:T(8,128)(2,1)S(1)} %get-tuple-element.22), channel_id=1, source_target_pairs={{0,128},{32,160},{64,192},{96,224},{128,256},{160,288},{192,320},{... | collective-permute-start | bytes 884744 | tf_op jit(solution)/shard_map/w_grad/ppermute | solution.py:149
  90.5 4.6 %collective-permute-start.4 = (bf16[2,192,384]{2,1,0:T(8,128)(2,1)S(1)}, bf16[2,192,384]{2,1,0:T(8,128)(2,1)S(1)}, u32[]{:S(2)}, u32[]{:S(2)}) collective-permute-start(bf16[2,192,384]{2,1,0:T(8,128)(2,1)S(1)} %get-tuple-element.23), channel_id=1, source_target_pairs={{0,384},{32,416},{64,448},{96,480},{128,0},{160,32},{192,64},{224,... | collective-permute-start | bytes 884744 | tf_op jit(solution)/shard_map/w_grad/ppermute | solution.py:149
  95.1 1.9 %collective-permute-start.3 = (bf16[2,192,384]{2,1,0:T(8,128)(2,1)S(1)}, bf16[2,192,384]{2,1,0:T(8,128)(2,1)S(1)}, u32[]{:S(2)}, u32[]{:S(2)}) collective-permute-start(bf16[2,192,384]{2,1,0:T(8,128)(2,1)S(1)} %get-tuple-element.24), channel_id=1, source_target_pairs={{0,256},{32,288},{64,320},{96,352},{128,384},{160,416},{192,448},{... | collective-permute-start | bytes 884744 | tf_op jit(solution)/shard_map/w_grad/ppermute | solution.py:149
  97.1 1.8 %convolution_convert_fusion.2 = bf16[256,128]{1,0:T(8,128)(2,1)} fusion(f32[256,384]{1,0:T(8,128)} %copy-done.4, f32[256,256]{0,1:T(8,128)S(1)} %get-tuple-element.48, f32[256]{0:T(256)S(1)} %copy-done.17), kind=kOutput, calls=%fused_computation.24 | convolution fusion | flops 16941056 | bytes 394240 | tf_op jit(solution)/shard_map/attention/dot_general | solution.py:37
  98.8 0.7 fusion.67
  99.5 0.8 collective-permute-done.4
  100.3 4.5 %collective-permute-done.3 = bf16[2,192,384]{2,1,0:T(8,128)(2,1)S(1)} collective-permute-done((bf16[2,192,384]{2,1,0:T(8,128)(2,1)S(1)}, bf16[2,192,384]{2,1,0:T(8,128)(2,1)S(1)}, u32[]{:S(2)}, u32[]{:S(2)}) %collective-permute-start.3) | collective-permute-done | bytes 294944 | tf_op jit(solution)/shard_map/w_grad/ppermute | solution.py:149
  104.8 0.2 fusion.10
  105.0 1.9 %collective-permute-start.5 = (bf16[192,384]{1,0:T(8,128)(2,1)S(1)}, bf16[192,384]{1,0:T(8,128)(2,1)S(1)}, u32[]{:S(2)}, u32[]{:S(2)}) collective-permute-start(bf16[192,384]{1,0:T(8,128)(2,1)S(1)} %fusion.16), channel_id=1, source_target_pairs={{0,64},{32,96},{64,0},{96,32},{128,192},{160,224},{192,128},{224,1... | collective-permute-start | bytes 442376 | tf_op jit(solution)/shard_map/w_grad_y/ppermute | solution.py:165
  107.1 1.7 %fusion.22 = (f32[96]{0:T(128)S(1)}, bf16[256,96]{0,1:T(8,128)(2,1)}) fusion(f32[256,3072]{0,1:T(8,128)} %fusion, s32[]{:T(128)S(6)} %select_n.135, f32[96,128]{1,0:T(8,128)S(1)} %get-tuple-element.28, f32[96,128]{1,0:T(8,128)S(1)} %get-tuple-element.27, f32[256]{0:T(256)S(1)} %copy-done.12, f32[256]{0:T(256)S(1)} %maximum_multiply_fusion.1, ...), kind=kLoop, calls=%fused_computation.76 | loop fusion | flops 221088 | bytes 249604 | tf_op jit(solution)/shard_map/input_gradient/reduce_sum | solution.py:182
  108.9 0.6 broadcast_in_dim.37
  109.5 10.3 %all-to-all-start.3 = ((f32[16,8,128]{2,1,0:T(8,128)}), f32[16,8,128]{2,1,0:T(8,128)S(1)}, u32[]{:S(2)}, u32[]{:S(2)}) async-start(f32[16,8,128]{2,1,0:T(8,128)} %broadcast_in_dim.37), calls=%async_computation.3 | async-start | bytes 131072 | tf_op jit(solution)/shard_map/gain_gradients/all_to_all | solution.py:195
  119.8 0.7 fusion.11
  120.5 5.1 %all-to-all-done.3 = f32[16,8,128]{2,1,0:T(8,128)S(1)} async-done(((f32[16,8,128]{2,1,0:T(8,128)}), f32[16,8,128]{2,1,0:T(8,128)S(1)}, u32[]{:S(2)}, u32[]{:S(2)}) %all-to-all-start.3) | async-done | bytes 65568 | tf_op jit(solution)/shard_map/gain_gradients/all_to_all | solution.py:195
  125.7 0.5 slice_bitcast_fusion
  126.2 0.5 fusion.83
  (99 shorter events, 0.9 us)
Async XLA Ops:
  0.6 33.8 %copy-start = (bf16[256,128]{1,0:T(8,128)(2,1)S(1)}, bf16[256,128]{1,0:T(8,128)(2,1)}, u32[]{:S(2)}) copy-start(bf16[256,128]{1,0:T(8,128)(2,1)} %param.11) | copy-start | bytes 196612
  0.6 7.9 %copy-start.10 = (f32[3072]{0:T(1024)S(1)}, f32[3072]{0:T(1024)}, u32[]{:S(2)}) copy-start(f32[3072]{0:T(1024)} %param.7) | copy-start | bytes 36868
  2.7 19.2 %all-to-all-start = ((bf16[8,192,384]{2,1,0:T(8,128)(2,1)}), bf16[8,192,384]{2,1,0:T(8,128)(2,1)S(1)}, u32[]{:S(2)}, u32[]{:S(2)}) async-start(bf16[8,192,384]{2,1,0:T(8,128)(2,1)} %broadcast_in_dim.24), calls=%async_computation | async-start | bytes 2359296 | tf_op jit(solution)/shard_map/gather_w/all_to_all | solution.py:101
  21.9 9.1 %collective-permute-start = (bf16[8,192,384]{2,1,0:T(8,128)(2,1)S(1)}, bf16[8,192,384]{2,1,0:T(8,128)(2,1)S(1)}, u32[]{:S(2)}, u32[]{:S(2)}) collective-permute-start(bf16[8,192,384]{2,1,0:T(8,128)(2,1)S(1)} %all-to-all-done), channel_id=1, source_target_pairs={{0,32},{32,0},{64,96},{96,64},{128,160},{160,128},{192,224},{224,1... | collective-permute-start | bytes 3538952 | tf_op jit(solution)/shard_map/gather_w/ppermute | solution.py:102
  29.1 14.4 %copy-start.18 = (pred[8]{0:T(512)(128)(4,1)}, pred[8]{0:T(512)(128)(4,1)S(1)}, u32[]{:S(2)}) copy-start(pred[8]{0:T(512)(128)(4,1)S(1)} %compare_and_fusion.1) | copy-start | bytes 28
  29.1 14.4 %copy-start.20 = (s32[8]{0:T(128)}, s32[8]{0:T(128)S(1)}, u32[]{:S(2)}) copy-start(s32[8]{0:T(128)S(1)} %get-tuple-element.54) | copy-start | bytes 100
  29.1 14.4 %copy-start.22 = (s32[8]{0:T(128)}, s32[8]{0:T(128)S(1)}, u32[]{:S(2)}) copy-start(s32[8]{0:T(128)S(1)} %get-tuple-element.55) | copy-start | bytes 100
  29.6 2.0 %copy-start.13 = (f32[256]{0:T(256)}, f32[256]{0:T(256)S(1)}, u32[]{:S(2)}) copy-start(f32[256]{0:T(256)S(1)} %broadcast_multiply_fusion.6) | copy-start | bytes 3076
  30.1 1.5 %copy-start.11 = (f32[256]{0:T(256)}, f32[256]{0:T(256)S(1)}, u32[]{:S(2)}) copy-start(f32[256]{0:T(256)S(1)} %add_rsqrt_fusion.2) | copy-start | bytes 3076
  31.6 2.5 %copy-start.15 = (f32[1,128]{1,0:T(1,128)S(1)}, f32[1,128]{1,0:T(1,128)}, u32[]{:S(2)}) copy-start(f32[1,128]{1,0:T(1,128)} %param.9) | copy-start | bytes 1540
  31.6 2.5 %copy-start.24 = (f32[1,128]{1,0:T(1,128)S(1)}, f32[1,128]{1,0:T(1,128)}, u32[]{:S(2)}) copy-start(f32[1,128]{1,0:T(1,128)} %param.10) | copy-start | bytes 1540
  33.6 3.4 %copy-start.4 = (f32[256,384]{1,0:T(8,128)}, f32[256,384]{1,0:T(8,128)S(1)}, u32[]{:S(2)}) copy-start(f32[256,384]{1,0:T(8,128)S(1)} %fusion.15) | copy-start | bytes 1179652
  34.4 1.1 copy-start.16
  34.6 2.7 %copy-start.8 = (bf16[256,128]{1,0:T(8,128)(2,1)}, bf16[256,128]{1,0:T(8,128)(2,1)S(1)}, u32[]{:S(2)}) copy-start(bf16[256,128]{1,0:T(8,128)(2,1)S(1)} %convolution_convert_fusion.1) | copy-start | bytes 196612
  37.3 0.6 copy-start.6
  40.8 1.9 %copy-start.5 = (f32[256,384]{1,0:T(8,128)S(1)}, f32[256,384]{1,0:T(8,128)}, u32[]{:S(2)}) copy-start(f32[256,384]{1,0:T(8,128)} %copy-done.4) | copy-start | bytes 1179652
  40.8 1.9 %copy-start.7 = (bf16[256,128]{1,0:T(8,128)(2,1)S(1)}, bf16[256,128]{1,0:T(8,128)(2,1)}, u32[]{:S(2)}) copy-start(bf16[256,128]{1,0:T(8,128)(2,1)} %copy-done.6) | copy-start | bytes 196612
  40.8 1.9 %copy-start.9 = (bf16[256,128]{1,0:T(8,128)(2,1)S(1)}, bf16[256,128]{1,0:T(8,128)(2,1)}, u32[]{:S(2)}) copy-start(bf16[256,128]{1,0:T(8,128)(2,1)} %copy-done.8) | copy-start | bytes 196612
  40.8 1.9 %copy-start.27 = (s32[8]{0:T(128)S(1)}, s32[8]{0:T(128)}, u32[]{:S(2)}) copy-start(s32[8]{0:T(128)} %broadcast_add_fusion) | copy-start | bytes 100
  40.8 1.9 %copy-start.28 = (s32[8]{0:T(128)S(1)}, s32[8]{0:T(128)}, u32[]{:S(2)}) copy-start(s32[8]{0:T(128)} %iota_and_fusion) | copy-start | bytes 100
  40.8 1.9 %copy-start.29 = (pred[8]{0:T(512)(128)(4,1)S(1)}, pred[8]{0:T(512)(128)(4,1)}, u32[]{:S(2)}) copy-start(pred[8]{0:T(512)(128)(4,1)} %compare_and_fusion) | copy-start | bytes 28
  44.9 26.4 %all-to-all-start.1 = ((bf16[4,1552,128]{2,1,0:T(8,128)(2,1)}), bf16[4,1552,128]{2,1,0:T(8,128)(2,1)S(1)}, u32[]{:S(2)}, u32[]{:S(2)}) async-start(bf16[4,1552,128]{2,1,0:T(8,128)(2,1)} %pad_maximum_fusion.1), calls=%async_computation.1 | async-start | bytes 3178496 | tf_op jit(solution)/shard_map/input_gradient_partial/all_to_all | solution.py:136
  54.1 1.4 %copy-start.1 = (bf16[3072,384]{1,0:T(8,128)(2,1)}, bf16[3072,384]{1,0:T(8,128)(2,1)S(1)}, u32[]{:S(2)}) copy-start(bf16[3072,384]{1,0:T(8,128)(2,1)S(1)} %add_convert_fusion) | copy-start | bytes 7077892
  56.7 5.4 %collective-permute-start.1 = (bf16[8,192,384]{2,1,0:T(8,128)(2,1)}, bf16[8,192,384]{2,1,0:T(8,128)(2,1)}, u32[]{:S(2)}, u32[]{:S(2)}) collective-permute-start(bf16[8,192,384]{2,1,0:T(8,128)(2,1)} %fusion.4), channel_id=1, source_target_pairs={{0,32},{32,0},{64,96},{96,64},{128,160},{160,128},{192,224},{224,1... | collective-permute-start | bytes 3538952 | tf_op jit(solution)/shard_map/w_grad/ppermute | solution.py:143
  60.2 11.1 %copy-start.19 = (pred[8]{0:T(512)(128)(4,1)S(1)}, pred[8]{0:T(512)(128)(4,1)}, u32[]{:S(2)}) copy-start(pred[8]{0:T(512)(128)(4,1)} %copy-done.18) | copy-start | bytes 28
  60.2 11.1 %copy-start.21 = (s32[8]{0:T(128)S(1)}, s32[8]{0:T(128)}, u32[]{:S(2)}) copy-start(s32[8]{0:T(128)} %copy-done.20) | copy-start | bytes 100
  60.2 11.1 %copy-start.23 = (s32[8]{0:T(128)S(1)}, s32[8]{0:T(128)}, u32[]{:S(2)}) copy-start(s32[8]{0:T(128)} %copy-done.22) | copy-start | bytes 100
  64.5 1.0 copy-start.2
  71.4 15.0 %copy-start.12 = (f32[256]{0:T(256)S(1)}, f32[256]{0:T(256)}, u32[]{:S(2)}) copy-start(f32[256]{0:T(256)} %copy-done.11) | copy-start | bytes 3076
  71.4 15.0 %copy-start.14 = (f32[256]{0:T(256)S(1)}, f32[256]{0:T(256)}, u32[]{:S(2)}) copy-start(f32[256]{0:T(256)} %copy-done.13) | copy-start | bytes 3076
  72.6 34.3 %all-to-all-start.2 = ((bf16[8,208,128]{2,1,0:T(8,128)(2,1)}), bf16[8,208,128]{2,1,0:T(8,128)(2,1)S(1)}, u32[]{:S(2)}, u32[]{:S(2)}) async-start(bf16[8,208,128]{2,1,0:T(8,128)(2,1)} %pad_maximum_fusion.2), calls=%async_computation.2 | async-start | bytes 851968 | tf_op jit(solution)/shard_map/sum_over_near/all_to_all | solution.py:159
  86.5 2.0 %copy-start.3 = (bf16[8,192,384]{2,1,0:T(8,128)(2,1)S(1)}, bf16[8,192,384]{2,1,0:T(8,128)(2,1)}, u32[]{:S(2)}) copy-start(bf16[8,192,384]{2,1,0:T(8,128)(2,1)} %copy-done.2) | copy-start | bytes 3538948
  86.5 10.5 %copy-start.17 = (f32[256]{0:T(256)S(1)}, f32[256]{0:T(256)}, u32[]{:S(2)}) copy-start(f32[256]{0:T(256)} %copy-done.16) | copy-start | bytes 3076
  88.6 20.2 %copy-start.25 = (f32[128]{0:T(128)S(1)}, f32[128]{0:T(128)}, u32[]{:S(2)}) copy-start(f32[128]{0:T(128)} %get-tuple-element.6) | copy-start | bytes 1540
  88.6 20.2 %copy-start.26 = (f32[128]{0:T(128)S(1)}, f32[128]{0:T(128)}, u32[]{:S(2)}) copy-start(f32[128]{0:T(128)} %get-tuple-element.11) | copy-start | bytes 1540
  88.6 10.9 %collective-permute-start.2 = (bf16[2,192,384]{2,1,0:T(8,128)(2,1)S(1)}, bf16[2,192,384]{2,1,0:T(8,128)(2,1)S(1)}, u32[]{:S(2)}, u32[]{:S(2)}) collective-permute-start(bf16[2,192,384]{2,1,0:T(8,128)(2,1)S(1)} %get-tuple-element.22), channel_id=1, source_target_pairs={{0,128},{32,160},{64,192},{96,224},{128,256},{160,288},{192,320},{... | collective-permute-start | bytes 884744 | tf_op jit(solution)/shard_map/w_grad/ppermute | solution.py:149
  90.5 9.8 %collective-permute-start.4 = (bf16[2,192,384]{2,1,0:T(8,128)(2,1)S(1)}, bf16[2,192,384]{2,1,0:T(8,128)(2,1)S(1)}, u32[]{:S(2)}, u32[]{:S(2)}) collective-permute-start(bf16[2,192,384]{2,1,0:T(8,128)(2,1)S(1)} %get-tuple-element.23), channel_id=1, source_target_pairs={{0,384},{32,416},{64,448},{96,480},{128,0},{160,32},{192,64},{224,... | collective-permute-start | bytes 884744 | tf_op jit(solution)/shard_map/w_grad/ppermute | solution.py:149
  95.1 9.7 %collective-permute-start.3 = (bf16[2,192,384]{2,1,0:T(8,128)(2,1)S(1)}, bf16[2,192,384]{2,1,0:T(8,128)(2,1)S(1)}, u32[]{:S(2)}, u32[]{:S(2)}) collective-permute-start(bf16[2,192,384]{2,1,0:T(8,128)(2,1)S(1)} %get-tuple-element.24), channel_id=1, source_target_pairs={{0,256},{32,288},{64,320},{96,352},{128,384},{160,416},{192,448},{... | collective-permute-start | bytes 884744 | tf_op jit(solution)/shard_map/w_grad/ppermute | solution.py:149
  105.0 14.8 %collective-permute-start.5 = (bf16[192,384]{1,0:T(8,128)(2,1)S(1)}, bf16[192,384]{1,0:T(8,128)(2,1)S(1)}, u32[]{:S(2)}, u32[]{:S(2)}) collective-permute-start(bf16[192,384]{1,0:T(8,128)(2,1)S(1)} %fusion.16), channel_id=1, source_target_pairs={{0,64},{32,96},{64,0},{96,32},{128,192},{160,224},{192,128},{224,1... | collective-permute-start | bytes 442376 | tf_op jit(solution)/shard_map/w_grad_y/ppermute | solution.py:165
  109.5 16.2 %all-to-all-start.3 = ((f32[16,8,128]{2,1,0:T(8,128)}), f32[16,8,128]{2,1,0:T(8,128)S(1)}, u32[]{:S(2)}, u32[]{:S(2)}) async-start(f32[16,8,128]{2,1,0:T(8,128)} %broadcast_in_dim.37), calls=%async_computation.3 | async-start | bytes 131072 | tf_op jit(solution)/shard_map/gain_gradients/all_to_all | solution.py:195

commit v5 on v4

v5 whole, which is shorter than its diff:
```python
import jax
import jax.numpy as jnp
from jax import lax
from jax.experimental import pallas as pl
from jax.experimental.pallas import tpu as pltpu
from jax.sharding import PartitionSpec as P

BF = jnp.bfloat16
F32 = jnp.float32
PATCHES = 256
DP, MP = "dp", "mp"
NX, NYL, NC = 4, 2, 2
NZ, NYH = 16, 2

CORE_SWAP = [(i, i ^ 1) for i in range(NX * NYL * NC)]
SAME_CORE = [[2 * i + c for i in range(NX * NYL)] for c in range(NC)]
YLO_SWAP = [(i, i ^ 2) for i in range(NX * NYL * NC)]
X_STEPS = [
    [(i, (i + step * NYL * NC) % (NX * NYL * NC)) for i in range(NX * NYL * NC)]
    for step in range(1, NX)
]
NEAR = [[2 * z + j for j in range(2 * NYH)] for z in range(0, NZ, 2)]
FAR = [[2 * NYH * k + j for k in range(NZ // 2)] for j in range(2 * NYH)]


def head_norm(raw):
    centered = raw - jnp.mean(raw, axis=-1, keepdims=True)
    inverse = lax.rsqrt(jnp.mean(centered * centered, axis=-1, keepdims=True) + 1e-06)
    return centered * inverse, inverse


def norm_backward_pass(grad_hat, normal, inverse):
    first = jnp.mean(grad_hat, axis=-1, keepdims=True)
    second = jnp.mean(grad_hat * normal, axis=-1, keepdims=True)
    return (grad_hat - first - normal * second) * inverse


def dot(a, b, ca, cb):
    return lax.dot_general(a, b, (((ca,), (cb,)), ((), ())), preferred_element_type=F32)


def hi_lo(value):
    hi = value.astype(BF)
    lo = (value - hi.astype(F32)).astype(BF)
    return hi, lo


def pack(sums):
    hi = sums.astype(BF).astype(F32)
    row = lax.broadcasted_iota(jnp.int32, sums.shape, 0)
    return jnp.where(row % 4 < 2, hi, sums - hi).astype(BF)


def unpack(got):
    first, second = got[0:2] + got[2:4], got[8:10] + got[10:12]
    return jnp.concatenate([first] * 4 + [second] * 4, axis=0)


def after(value, other):
    first = other.reshape(-1, other.shape[-1])[:1, :128].astype(F32)
    zero = jnp.minimum(jnp.abs(first), 0.0)
    return value + jnp.concatenate([zero] * (value.shape[-1] // 128), axis=1)


def head_kernel(
    core_ref, x_ref, own_ref, other_ref, grad_ref, q_gain_ref, k_gain_ref,
    context_ref, dqkv_ref, part_ref, gains_ref, full_ref,
):
    rows, hd = grad_ref.shape
    lane = rows // 2
    blocks, w_rows, columns = own_ref.shape
    share = w_rows // 2
    own_first = core_ref[0] == 0
    for at in range(blocks):
        own, other = own_ref[at], other_ref[at]
        full_ref[2 * at] = jnp.where(own_first, own, other)
        full_ref[2 * at + 1] = jnp.where(own_first, other, own)
    full = full_ref[...].reshape(2 * blocks * w_rows, columns)
    product = dot(x_ref[...], full, 1, 0)
    raw = product[:rows]
    weighted = product[rows : rows + 1] + product[rows + 1 : rows + 2]

    q_gain, k_gain, grad = q_gain_ref[...], k_gain_ref[...], grad_ref[...]
    scale = hd ** (-0.5)
    qhat, q_inv = head_norm(raw[:, :hd])
    khat, k_inv = head_norm(raw[:, hd : 2 * hd])
    value = raw[:, 2 * hd :].astype(BF)
    q_norm = (qhat * q_gain).astype(BF)
    k_norm = (khat * k_gain).astype(BF)
    expo = jnp.exp(dot(q_norm, k_norm, 1, 1) * scale)
    probs = expo / jnp.sum(expo, axis=-1, keepdims=True)
    probs_b = probs.astype(BF)
    context_ref[...] = dot(probs_b, value, 1, 0).astype(BF)
    dprob = dot(grad, value, 1, 1)
    dscore = (probs * (dprob - jnp.sum(probs * dprob, axis=-1, keepdims=True)) * scale).astype(BF)
    dqn = dot(dscore, k_norm, 1, 0)
    dkn = dot(dscore, q_norm, 0, 0)
    gains_ref[0:1] = jnp.sum(dqn * qhat, axis=0, keepdims=True)
    gains_ref[1:2] = jnp.sum(dkn * khat, axis=0, keepdims=True)
    gains_ref[2:] = jnp.zeros((gains_ref.shape[0] - 2, hd), F32)
    dqkv = jnp.concatenate(
        [
            norm_backward_pass(dqn * q_gain, qhat, q_inv).astype(BF),
            norm_backward_pass(dkn * k_gain, khat, k_inv).astype(BF),
            dot(probs_b, grad, 0, 0).astype(BF),
        ],
        axis=1,
    )
    dqkv_ref[...] = dqkv

    for k in range(blocks):
        pair = full_ref[2 * k : 2 * k + 2].reshape(2 * w_rows, columns)
        part = dot(pair, dqkv, 1, 1).astype(BF)
        for group in range(4):
            for half in range(2):
                at = (2 * k + half) * share
                part_ref[group, at : at + share] = part[
                    group * share : (group + 1) * share, half * lane : (half + 1) * lane
                ]

    row = lax.broadcasted_iota(jnp.int32, (8, columns), 0)
    w_hi, w_lo = hi_lo(jnp.where(row % 2 == 0, weighted, 0.0))
    ones = jnp.where(row % 2 == 1, 1.0, 0.0).astype(BF)
    p_hi, p_lo = hi_lo(dqkv.astype(F32) * raw)
    sums = (dot(w_hi, dqkv, 1, 1) + dot(w_lo, dqkv, 1, 1)) + (
        dot(ones, p_hi, 1, 1) + dot(ones, p_lo, 1, 1)
    )
    packed = pack(jnp.concatenate([sums[:, :lane], sums[:, lane:]], axis=0))
    for group in range(4):
        part_ref[group, 2 * blocks * share :] = packed


def run_head(core, x, own, other, grad, q_gain, k_gain):
    rows, hd = grad.shape
    blocks, w_rows, columns = own.shape
    vmem = pl.BlockSpec(memory_space=pltpu.VMEM)
    return pl.pallas_call(
        head_kernel,
        in_specs=[pl.BlockSpec(memory_space=pltpu.SMEM)] + [vmem] * 6,
        out_specs=[vmem] * 4,
        out_shape=[
            jax.ShapeDtypeStruct((rows, hd), BF),
            jax.ShapeDtypeStruct((rows, columns), BF),
            jax.ShapeDtypeStruct((4, blocks * w_rows + 16, rows // 2), BF),
            jax.ShapeDtypeStruct((8, hd), F32),
        ],
        scratch_shapes=[pltpu.VMEM((2 * blocks, w_rows, columns), BF)],
        compiler_params=pltpu.CompilerParams(vmem_limit_bytes=48 * 2**20),
        cost_estimate=pl.CostEstimate(
            flops=1_400_000_000, bytes_accessed=9_000_000, transcendentals=65536
        ),
    )(core.reshape(1), x, own, other, grad, q_gain, k_gain)


def per_device(tokens, layer_norm_gain, w_qkv, q_gain, k_gain, ctx_grad):
    rows, width = tokens.shape
    w_rows, columns = w_qkv.shape
    share = width // (NZ * NYH)
    core = lax.axis_index(DP) % 2
    y_lo = (lax.axis_index(DP) // NC) % NYL
    x_at = lax.axis_index(DP) // (NYL * NC)
    mp = lax.axis_index(MP)
    lane = rows // 2

    with jax.named_scope("gather_w"):
        copies = jnp.broadcast_to(w_qkv[None], (NX * NYL, w_rows, columns))
        own = lax.all_to_all(copies, DP, 0, 0, axis_index_groups=SAME_CORE, tiled=True)
        other = lax.ppermute(own, DP, CORE_SWAP)

    with jax.named_scope("input_norm"):
        x_float = tokens.astype(F32)
        centered = x_float - jnp.mean(x_float, axis=-1, keepdims=True)
        inverse = lax.rsqrt(jnp.mean(centered * centered, axis=-1, keepdims=True) + 1e-06)
        xhat = centered * inverse
        normed = (xhat * layer_norm_gain).astype(BF)

        extra = jnp.concatenate(
            [jnp.stack(hi_lo(layer_norm_gain)), jnp.zeros((14, width), BF)], axis=0
        )
        lhs = jnp.concatenate([normed, extra], axis=0)

    with jax.named_scope("head"):
        context, dqkv, part, head_gains = run_head(
            core, lhs, own, other, ctx_grad, q_gain, k_gain
        )

    with jax.named_scope("input_gradient_near"):
        chunk = 2 * share
        near = lax.all_to_all(part, MP, 0, 0, axis_index_groups=NEAR, tiled=True)

    with jax.named_scope("w_grad"):
        term = dot(normed, dqkv, 0, 0).astype(BF).reshape(NX * NYL, NC, w_rows, columns)
        term_keep = jnp.where(core == 0, term[:, 0], term[:, 1])
        term_send = jnp.where(core == 0, term[:, 1], term[:, 0])
        term_got = lax.ppermute(term_send, DP, CORE_SWAP)
        chip = (term_keep.astype(F32) + term_got.astype(F32)).astype(BF)
        chip = chip.reshape(NX, NYL, w_rows, columns)
        x_term = lax.dynamic_index_in_dim(chip, x_at, 0, False).astype(F32)
        for step, pairs in enumerate(X_STEPS, 1):
            leaves = lax.dynamic_index_in_dim(chip, (x_at + step) % NX, 0, False)
            x_term = x_term + lax.ppermute(leaves, DP, pairs).astype(F32)

    with jax.named_scope("sum_over_near"):
        many = NZ // 2 * chunk
        pair = jnp.sum(near[:, :many].astype(F32), axis=0)
        pair = after(pair, x_term).astype(BF).reshape(NZ // 2, chunk, lane)
        sums = unpack(jnp.sum(near[:, many:].astype(F32), axis=0))
        riding = jnp.broadcast_to(pack(sums)[None], (NZ // 2, 16, lane))
        pair = jnp.concatenate([pair, riding], axis=1)
        far = lax.all_to_all(pair, MP, 0, 0, axis_index_groups=FAR, tiled=True)

    with jax.named_scope("w_grad_y"):
        x_term = after(x_term, pair)
        leaves = jnp.where(y_lo == 0, x_term[1], x_term[0]).astype(BF)
        stays = jnp.where(y_lo == 0, x_term[0], x_term[1])
        w_grad = (stays + lax.ppermute(leaves, DP, YLO_SWAP).astype(F32)).astype(BF)

    with jax.named_scope("sum_over_far"):
        total = jnp.sum(far.astype(F32), axis=0)
        dnormed = jnp.concatenate([total[:share], total[share:chunk]], axis=1)
        sums = unpack(total[chunk:])
        plain = jnp.concatenate([sums[0:1], sums[8:9]], axis=1)
        cross = jnp.concatenate([sums[1:2], sums[9:10]], axis=1)

    with jax.named_scope("input_gradient"):
        start = mp * share
        xhat_share = lax.dynamic_slice_in_dim(xhat, start, share, 1).T
        gain_share = lax.dynamic_slice_in_dim(layer_norm_gain, start, share, 0)
        input_gradient_rows = (
            (dnormed * gain_share[:, None] - plain / width - xhat_share * (cross / width))
            * inverse.T
        ).T.astype(BF)
        gain_portion = jnp.sum(dnormed * xhat_share, axis=1)

    with jax.named_scope("gain_gradients"):
        portion = jnp.pad(gain_portion, (0, 128 - share))[None]
        small = jnp.concatenate([head_gains[:7], portion], axis=0)
        copies = jnp.broadcast_to(small[None], (NX * NYL * NC, 8, 128))
        summed = jnp.sum(lax.all_to_all(copies, DP, 0, 0, tiled=True), axis=0)
    return (
        context,
        input_gradient_rows,
        summed[7, :share],
        w_grad,
        summed[0:1],
        summed[1:2],
    )


def solution(mesh):
    placed = (P("dp", None), P(), P("dp", "mp"), P("mp", None), P("mp", None), P("dp", "mp"))
    return jax.shard_map(
        per_device,
        mesh=mesh,
        in_specs=placed,
        out_specs=(
            P("dp", "mp"),
            P("dp", "mp"),
            P("mp"),
            P("dp", "mp"),
            P("mp", None),
            P("mp", None),
        ),
        check_vma=False,
    )
```

time: 128 us -> 132 us (1.031)
  the two profiles are of different devices: /device:TPU:1 before, /device:TPU:33 now
where the time goes in v5:
time: 132 us; the launch traced here: 131 us
  waiting for transfers between devices  55.2 us (42%)
  starting transfers between devices  49 us (37%)
  other arithmetic  13.8 us (10%)
  local copies, waits for them, and re-layouts  6.73 us (5%)
  Pallas kernels  4.28 us (3%)
    all_to_all x1, waiting for transfers between devices, per_device(): far = lax.all_to_all(pair, MP, 0, 0, axis_index_groups=FAR, tiled=True)  20.8 us
    all_to_all x1, waiting for transfers between devices, per_device(): lax.all_to_all(copies, DP, 0, 0, axis_index_groups=SAME_CORE, tiled=True)  16.2 us
    all_to_all x1, starting transfers between devices, per_device(): far = lax.all_to_all(pair, MP, 0, 0, axis_index_groups=FAR, tiled=True)  13.9 us
    ppermute x3, waiting for transfers between devices, per_device(): x_term = x_term + lax.ppermute(leaves, DP, pairs).astype(F32)  11.4 us
    all_to_all x1, starting transfers between devices, per_device(): summed = jnp.sum(lax.all_to_all(copies, DP, 0, 0, tiled=True), axis=0)  8.64 us
    ppermute x3, starting transfers between devices, per_device(): x_term = x_term + lax.ppermute(leaves, DP, pairs).astype(F32)  8.41 us
    all_to_all x1, starting transfers between devices, per_device(): near = lax.all_to_all(part, MP, 0, 0, axis_index_groups=NEAR, tiled=True)  5.07 us
    all_to_all x1, starting transfers between devices, per_device(): lax.all_to_all(copies, DP, 0, 0, axis_index_groups=SAME_CORE, tiled=True)  5.03 us
  transfers between devices with their start and end apart: 10, of which 6 were waited for; matrix products, arithmetic and copies ran while one was open for 10% of the time, Pallas kernels for 0%

profile of v5, /device:TPU:33, one launch (start us, length us, event | category | flops | bytes accessed | tf_op | source)
XLA Modules:
  0.0 131.1 jit_solution(11559290840659049031)
XLA Ops:
  0.6 0.0 copy-start.5
  0.6 0.0 copy-start.4
  0.7 2.2 %broadcast_in_dim.11 = bf16[8,192,384]{2,1,0:T(8,128)(2,1)} broadcast(bf16[192,384]{1,0:T(8,128)(2,1)} %param.8), dimensions={1,2} | broadcast | bytes 1327104 | tf_op jit(solution)/shard_map/gather_w/broadcast_in_dim | solution.py:166
  2.8 5.0 %all-to-all-start = ((bf16[8,192,384]{2,1,0:T(8,128)(2,1)}), bf16[8,192,384]{2,1,0:T(8,128)(2,1)S(1)}, u32[]{:S(2)}, u32[]{:S(2)}) async-start(bf16[8,192,384]{2,1,0:T(8,128)(2,1)} %broadcast_in_dim.11), calls=%async_computation | async-start | bytes 2359296 | tf_op jit(solution)/shard_map/gather_w/all_to_all | solution.py:167
  7.9 0.0 copy-done.5
  7.9 0.1 pad.21.clone
  8.0 0.0 copy-done.4
  8.0 0.3 convert_reduce_fusion
  8.3 0.6 fusion.2
  8.9 16.2 %all-to-all-done.own_ref = bf16[8,192,384]{2,1,0:T(8,128)(2,1)S(1)} async-done(((bf16[8,192,384]{2,1,0:T(8,128)(2,1)}), bf16[8,192,384]{2,1,0:T(8,128)(2,1)S(1)}, u32[]{:S(2)}, u32[]{:S(2)}) %all-to-all-start) | async-done | bytes 1179680 | tf_op jit(solution)/shard_map/gather_w/all_to_all | solution.py:167
  25.1 3.5 %collective-permute-start = (bf16[8,192,384]{2,1,0:T(8,128)(2,1)S(1)}, bf16[8,192,384]{2,1,0:T(8,128)(2,1)S(1)}, u32[]{:S(2)}, u32[]{:S(2)}) collective-permute-start(bf16[8,192,384]{2,1,0:T(8,128)(2,1)S(1)} %all-to-all-done.own_ref), channel_id=1, source_target_pairs={{0,32},{32,0},{64,96},{96,64},{128,160},{160,128},{192,224},{224,1... | collective-permute-start | bytes 3538952 | tf_op jit(solution)/shard_map/gather_w/ppermute | solution.py:168
  28.6 3.8 %fusion = (f32[256,3072]{1,0:T(8,128)}, bf16[256,3072]{1,0:T(8,128)(2,1)S(1)}) fusion(bf16[256,3072]{1,0:T(8,128)(2,1)} %param.6, f32[256]{0:T(256)S(1)} %add_rsqrt_fusion, f32[256]{0:T(256)S(1)} %broadcast_multiply_fusion, f32[3072]{0:T(1024)S(1)} %copy-done.5), kind=kLoop, calls=%fused_computation.3 | loop fusion | flops 3932160 | bytes 6305792 | tf_op jit(solution)/shard_map/input_norm/mul | solution.py:174
  32.5 0.0 copy-start
  32.5 0.0 copy-start.1
  32.5 0.0 copy-start.2
  32.5 0.5 maximum_maximum_fusion.x_ref
  33.0 0.0 collective-permute-done.other_ref
  33.0 0.3 copy-done
  33.3 0.0 copy-done.1
  33.3 0.0 copy-done.2
  33.3 4.3 %head.1 = (bf16[256,128]{1,0:T(8,128)(2,1)}, bf16[256,384]{1,0:T(8,128)(2,1)S(1)}, bf16[4,1552,128]{2,1,0:T(8,128)(2,1)}, f32[8,128]{1,0:T(8,128)S(1)}) custom-call(s32[1]{0:T(128)} %bitcast.core_ref, bf16[272,3072]{1,0:T(8,128)(2,1)S(1)} %maximum_maximum_fusion.x_ref, bf16[8,192,384]{2,1,0:T(8,128)(2,1)S(1)} %all-to-all-done.own_ref, ...), custom_call_target="tpu_custom_call" | custom-call | flops 1400000000 | bytes 9000000 | tf_op jit(solution)/shard_map/head/pallas_call | solution.py:137
  37.6 5.1 %all-to-all-start.1 = ((bf16[4,1552,128]{2,1,0:T(8,128)(2,1)}), bf16[4,1552,128]{2,1,0:T(8,128)(2,1)}, u32[]{:S(2)}, u32[]{:S(2)}) async-start(bf16[4,1552,128]{2,1,0:T(8,128)(2,1)} %get-tuple-element.11), calls=%async_computation.1 | async-start | bytes 3178496 | tf_op jit(solution)/shard_map/input_gradient_near/all_to_all | solution.py:189
  42.7 1.0 convolution_convert_fusion
  43.7 0.0 copy-start.3
  43.7 0.1 fusion.4
  43.8 1.3 %copy-done.3 = bf16[3072,384]{1,0:T(8,128)(2,1)} copy-done((bf16[3072,384]{1,0:T(8,128)(2,1)}, bf16[3072,384]{1,0:T(8,128)(2,1)S(1)}, u32[]{:S(2)}) %copy-start.3) | copy-done | bytes 2359320
  45.2 2.5 %collective-permute-start.1 = (bf16[8,192,384]{2,1,0:T(8,128)(2,1)S(1)}, bf16[8,192,384]{2,1,0:T(8,128)(2,1)S(1)}, u32[]{:S(2)}, u32[]{:S(2)}) collective-permute-start(bf16[8,192,384]{2,1,0:T(8,128)(2,1)S(1)} %fusion.4), channel_id=1, source_target_pairs={{0,32},{32,0},{64,96},{96,64},{128,160},{160,128},{192,224},{224,1... | collective-permute-start | bytes 3538952 | tf_op jit(solution)/shard_map/w_grad/ppermute | solution.py:195
  47.7 2.4 %collective-permute-done.1 = bf16[8,192,384]{2,1,0:T(8,128)(2,1)S(1)} collective-permute-done((bf16[8,192,384]{2,1,0:T(8,128)(2,1)S(1)}, bf16[8,192,384]{2,1,0:T(8,128)(2,1)S(1)}, u32[]{:S(2)}, u32[]{:S(2)}) %collective-permute-start.1) | collective-permute-done | bytes 1179680 | tf_op jit(solution)/shard_map/w_grad/ppermute | solution.py:195
  50.1 2.2 %fusion.3 = bf16[8,192,384]{2,1,0:T(8,128)(2,1)S(1)} fusion(bf16[8,192,384]{2,1,0:T(8,128)(2,1)S(1)} %collective-permute-done.1, pred[]{:T(512)S(6)} %eq.16, bf16[8,2,192,384]{3,2,1,0:T(8,128)(2,1)} %bitcast.76), kind=kLoop, calls=%fused_computation.9 | loop fusion | flops 2949120 | bytes 4718593 | tf_op jit(solution)/shard_map/w_grad/convert_element_type | solution.py:196
  52.3 0.1 dynamic-slice_bitcast_fusion.2
  52.4 1.9 %collective-permute-start.2 = (bf16[2,192,384]{2,1,0:T(8,128)(2,1)S(1)}, bf16[2,192,384]{2,1,0:T(8,128)(2,1)S(1)}, u32[]{:S(2)}, u32[]{:S(2)}) collective-permute-start(bf16[2,192,384]{2,1,0:T(8,128)(2,1)S(1)} %get-tuple-element.44), channel_id=1, source_target_pairs={{0,128},{32,160},{64,192},{96,224},{128,256},{160,288},{192,320},{... | collective-permute-start | bytes 884744 | tf_op jit(solution)/shard_map/w_grad/ppermute | solution.py:201
  54.3 2.7 %collective-permute-start.3 = (bf16[2,192,384]{2,1,0:T(8,128)(2,1)S(1)}, bf16[2,192,384]{2,1,0:T(8,128)(2,1)S(1)}, u32[]{:S(2)}, u32[]{:S(2)}) collective-permute-start(bf16[2,192,384]{2,1,0:T(8,128)(2,1)S(1)} %get-tuple-element.46), channel_id=1, source_target_pairs={{0,256},{32,288},{64,320},{96,352},{128,384},{160,416},{192,448},{... | collective-permute-start | bytes 884744 | tf_op jit(solution)/shard_map/w_grad/ppermute | solution.py:201
  57.0 3.8 %collective-permute-start.4 = (bf16[2,192,384]{2,1,0:T(8,128)(2,1)S(1)}, bf16[2,192,384]{2,1,0:T(8,128)(2,1)S(1)}, u32[]{:S(2)}, u32[]{:S(2)}) collective-permute-start(bf16[2,192,384]{2,1,0:T(8,128)(2,1)S(1)} %get-tuple-element.45), channel_id=1, source_target_pairs={{0,384},{32,416},{64,448},{96,480},{128,0},{160,32},{192,64},{224,... | collective-permute-start | bytes 884744 | tf_op jit(solution)/shard_map/w_grad/ppermute | solution.py:201
  60.9 9.2 %collective-permute-done.2 = bf16[2,192,384]{2,1,0:T(8,128)(2,1)S(1)} collective-permute-done((bf16[2,192,384]{2,1,0:T(8,128)(2,1)S(1)}, bf16[2,192,384]{2,1,0:T(8,128)(2,1)S(1)}, u32[]{:S(2)}, u32[]{:S(2)}) %collective-permute-start.2) | collective-permute-done | bytes 294944 | tf_op jit(solution)/shard_map/w_grad/ppermute | solution.py:201
  70.1 0.0 collective-permute-done.3
  70.1 2.2 %collective-permute-done.4 = bf16[2,192,384]{2,1,0:T(8,128)(2,1)S(1)} collective-permute-done((bf16[2,192,384]{2,1,0:T(8,128)(2,1)S(1)}, bf16[2,192,384]{2,1,0:T(8,128)(2,1)S(1)}, u32[]{:S(2)}, u32[]{:S(2)}) %collective-permute-start.4) | collective-permute-done | bytes 294944 | tf_op jit(solution)/shard_map/w_grad/ppermute | solution.py:201
  72.3 0.1 fusion.7
  72.4 0.0 all-to-all-done.1
  72.4 0.7 convert_reduce_fusion.3
  73.2 1.7 %convert_reduce_fusion.1 = f32[1536,128]{1,0:T(8,128)S(1)} fusion(bf16[4,1552,128]{2,1,0:T(8,128)(2,1)} %all-to-all-done.1), kind=kLoop, calls=%fused_computation.6 | loop fusion | flops 1376256 | bytes 2359296 | tf_op jit(solution)/shard_map/sum_over_near/reduce_sum | solution.py:205
  74.9 0.1 add_convert_fusion
  75.0 0.1 fusion.15
  75.1 0.8 pad_maximum_fusion
  75.9 13.9 %all-to-all-start.2 = ((bf16[8,208,128]{2,1,0:T(8,128)(2,1)}), bf16[8,208,128]{2,1,0:T(8,128)(2,1)S(1)}, u32[]{:S(2)}, u32[]{:S(2)}) async-start(bf16[8,208,128]{2,1,0:T(8,128)(2,1)} %pad_maximum_fusion), calls=%async_computation.2 | async-start | bytes 851968 | tf_op jit(solution)/shard_map/sum_over_near/all_to_all | solution.py:210
  89.8 0.1 dynamic_slice.23
  89.9 0.6 fusion.17
  90.6 1.9 %collective-permute-start.5 = (bf16[192,384]{1,0:T(8,128)(2,1)S(1)}, bf16[192,384]{1,0:T(8,128)(2,1)S(1)}, u32[]{:S(2)}, u32[]{:S(2)}) collective-permute-start(bf16[192,384]{1,0:T(8,128)(2,1)S(1)} %fusion.9), channel_id=1, source_target_pairs={{0,64},{32,96},{64,0},{96,32},{128,192},{160,224},{192,128},{224,1... | collective-permute-start | bytes 442376 | tf_op jit(solution)/shard_map/w_grad_y/ppermute | solution.py:216
  92.6 20.8 %all-to-all-done.2 = bf16[8,208,128]{2,1,0:T(8,128)(2,1)S(1)} async-done(((bf16[8,208,128]{2,1,0:T(8,128)(2,1)}), bf16[8,208,128]{2,1,0:T(8,128)(2,1)S(1)}, u32[]{:S(2)}, u32[]{:S(2)}) %all-to-all-start.2) | async-done | bytes 426016 | tf_op jit(solution)/shard_map/sum_over_near/all_to_all | solution.py:210
  113.3 0.1 convert_reduce_fusion.2
  113.4 0.1 copy.37
  113.5 0.1 copy.38
  113.7 1.2 fusion.13
  114.9 0.6 broadcast_in_dim.14
  115.5 8.6 %all-to-all-start.3 = ((f32[16,8,128]{2,1,0:T(8,128)}), f32[16,8,128]{2,1,0:T(8,128)S(1)}, u32[]{:S(2)}, u32[]{:S(2)}) async-start(f32[16,8,128]{2,1,0:T(8,128)} %broadcast_in_dim.14), calls=%async_computation.3 | async-start | bytes 131072 | tf_op jit(solution)/shard_map/gain_gradients/all_to_all | solution.py:239
  124.1 0.0 collective-permute-done.5
  124.1 0.7 fusion.8
  124.8 0.7 copy.35
  125.6 4.4 %all-to-all-done.3 = f32[16,8,128]{2,1,0:T(8,128)S(1)} async-done(((f32[16,8,128]{2,1,0:T(8,128)}), f32[16,8,128]{2,1,0:T(8,128)S(1)}, u32[]{:S(2)}, u32[]{:S(2)}) %all-to-all-start.3) | async-done | bytes 65568 | tf_op jit(solution)/shard_map/gain_gradients/all_to_all | solution.py:239
  130.0 0.5 fusion.21
  130.5 0.5 slice_bitcast_fusion
  (24 shorter events, 0.3 us)
Async XLA Ops:
  0.6 7.2 %copy-start.5 = (f32[3072]{0:T(1024)S(1)}, f32[3072]{0:T(1024)}, u32[]{:S(2)}) copy-start(f32[3072]{0:T(1024)} %param.7) | copy-start | bytes 36868
  0.6 7.4 %copy-start.4 = (bf16[256,3072]{1,0:T(8,128)(2,1)S(1)}, bf16[256,3072]{1,0:T(8,128)(2,1)}, u32[]{:S(2)}) copy-start(bf16[256,3072]{1,0:T(8,128)(2,1)} %param.6) | copy-start | bytes 4718596
  2.8 22.3 %all-to-all-start = ((bf16[8,192,384]{2,1,0:T(8,128)(2,1)}), bf16[8,192,384]{2,1,0:T(8,128)(2,1)S(1)}, u32[]{:S(2)}, u32[]{:S(2)}) async-start(bf16[8,192,384]{2,1,0:T(8,128)(2,1)} %broadcast_in_dim.11), calls=%async_computation | async-start | bytes 2359296 | tf_op jit(solution)/shard_map/gather_w/all_to_all | solution.py:167
  25.1 7.9 %collective-permute-start = (bf16[8,192,384]{2,1,0:T(8,128)(2,1)S(1)}, bf16[8,192,384]{2,1,0:T(8,128)(2,1)S(1)}, u32[]{:S(2)}, u32[]{:S(2)}) collective-permute-start(bf16[8,192,384]{2,1,0:T(8,128)(2,1)S(1)} %all-to-all-done.own_ref), channel_id=1, source_target_pairs={{0,32},{32,0},{64,96},{96,64},{128,160},{160,128},{192,224},{224,1... | collective-permute-start | bytes 3538952 | tf_op jit(solution)/shard_map/gather_w/ppermute | solution.py:168
  32.5 0.8 copy-start
  32.5 0.8 copy-start.1
  32.5 0.8 copy-start.2
  37.6 34.8 %all-to-all-start.1 = ((bf16[4,1552,128]{2,1,0:T(8,128)(2,1)}), bf16[4,1552,128]{2,1,0:T(8,128)(2,1)}, u32[]{:S(2)}, u32[]{:S(2)}) async-start(bf16[4,1552,128]{2,1,0:T(8,128)(2,1)} %get-tuple-element.11), calls=%async_computation.1 | async-start | bytes 3178496 | tf_op jit(solution)/shard_map/input_gradient_near/all_to_all | solution.py:189
  43.7 1.5 %copy-start.3 = (bf16[3072,384]{1,0:T(8,128)(2,1)}, bf16[3072,384]{1,0:T(8,128)(2,1)S(1)}, u32[]{:S(2)}) copy-start(bf16[3072,384]{1,0:T(8,128)(2,1)S(1)} %convolution_convert_fusion) | copy-start | bytes 7077892
  45.2 4.9 %collective-permute-start.1 = (bf16[8,192,384]{2,1,0:T(8,128)(2,1)S(1)}, bf16[8,192,384]{2,1,0:T(8,128)(2,1)S(1)}, u32[]{:S(2)}, u32[]{:S(2)}) collective-permute-start(bf16[8,192,384]{2,1,0:T(8,128)(2,1)S(1)} %fusion.4), channel_id=1, source_target_pairs={{0,32},{32,0},{64,96},{96,64},{128,160},{160,128},{192,224},{224,1... | collective-permute-start | bytes 3538952 | tf_op jit(solution)/shard_map/w_grad/ppermute | solution.py:195
  52.4 17.6 %collective-permute-start.2 = (bf16[2,192,384]{2,1,0:T(8,128)(2,1)S(1)}, bf16[2,192,384]{2,1,0:T(8,128)(2,1)S(1)}, u32[]{:S(2)}, u32[]{:S(2)}) collective-permute-start(bf16[2,192,384]{2,1,0:T(8,128)(2,1)S(1)} %get-tuple-element.44), channel_id=1, source_target_pairs={{0,128},{32,160},{64,192},{96,224},{128,256},{160,288},{192,320},{... | collective-permute-start | bytes 884744 | tf_op jit(solution)/shard_map/w_grad/ppermute | solution.py:201
  54.3 15.7 %collective-permute-start.3 = (bf16[2,192,384]{2,1,0:T(8,128)(2,1)S(1)}, bf16[2,192,384]{2,1,0:T(8,128)(2,1)S(1)}, u32[]{:S(2)}, u32[]{:S(2)}) collective-permute-start(bf16[2,192,384]{2,1,0:T(8,128)(2,1)S(1)} %get-tuple-element.46), channel_id=1, source_target_pairs={{0,256},{32,288},{64,320},{96,352},{128,384},{160,416},{192,448},{... | collective-permute-start | bytes 884744 | tf_op jit(solution)/shard_map/w_grad/ppermute | solution.py:201
  57.0 15.2 %collective-permute-start.4 = (bf16[2,192,384]{2,1,0:T(8,128)(2,1)S(1)}, bf16[2,192,384]{2,1,0:T(8,128)(2,1)S(1)}, u32[]{:S(2)}, u32[]{:S(2)}) collective-permute-start(bf16[2,192,384]{2,1,0:T(8,128)(2,1)S(1)} %get-tuple-element.45), channel_id=1, source_target_pairs={{0,384},{32,416},{64,448},{96,480},{128,0},{160,32},{192,64},{224,... | collective-permute-start | bytes 884744 | tf_op jit(solution)/shard_map/w_grad/ppermute | solution.py:201
  75.9 37.4 %all-to-all-start.2 = ((bf16[8,208,128]{2,1,0:T(8,128)(2,1)}), bf16[8,208,128]{2,1,0:T(8,128)(2,1)S(1)}, u32[]{:S(2)}, u32[]{:S(2)}) async-start(bf16[8,208,128]{2,1,0:T(8,128)(2,1)} %pad_maximum_fusion), calls=%async_computation.2 | async-start | bytes 851968 | tf_op jit(solution)/shard_map/sum_over_near/all_to_all | solution.py:210
  90.6 33.5 %collective-permute-start.5 = (bf16[192,384]{1,0:T(8,128)(2,1)S(1)}, bf16[192,384]{1,0:T(8,128)(2,1)S(1)}, u32[]{:S(2)}, u32[]{:S(2)}) collective-permute-start(bf16[192,384]{1,0:T(8,128)(2,1)S(1)} %fusion.9), channel_id=1, source_target_pairs={{0,64},{32,96},{64,0},{96,32},{128,192},{160,224},{192,128},{224,1... | collective-permute-start | bytes 442376 | tf_op jit(solution)/shard_map/w_grad_y/ppermute | solution.py:216
  115.5 14.5 %all-to-all-start.3 = ((f32[16,8,128]{2,1,0:T(8,128)}), f32[16,8,128]{2,1,0:T(8,128)S(1)}, u32[]{:S(2)}, u32[]{:S(2)}) async-start(f32[16,8,128]{2,1,0:T(8,128)} %broadcast_in_dim.14), calls=%async_computation.3 | async-start | bytes 131072 | tf_op jit(solution)/shard_map/gain_gradients/all_to_all | solution.py:239

commit v6 on v5

--- a/solution.py
+++ b/solution.py
@@ -169,10 +169,10 @@
 
     with jax.named_scope("input_norm"):
         x_float = tokens.astype(F32)
-        centered = x_float - jnp.mean(x_float, axis=-1, keepdims=True)
+        mean = jnp.mean(x_float, axis=-1, keepdims=True)
+        centered = x_float - mean
         inverse = lax.rsqrt(jnp.mean(centered * centered, axis=-1, keepdims=True) + 1e-06)
-        xhat = centered * inverse
-        normed = (xhat * layer_norm_gain).astype(BF)
+        normed = (centered * inverse * layer_norm_gain).astype(BF)
 
         extra = jnp.concatenate(
             [jnp.stack(hi_lo(layer_norm_gain)), jnp.zeros((14, width), BF)], axis=0
@@ -203,7 +203,7 @@
     with jax.named_scope("sum_over_near"):
         many = NZ // 2 * chunk
         pair = jnp.sum(near[:, :many].astype(F32), axis=0)
-        pair = after(pair, x_term).astype(BF).reshape(NZ // 2, chunk, lane)
+        pair = after(pair, chip).astype(BF).reshape(NZ // 2, chunk, lane)
         sums = unpack(jnp.sum(near[:, many:].astype(F32), axis=0))
         riding = jnp.broadcast_to(pack(sums)[None], (NZ // 2, 16, lane))
         pair = jnp.concatenate([pair, riding], axis=1)
@@ -224,7 +224,8 @@
 
     with jax.named_scope("input_gradient"):
         start = mp * share
-        xhat_share = lax.dynamic_slice_in_dim(xhat, start, share, 1).T
+        tokens_share = lax.dynamic_slice_in_dim(tokens, start, share, 1).astype(F32)
+        xhat_share = ((tokens_share - mean) * inverse).T
         gain_share = lax.dynamic_slice_in_dim(layer_norm_gain, start, share, 0)
         input_gradient_rows = (
             (dnormed * gain_share[:, None] - plain / width - xhat_share * (cross / width))

time: 132 us -> 120 us (0.909)
  waiting for transfers between devices: 55.2 us -> 50.2 us
  other arithmetic: 13.8 us -> 10.1 us
  starting transfers between devices: 49 us -> 46.9 us
    all_to_all x1, waiting for transfers between devices: 20.8 us -> 2.24 us  [per_device(): far = lax.all_to_all(pair, MP, 0, 0, axis_index_groups=FAR, tiled=True)]
    all_to_all x1, waiting for transfers between devices: 0.01 us -> 14.6 us  [per_device(): near = lax.all_to_all(part, MP, 0, 0, axis_index_groups=NEAR, tiled=True)]
    mul x1 -> x0, other arithmetic: 3.85 us -> none  [per_device(): xhat = centered * inverse]
    unnamed x15 -> x11, local copies, waits for them, and re-layouts: 2.54 us -> 0.38 us
    convert_element_type x1 -> x2, other arithmetic: 0.07 us -> 2.16 us  [the longest x1 2.1 us: per_device(): normed = (centered * inverse * layer_norm_gain).astype(BF)]
    all_to_all x1, starting transfers between devices: 8.64 us -> 6.57 us  [per_device(): summed = jnp.sum(lax.all_to_all(copies, DP, 0, 0, tiled=True), axis=0)]
    ppermute x3, waiting for transfers between devices: 11.4 us -> 9.57 us  [per_device(): x_term = x_term + lax.ppermute(leaves, DP, pairs).astype(F32)]
    convert_element_type x1, other arithmetic: 2.2 us -> 0.5 us  [per_device(): chip = (term_keep.astype(F32) + term_got.astype(F32)).astype(BF)]
  transfers between devices with their start and end apart: 10 -> 10, of which waited for: 6 -> 7; matrix products, arithmetic and copies ran while one was open for 10% -> 8% of each run, Pallas kernels for 0% -> 0%
where the time goes in v6:
time: 120 us; the launch traced here: 119 us
  waiting for transfers between devices  50.2 us (42%)
  starting transfers between devices  46.9 us (39%)
  other arithmetic  10.1 us (8%)
  local copies, waits for them, and re-layouts  5.55 us (5%)
  Pallas kernels  4.17 us (3%)
    all_to_all x1, waiting for transfers between devices, per_device(): lax.all_to_all(copies, DP, 0, 0, axis_index_groups=SAME_CORE, tiled=True)  16.2 us
    all_to_all x1, waiting for transfers between devices, per_device(): near = lax.all_to_all(part, MP, 0, 0, axis_index_groups=NEAR, tiled=True)  14.6 us
    all_to_all x1, starting transfers between devices, per_device(): far = lax.all_to_all(pair, MP, 0, 0, axis_index_groups=FAR, tiled=True)  13.9 us
    ppermute x3, waiting for transfers between devices, per_device(): x_term = x_term + lax.ppermute(leaves, DP, pairs).astype(F32)  9.57 us
    ppermute x3, starting transfers between devices, per_device(): x_term = x_term + lax.ppermute(leaves, DP, pairs).astype(F32)  8.41 us
    all_to_all x1, starting transfers between devices, per_device(): summed = jnp.sum(lax.all_to_all(copies, DP, 0, 0, tiled=True), axis=0)  6.57 us
    all_to_all x1, waiting for transfers between devices, per_device(): summed = jnp.sum(lax.all_to_all(copies, DP, 0, 0, tiled=True), axis=0)  5.2 us
    all_to_all x1, starting transfers between devices, per_device(): near = lax.all_to_all(part, MP, 0, 0, axis_index_groups=NEAR, tiled=True)  5.07 us
  transfers between devices with their start and end apart: 10, of which 7 were waited for; matrix products, arithmetic and copies ran while one was open for 8% of the time, Pallas kernels for 0%

profile of v6, /device:TPU:33, one launch (start us, length us, event | category | flops | bytes accessed | tf_op | source)
XLA Modules:
  0.0 118.9 jit_solution(13786158427892955849)
XLA Ops:
  0.6 0.0 copy-start.4
  0.6 0.0 copy-start.3
  0.7 2.2 %broadcast_in_dim.11 = bf16[8,192,384]{2,1,0:T(8,128)(2,1)} broadcast(bf16[192,384]{1,0:T(8,128)(2,1)} %param.8), dimensions={1,2} | broadcast | bytes 1327104 | tf_op jit(solution)/shard_map/gather_w/broadcast_in_dim | solution.py:166
  2.8 5.0 %all-to-all-start = ((bf16[8,192,384]{2,1,0:T(8,128)(2,1)}), bf16[8,192,384]{2,1,0:T(8,128)(2,1)S(1)}, u32[]{:S(2)}, u32[]{:S(2)}) async-start(bf16[8,192,384]{2,1,0:T(8,128)(2,1)} %broadcast_in_dim.11), calls=%async_computation | async-start | bytes 2359296 | tf_op jit(solution)/shard_map/gather_w/all_to_all | solution.py:167
  7.8 0.0 copy-done.4
  7.9 0.1 pad.21.clone
  8.0 0.0 copy-done.3
  8.0 0.3 convert_reduce_fusion
  8.3 0.6 fusion.2
  8.9 16.2 %all-to-all-done.own_ref = bf16[8,192,384]{2,1,0:T(8,128)(2,1)S(1)} async-done(((bf16[8,192,384]{2,1,0:T(8,128)(2,1)}), bf16[8,192,384]{2,1,0:T(8,128)(2,1)S(1)}, u32[]{:S(2)}, u32[]{:S(2)}) %all-to-all-start) | async-done | bytes 1179680 | tf_op jit(solution)/shard_map/gather_w/all_to_all | solution.py:167
  25.1 3.5 %collective-permute-start = (bf16[8,192,384]{2,1,0:T(8,128)(2,1)S(1)}, bf16[8,192,384]{2,1,0:T(8,128)(2,1)S(1)}, u32[]{:S(2)}, u32[]{:S(2)}) collective-permute-start(bf16[8,192,384]{2,1,0:T(8,128)(2,1)S(1)} %all-to-all-done.own_ref), channel_id=1, source_target_pairs={{0,32},{32,0},{64,96},{96,64},{128,160},{160,128},{192,224},{224,1... | collective-permute-start | bytes 3538952 | tf_op jit(solution)/shard_map/gather_w/ppermute | solution.py:168
  28.6 2.1 %fusion.4 = bf16[256,3072]{1,0:T(8,128)(2,1)S(1)} fusion(bf16[256,3072]{1,0:T(8,128)(2,1)} %param.6, f32[3072]{0:T(1024)S(1)} %copy-done.4, f32[256]{0:T(256)S(1)} %add_rsqrt_fusion, f32[256]{0:T(256)S(1)} %broadcast_multiply_fusion), kind=kLoop, calls=%fused_computation.7 | loop fusion | flops 3932160 | bytes 3160064 | tf_op jit(solution)/shard_map/input_norm/convert_element_type | solution.py:175
  30.7 0.0 copy-start
  30.7 0.0 copy-start.1
  30.7 0.0 copy-start.2
  30.8 0.5 maximum_maximum_fusion.x_ref
  31.3 0.0 collective-permute-done.other_ref
  31.3 0.3 copy-done
  31.6 0.0 copy-done.1
  31.6 0.0 copy-done.2
  31.6 4.2 %head.1 = (bf16[256,128]{1,0:T(8,128)(2,1)}, bf16[256,384]{1,0:T(8,128)(2,1)S(1)}, bf16[4,1552,128]{2,1,0:T(8,128)(2,1)}, f32[8,128]{1,0:T(8,128)S(1)}) custom-call(s32[1]{0:T(128)} %bitcast.core_ref, bf16[272,3072]{1,0:T(8,128)(2,1)S(1)} %maximum_maximum_fusion.x_ref, bf16[8,192,384]{2,1,0:T(8,128)(2,1)S(1)} %all-to-all-done.own_ref, ...), custom_call_target="tpu_custom_call" | custom-call | flops 1400000000 | bytes 9000000 | tf_op jit(solution)/shard_map/head/pallas_call | solution.py:137
  35.7 5.1 %all-to-all-start.1 = ((bf16[4,1552,128]{2,1,0:T(8,128)(2,1)}), bf16[4,1552,128]{2,1,0:T(8,128)(2,1)}, u32[]{:S(2)}, u32[]{:S(2)}) async-start(bf16[4,1552,128]{2,1,0:T(8,128)(2,1)} %get-tuple-element.11), calls=%async_computation.1 | async-start | bytes 3178496 | tf_op jit(solution)/shard_map/input_gradient_near/all_to_all | solution.py:189
  40.8 1.0 convolution_convert_fusion
  41.8 0.1 fusion.6
  42.0 2.5 %collective-permute-start.1 = (bf16[8,192,384]{2,1,0:T(8,128)(2,1)S(1)}, bf16[8,192,384]{2,1,0:T(8,128)(2,1)S(1)}, u32[]{:S(2)}, u32[]{:S(2)}) collective-permute-start(bf16[8,192,384]{2,1,0:T(8,128)(2,1)S(1)} %fusion.6), channel_id=1, source_target_pairs={{0,32},{32,0},{64,96},{96,64},{128,160},{160,128},{192,224},{224,1... | collective-permute-start | bytes 3538952 | tf_op jit(solution)/shard_map/w_grad/ppermute | solution.py:195
  44.5 2.4 %collective-permute-done.1 = bf16[8,192,384]{2,1,0:T(8,128)(2,1)S(1)} collective-permute-done((bf16[8,192,384]{2,1,0:T(8,128)(2,1)S(1)}, bf16[8,192,384]{2,1,0:T(8,128)(2,1)S(1)}, u32[]{:S(2)}, u32[]{:S(2)}) %collective-permute-start.1) | collective-permute-done | bytes 1179680 | tf_op jit(solution)/shard_map/w_grad/ppermute | solution.py:195
  46.9 0.5 fusion.5
  47.4 14.6 %all-to-all-done.1 = bf16[4,1552,128]{2,1,0:T(8,128)(2,1)} async-done(((bf16[4,1552,128]{2,1,0:T(8,128)(2,1)}), bf16[4,1552,128]{2,1,0:T(8,128)(2,1)}, u32[]{:S(2)}, u32[]{:S(2)}) %all-to-all-start.1) | async-done | bytes 1589280 | tf_op jit(solution)/shard_map/input_gradient_near/all_to_all | solution.py:189
  62.0 0.7 convert_reduce_fusion.3
  62.7 1.7 %convert_reduce_fusion.1 = f32[1536,128]{1,0:T(8,128)S(1)} fusion(bf16[4,1552,128]{2,1,0:T(8,128)(2,1)} %all-to-all-done.1), kind=kLoop, calls=%fused_computation.8 | loop fusion | flops 1376256 | bytes 2359296 | tf_op jit(solution)/shard_map/sum_over_near/reduce_sum | solution.py:205
  64.4 0.1 add_convert_fusion
  64.6 0.1 fusion.18
  64.7 0.8 pad_maximum_fusion
  65.4 13.9 %all-to-all-start.2 = ((bf16[8,208,128]{2,1,0:T(8,128)(2,1)}), bf16[8,208,128]{2,1,0:T(8,128)(2,1)S(1)}, u32[]{:S(2)}, u32[]{:S(2)}) async-start(bf16[8,208,128]{2,1,0:T(8,128)(2,1)} %pad_maximum_fusion), calls=%async_computation.2 | async-start | bytes 851968 | tf_op jit(solution)/shard_map/sum_over_near/all_to_all | solution.py:210
  79.4 0.1 dynamic_slice.19
  79.4 0.1 dynamic-slice_bitcast_fusion.2
  79.5 1.9 %collective-permute-start.2 = (bf16[2,192,384]{2,1,0:T(8,128)(2,1)S(1)}, bf16[2,192,384]{2,1,0:T(8,128)(2,1)S(1)}, u32[]{:S(2)}, u32[]{:S(2)}) collective-permute-start(bf16[2,192,384]{2,1,0:T(8,128)(2,1)S(1)} %get-tuple-element.16), channel_id=1, source_target_pairs={{0,128},{32,160},{64,192},{96,224},{128,256},{160,288},{192,320},{... | collective-permute-start | bytes 884744 | tf_op jit(solution)/shard_map/w_grad/ppermute | solution.py:201
  81.5 2.7 %collective-permute-start.3 = (bf16[2,192,384]{2,1,0:T(8,128)(2,1)S(1)}, bf16[2,192,384]{2,1,0:T(8,128)(2,1)S(1)}, u32[]{:S(2)}, u32[]{:S(2)}) collective-permute-start(bf16[2,192,384]{2,1,0:T(8,128)(2,1)S(1)} %get-tuple-element.18), channel_id=1, source_target_pairs={{0,256},{32,288},{64,320},{96,352},{128,384},{160,416},{192,448},{... | collective-permute-start | bytes 884744 | tf_op jit(solution)/shard_map/w_grad/ppermute | solution.py:201
  84.1 3.8 %collective-permute-start.4 = (bf16[2,192,384]{2,1,0:T(8,128)(2,1)S(1)}, bf16[2,192,384]{2,1,0:T(8,128)(2,1)S(1)}, u32[]{:S(2)}, u32[]{:S(2)}) collective-permute-start(bf16[2,192,384]{2,1,0:T(8,128)(2,1)S(1)} %get-tuple-element.17), channel_id=1, source_target_pairs={{0,384},{32,416},{64,448},{96,480},{128,0},{160,32},{192,64},{224,... | collective-permute-start | bytes 884744 | tf_op jit(solution)/shard_map/w_grad/ppermute | solution.py:201
  88.0 1.0 constant_dynamic-slice_fusion
  89.0 0.1 copy.23
  89.1 0.7 fusion.20
  89.8 7.0 %collective-permute-done.2 = bf16[2,192,384]{2,1,0:T(8,128)(2,1)S(1)} collective-permute-done((bf16[2,192,384]{2,1,0:T(8,128)(2,1)S(1)}, bf16[2,192,384]{2,1,0:T(8,128)(2,1)S(1)}, u32[]{:S(2)}, u32[]{:S(2)}) %collective-permute-start.2) | collective-permute-done | bytes 294944 | tf_op jit(solution)/shard_map/w_grad/ppermute | solution.py:201
  96.8 0.0 collective-permute-done.3
  96.8 2.6 %collective-permute-done.4 = bf16[2,192,384]{2,1,0:T(8,128)(2,1)S(1)} collective-permute-done((bf16[2,192,384]{2,1,0:T(8,128)(2,1)S(1)}, bf16[2,192,384]{2,1,0:T(8,128)(2,1)S(1)}, u32[]{:S(2)}, u32[]{:S(2)}) %collective-permute-start.4) | collective-permute-done | bytes 294944 | tf_op jit(solution)/shard_map/w_grad/ppermute | solution.py:201
  99.4 0.2 fusion.10
  99.6 1.9 %collective-permute-start.5 = (bf16[192,384]{1,0:T(8,128)(2,1)S(1)}, bf16[192,384]{1,0:T(8,128)(2,1)S(1)}, u32[]{:S(2)}, u32[]{:S(2)}) collective-permute-start(bf16[192,384]{1,0:T(8,128)(2,1)S(1)} %fusion.12), channel_id=1, source_target_pairs={{0,64},{32,96},{64,0},{96,32},{128,192},{160,224},{192,128},{224,1... | collective-permute-start | bytes 442376 | tf_op jit(solution)/shard_map/w_grad_y/ppermute | solution.py:216
  101.5 2.2 %all-to-all-done.2 = bf16[8,208,128]{2,1,0:T(8,128)(2,1)S(1)} async-done(((bf16[8,208,128]{2,1,0:T(8,128)(2,1)}), bf16[8,208,128]{2,1,0:T(8,128)(2,1)S(1)}, u32[]{:S(2)}, u32[]{:S(2)}) %all-to-all-start.2) | async-done | bytes 426016 | tf_op jit(solution)/shard_map/sum_over_near/all_to_all | solution.py:210
  103.7 0.1 convert_reduce_fusion.2
  103.9 0.8 fusion.16
  104.7 0.6 broadcast_in_dim.14
  105.4 6.6 %all-to-all-start.3 = ((f32[16,8,128]{2,1,0:T(8,128)}), f32[16,8,128]{2,1,0:T(8,128)S(1)}, u32[]{:S(2)}, u32[]{:S(2)}) async-start(f32[16,8,128]{2,1,0:T(8,128)} %broadcast_in_dim.14), calls=%async_computation.3 | async-start | bytes 131072 | tf_op jit(solution)/shard_map/gain_gradients/all_to_all | solution.py:240
  111.9 0.0 collective-permute-done.5
  111.9 0.7 fusion.11
  112.6 5.2 %all-to-all-done.3 = f32[16,8,128]{2,1,0:T(8,128)S(1)} async-done(((f32[16,8,128]{2,1,0:T(8,128)}), f32[16,8,128]{2,1,0:T(8,128)S(1)}, u32[]{:S(2)}, u32[]{:S(2)}) %all-to-all-start.3) | async-done | bytes 65568 | tf_op jit(solution)/shard_map/gain_gradients/all_to_all | solution.py:240
  117.9 0.5 fusion.25
  118.4 0.5 slice_bitcast_fusion
  (23 shorter events, 0.2 us)
Async XLA Ops:
  0.6 7.2 %copy-start.4 = (f32[3072]{0:T(1024)S(1)}, f32[3072]{0:T(1024)}, u32[]{:S(2)}) copy-start(f32[3072]{0:T(1024)} %param.7) | copy-start | bytes 36868
  0.6 7.4 %copy-start.3 = (bf16[256,3072]{1,0:T(8,128)(2,1)S(1)}, bf16[256,3072]{1,0:T(8,128)(2,1)}, u32[]{:S(2)}) copy-start(bf16[256,3072]{1,0:T(8,128)(2,1)} %param.6) | copy-start | bytes 4718596
  2.8 22.3 %all-to-all-start = ((bf16[8,192,384]{2,1,0:T(8,128)(2,1)}), bf16[8,192,384]{2,1,0:T(8,128)(2,1)S(1)}, u32[]{:S(2)}, u32[]{:S(2)}) async-start(bf16[8,192,384]{2,1,0:T(8,128)(2,1)} %broadcast_in_dim.11), calls=%async_computation | async-start | bytes 2359296 | tf_op jit(solution)/shard_map/gather_w/all_to_all | solution.py:167
  25.1 6.2 %collective-permute-start = (bf16[8,192,384]{2,1,0:T(8,128)(2,1)S(1)}, bf16[8,192,384]{2,1,0:T(8,128)(2,1)S(1)}, u32[]{:S(2)}, u32[]{:S(2)}) collective-permute-start(bf16[8,192,384]{2,1,0:T(8,128)(2,1)S(1)} %all-to-all-done.own_ref), channel_id=1, source_target_pairs={{0,32},{32,0},{64,96},{96,64},{128,160},{160,128},{192,224},{224,1... | collective-permute-start | bytes 3538952 | tf_op jit(solution)/shard_map/gather_w/ppermute | solution.py:168
  30.7 0.8 copy-start
  30.7 0.8 copy-start.1
  30.7 0.8 copy-start.2
  35.7 26.3 %all-to-all-start.1 = ((bf16[4,1552,128]{2,1,0:T(8,128)(2,1)}), bf16[4,1552,128]{2,1,0:T(8,128)(2,1)}, u32[]{:S(2)}, u32[]{:S(2)}) async-start(bf16[4,1552,128]{2,1,0:T(8,128)(2,1)} %get-tuple-element.11), calls=%async_computation.1 | async-start | bytes 3178496 | tf_op jit(solution)/shard_map/input_gradient_near/all_to_all | solution.py:189
  42.0 4.9 %collective-permute-start.1 = (bf16[8,192,384]{2,1,0:T(8,128)(2,1)S(1)}, bf16[8,192,384]{2,1,0:T(8,128)(2,1)S(1)}, u32[]{:S(2)}, u32[]{:S(2)}) collective-permute-start(bf16[8,192,384]{2,1,0:T(8,128)(2,1)S(1)} %fusion.6), channel_id=1, source_target_pairs={{0,32},{32,0},{64,96},{96,64},{128,160},{160,128},{192,224},{224,1... | collective-permute-start | bytes 3538952 | tf_op jit(solution)/shard_map/w_grad/ppermute | solution.py:195
  65.4 38.3 %all-to-all-start.2 = ((bf16[8,208,128]{2,1,0:T(8,128)(2,1)}), bf16[8,208,128]{2,1,0:T(8,128)(2,1)S(1)}, u32[]{:S(2)}, u32[]{:S(2)}) async-start(bf16[8,208,128]{2,1,0:T(8,128)(2,1)} %pad_maximum_fusion), calls=%async_computation.2 | async-start | bytes 851968 | tf_op jit(solution)/shard_map/sum_over_near/all_to_all | solution.py:210
  79.5 17.2 %collective-permute-start.2 = (bf16[2,192,384]{2,1,0:T(8,128)(2,1)S(1)}, bf16[2,192,384]{2,1,0:T(8,128)(2,1)S(1)}, u32[]{:S(2)}, u32[]{:S(2)}) collective-permute-start(bf16[2,192,384]{2,1,0:T(8,128)(2,1)S(1)} %get-tuple-element.16), channel_id=1, source_target_pairs={{0,128},{32,160},{64,192},{96,224},{128,256},{160,288},{192,320},{... | collective-permute-start | bytes 884744 | tf_op jit(solution)/shard_map/w_grad/ppermute | solution.py:201
  81.5 15.3 %collective-permute-start.3 = (bf16[2,192,384]{2,1,0:T(8,128)(2,1)S(1)}, bf16[2,192,384]{2,1,0:T(8,128)(2,1)S(1)}, u32[]{:S(2)}, u32[]{:S(2)}) collective-permute-start(bf16[2,192,384]{2,1,0:T(8,128)(2,1)S(1)} %get-tuple-element.18), channel_id=1, source_target_pairs={{0,256},{32,288},{64,320},{96,352},{128,384},{160,416},{192,448},{... | collective-permute-start | bytes 884744 | tf_op jit(solution)/shard_map/w_grad/ppermute | solution.py:201
  84.1 15.2 %collective-permute-start.4 = (bf16[2,192,384]{2,1,0:T(8,128)(2,1)S(1)}, bf16[2,192,384]{2,1,0:T(8,128)(2,1)S(1)}, u32[]{:S(2)}, u32[]{:S(2)}) collective-permute-start(bf16[2,192,384]{2,1,0:T(8,128)(2,1)S(1)} %get-tuple-element.17), channel_id=1, source_target_pairs={{0,384},{32,416},{64,448},{96,480},{128,0},{160,32},{192,64},{224,... | collective-permute-start | bytes 884744 | tf_op jit(solution)/shard_map/w_grad/ppermute | solution.py:201
  99.6 12.4 %collective-permute-start.5 = (bf16[192,384]{1,0:T(8,128)(2,1)S(1)}, bf16[192,384]{1,0:T(8,128)(2,1)S(1)}, u32[]{:S(2)}, u32[]{:S(2)}) collective-permute-start(bf16[192,384]{1,0:T(8,128)(2,1)S(1)} %fusion.12), channel_id=1, source_target_pairs={{0,64},{32,96},{64,0},{96,32},{128,192},{160,224},{192,128},{224,1... | collective-permute-start | bytes 442376 | tf_op jit(solution)/shard_map/w_grad_y/ppermute | solution.py:216
  105.4 12.5 %all-to-all-start.3 = ((f32[16,8,128]{2,1,0:T(8,128)}), f32[16,8,128]{2,1,0:T(8,128)S(1)}, u32[]{:S(2)}, u32[]{:S(2)}) async-start(f32[16,8,128]{2,1,0:T(8,128)} %broadcast_in_dim.14), calls=%async_computation.3 | async-start | bytes 131072 | tf_op jit(solution)/shard_map/gain_gradients/all_to_all | solution.py:240

commit v7 on v6

--- a/solution.py
+++ b/solution.py
@@ -1,3 +1,5 @@
+import functools
+
 import jax
 import jax.numpy as jnp
 from jax import lax
@@ -49,17 +51,6 @@
     hi = sums.astype(BF).astype(F32)
     row = lax.broadcasted_iota(jnp.int32, sums.shape, 0)
     return jnp.where(row % 4 < 2, hi, sums - hi).astype(BF)
-
-
-def unpack(got):
-    first, second = got[0:2] + got[2:4], got[8:10] + got[10:12]
-    return jnp.concatenate([first] * 4 + [second] * 4, axis=0)
-
-
-def after(value, other):
-    first = other.reshape(-1, other.shape[-1])[:1, :128].astype(F32)
-    zero = jnp.minimum(jnp.abs(first), 0.0)
-    return value + jnp.concatenate([zero] * (value.shape[-1] // 128), axis=1)
 
 
 def head_kernel(
@@ -152,6 +143,73 @@
     )(core.reshape(1), x, own, other, grad, q_gain, k_gain)
 
 
+def near_kernel(near_ref, *refs):
+    out_ref = refs[-1]
+    blocks, chunk = out_ref.shape[0], out_ref.shape[1] - 16
+    add = lambda at, size: sum(
+        near_ref[group, at : at + size].astype(F32) for group in range(near_ref.shape[0])
+    )
+    got = add(blocks * chunk, 16)
+    row = lax.broadcasted_iota(jnp.int32, got.shape, 0)
+    both = got + pltpu.roll(got, 14, 0)
+    packed = pack(jnp.where(row % 8 < 2, both, pltpu.roll(both, 2, 0)))
+    for k in range(blocks):
+        out_ref[k, :chunk] = add(k * chunk, chunk).astype(BF)
+        out_ref[k, chunk:] = packed
+
+
+def sum_near(near, order):
+    vmem = pl.BlockSpec(memory_space=pltpu.VMEM)
+    blocks = NZ // 2
+    chunk = (near.shape[1] - 16) // blocks
+    return pl.pallas_call(
+        near_kernel,
+        in_specs=[vmem] + [pl.BlockSpec(memory_space=pl.ANY)] * len(order),
+        out_specs=vmem,
+        out_shape=jax.ShapeDtypeStruct((blocks, chunk + 16, near.shape[2]), BF),
+        compiler_params=pltpu.CompilerParams(vmem_limit_bytes=24 * 2**20),
+    )(near, *order)
+
+
+def far_kernel(width, far_ref, xhat_ref, gain_ref, inverse_ref, heads_ref, rows_ref, small_ref):
+    share = xhat_ref.shape[0]
+    lane = far_ref.shape[2]
+    total = sum(far_ref[k].astype(F32) for k in range(far_ref.shape[0]))
+    last = 2 * share
+    product = jnp.zeros((share, lane), F32)
+    for half in range(2):
+        at = slice(half * lane, (half + 1) * lane)
+        dnormed = total[half * share : (half + 1) * share]
+        sums = total[last + 8 * half : last + 8 * half + 8]
+        plain = sums[0:1] + sums[2:3]
+        cross = sums[1:2] + sums[3:4]
+        xhat = xhat_ref[:, at]
+        rows_ref[:, at] = (
+            (dnormed * gain_ref[...] - plain / width - xhat * (cross / width))
+            * inverse_ref[:, at]
+        ).astype(BF)
+        product = product + dnormed * xhat
+    small_ref[0] = heads_ref[...]
+    small_ref[0, 7:8, :share] = jnp.sum(product.T, axis=0, keepdims=True)
+    small = small_ref[0]
+    for at in range(1, small_ref.shape[0]):
+        small_ref[at] = small
+
+
+def finish(width, far, xhat, gain, inverse, head_gains):
+    vmem = pl.BlockSpec(memory_space=pltpu.VMEM)
+    return pl.pallas_call(
+        functools.partial(far_kernel, width),
+        in_specs=[vmem] * 5,
+        out_specs=[vmem] * 2,
+        out_shape=[
+            jax.ShapeDtypeStruct(xhat.shape, BF),
+            jax.ShapeDtypeStruct((NX * NYL * NC,) + head_gains.shape, F32),
+        ],
+        compiler_params=pltpu.CompilerParams(vmem_limit_bytes=24 * 2**20),
+    )(far, xhat, gain, inverse, head_gains)
+
+
 def per_device(tokens, layer_norm_gain, w_qkv, q_gain, k_gain, ctx_grad):
     rows, width = tokens.shape
     w_rows, columns = w_qkv.shape
@@ -185,7 +243,6 @@
         )
 
     with jax.named_scope("input_gradient_near"):
-        chunk = 2 * share
         near = lax.all_to_all(part, MP, 0, 0, axis_index_groups=NEAR, tiled=True)
 
     with jax.named_scope("w_grad"):
@@ -196,51 +253,37 @@
         chip = (term_keep.astype(F32) + term_got.astype(F32)).astype(BF)
         chip = chip.reshape(NX, NYL, w_rows, columns)
         x_term = lax.dynamic_index_in_dim(chip, x_at, 0, False).astype(F32)
-        for step, pairs in enumerate(X_STEPS, 1):
-            leaves = lax.dynamic_index_in_dim(chip, (x_at + step) % NX, 0, False)
-            x_term = x_term + lax.ppermute(leaves, DP, pairs).astype(F32)
+        x_got = [
+            lax.ppermute(
+                lax.dynamic_index_in_dim(chip, (x_at + step) % NX, 0, False), DP, pairs
+            )
+            for step, pairs in enumerate(X_STEPS, 1)
+        ]
 
     with jax.named_scope("sum_over_near"):
-        many = NZ // 2 * chunk
-        pair = jnp.sum(near[:, :many].astype(F32), axis=0)
-        pair = after(pair, chip).astype(BF).reshape(NZ // 2, chunk, lane)
-        sums = unpack(jnp.sum(near[:, many:].astype(F32), axis=0))
-        riding = jnp.broadcast_to(pack(sums)[None], (NZ // 2, 16, lane))
-        pair = jnp.concatenate([pair, riding], axis=1)
+        pair = sum_near(near, [x_got[0], x_got[2]])
         far = lax.all_to_all(pair, MP, 0, 0, axis_index_groups=FAR, tiled=True)
 
     with jax.named_scope("w_grad_y"):
-        x_term = after(x_term, pair)
+        x_term = x_term + sum(got.astype(F32) for got in x_got)
         leaves = jnp.where(y_lo == 0, x_term[1], x_term[0]).astype(BF)
         stays = jnp.where(y_lo == 0, x_term[0], x_term[1])
         w_grad = (stays + lax.ppermute(leaves, DP, YLO_SWAP).astype(F32)).astype(BF)
-
-    with jax.named_scope("sum_over_far"):
-        total = jnp.sum(far.astype(F32), axis=0)
-        dnormed = jnp.concatenate([total[:share], total[share:chunk]], axis=1)
-        sums = unpack(total[chunk:])
-        plain = jnp.concatenate([sums[0:1], sums[8:9]], axis=1)
-        cross = jnp.concatenate([sums[1:2], sums[9:10]], axis=1)
 
     with jax.named_scope("input_gradient"):
         start = mp * share
         tokens_share = lax.dynamic_slice_in_dim(tokens, start, share, 1).astype(F32)
         xhat_share = ((tokens_share - mean) * inverse).T
         gain_share = lax.dynamic_slice_in_dim(layer_norm_gain, start, share, 0)
-        input_gradient_rows = (
-            (dnormed * gain_share[:, None] - plain / width - xhat_share * (cross / width))
-            * inverse.T
-        ).T.astype(BF)
-        gain_portion = jnp.sum(dnormed * xhat_share, axis=1)
+        gradient, copies = finish(
+            width, far, xhat_share, gain_share[:, None], inverse.T, head_gains
+        )
 
     with jax.named_scope("gain_gradients"):
-        portion = jnp.pad(gain_portion, (0, 128 - share))[None]
-        small = jnp.concatenate([head_gains[:7], portion], axis=0)
-        copies = jnp.broadcast_to(small[None], (NX * NYL * NC, 8, 128))
         summed = jnp.sum(lax.all_to_all(copies, DP, 0, 0, tiled=True), axis=0)
     return (
         context,
-        input_gradient_rows,
+        gradient.T,
         summed[7, :share],
         w_grad,
         summed[0:1],

time: 120 us -> 120 us (level)
  starting transfers between devices: 46.9 us -> 51.4 us
  waiting for transfers between devices: 50.2 us -> 45.7 us
  other arithmetic: 10.1 us -> 6.99 us
  Pallas kernels: 4.17 us -> 5.9 us
  local copies, waits for them, and re-layouts: 5.55 us -> 6.96 us
    all_to_all x1, waiting for transfers between devices: 14.6 us -> 0.01 us  [per_device(): near = lax.all_to_all(part, MP, 0, 0, axis_index_groups=NEAR, tiled=True)]
    all_to_all x1, waiting for transfers between devices: 2.24 us -> 11.3 us  [per_device(): far = lax.all_to_all(pair, MP, 0, 0, axis_index_groups=FAR, tiled=True)]
    reduce_sum x4 -> x0, other arithmetic: 3.3 us -> none  [the longest x1 1.7 us: per_device(): pair = jnp.sum(near[:, :many].astype(F32), axis=0)]
    all_to_all x1, starting transfers between devices: 6.57 us -> 8.8 us  [per_device(): summed = jnp.sum(lax.all_to_all(copies, DP, 0, 0, tiled=True), axis=0)]
    ppermute x3, starting transfers between devices: 8.41 us -> 10.6 us  [per_device(): lax.ppermute(lax.dynamic_index_in_dim(chip, (x_at + step) % NX, 0, False)...]
    convert_element_type x1, other arithmetic: 0.5 us -> 2.44 us  [per_device(): chip = (term_keep.astype(F32) + term_got.astype(F32)).astype(BF)]
    pallas_call x0 -> x2, Pallas kernels: none -> 1.74 us  [the longest x1 0.96 us: sum_near(): pl.pallas_call(near_kernel, in_specs=[vmem] + [pl.BlockSpec(memory_space=...]
    unnamed x11 -> x13, local copies, waits for them, and re-layouts: 0.38 us -> 1.66 us
  transfers between devices with their start and end apart: 10 -> 10, of which waited for: 7 -> 7; matrix products, arithmetic and copies ran while one was open for 8% -> 9% of each run, Pallas kernels for 0% -> 1%
where the time goes in v7:
time: 120 us; the launch traced here: 119 us
  starting transfers between devices  51.4 us (43%)
  waiting for transfers between devices  45.7 us (38%)
  other arithmetic  6.99 us (6%)
  local copies, waits for them, and re-layouts  6.96 us (6%)
  Pallas kernels  5.9 us (5%)
    all_to_all x1, waiting for transfers between devices, per_device(): lax.all_to_all(copies, DP, 0, 0, axis_index_groups=SAME_CORE, tiled=True)  16.2 us
    all_to_all x1, starting transfers between devices, per_device(): far = lax.all_to_all(pair, MP, 0, 0, axis_index_groups=FAR, tiled=True)  13.9 us
    all_to_all x1, waiting for transfers between devices, per_device(): far = lax.all_to_all(pair, MP, 0, 0, axis_index_groups=FAR, tiled=True)  11.3 us
    ppermute x3, starting transfers between devices, per_device(): lax.ppermute(lax.dynamic_index_in_dim(chip, (x_at + step) % NX, 0, False)...  10.6 us
    ppermute x3, waiting for transfers between devices, per_device(): lax.ppermute(lax.dynamic_index_in_dim(chip, (x_at + step) % NX, 0, False)...  10.5 us
    all_to_all x1, starting transfers between devices, per_device(): summed = jnp.sum(lax.all_to_all(copies, DP, 0, 0, tiled=True), axis=0)  8.8 us
    all_to_all x1, waiting for transfers between devices, per_device(): summed = jnp.sum(lax.all_to_all(copies, DP, 0, 0, tiled=True), axis=0)  5.16 us
    all_to_all x1, starting transfers between devices, per_device(): near = lax.all_to_all(part, MP, 0, 0, axis_index_groups=NEAR, tiled=True)  5.07 us
  transfers between devices with their start and end apart: 10, of which 7 were waited for; matrix products, arithmetic and copies ran while one was open for 9% of the time, Pallas kernels for 1%

profile of v7, /device:TPU:33, one launch (start us, length us, event | category | flops | bytes accessed | tf_op | source)
XLA Modules:
  0.0 118.8 jit_solution(7546023327961612597)
XLA Ops:
  0.6 0.0 copy-start.5
  0.6 0.0 copy-start.4
  0.7 2.2 %broadcast_in_dim.7 = bf16[8,192,384]{2,1,0:T(8,128)(2,1)} broadcast(bf16[192,384]{1,0:T(8,128)(2,1)} %param.8), dimensions={1,2} | broadcast | bytes 1327104 | tf_op jit(solution)/shard_map/gather_w/broadcast_in_dim | solution.py:224
  2.8 5.0 %all-to-all-start = ((bf16[8,192,384]{2,1,0:T(8,128)(2,1)}), bf16[8,192,384]{2,1,0:T(8,128)(2,1)S(1)}, u32[]{:S(2)}, u32[]{:S(2)}) async-start(bf16[8,192,384]{2,1,0:T(8,128)(2,1)} %broadcast_in_dim.7), calls=%async_computation | async-start | bytes 2359296 | tf_op jit(solution)/shard_map/gather_w/all_to_all | solution.py:225
  7.8 0.0 copy-done.5
  7.9 0.1 pad.3.clone
  8.0 0.0 copy-done.4
  8.0 0.3 convert_reduce_fusion
  8.3 0.6 fusion.2
  8.9 16.2 %all-to-all-done.own_ref = bf16[8,192,384]{2,1,0:T(8,128)(2,1)S(1)} async-done(((bf16[8,192,384]{2,1,0:T(8,128)(2,1)}), bf16[8,192,384]{2,1,0:T(8,128)(2,1)S(1)}, u32[]{:S(2)}, u32[]{:S(2)}) %all-to-all-start) | async-done | bytes 1179680 | tf_op jit(solution)/shard_map/gather_w/all_to_all | solution.py:225
  25.1 3.5 %collective-permute-start = (bf16[8,192,384]{2,1,0:T(8,128)(2,1)S(1)}, bf16[8,192,384]{2,1,0:T(8,128)(2,1)S(1)}, u32[]{:S(2)}, u32[]{:S(2)}) collective-permute-start(bf16[8,192,384]{2,1,0:T(8,128)(2,1)S(1)} %all-to-all-done.own_ref), channel_id=1, source_target_pairs={{0,32},{32,0},{64,96},{96,64},{128,160},{160,128},{192,224},{224,1... | collective-permute-start | bytes 3538952 | tf_op jit(solution)/shard_map/gather_w/ppermute | solution.py:226
  28.6 2.1 %fusion.4 = bf16[256,3072]{1,0:T(8,128)(2,1)S(1)} fusion(bf16[256,3072]{1,0:T(8,128)(2,1)} %param.6, f32[3072]{0:T(1024)S(1)} %copy-done.5, f32[256]{0:T(256)S(1)} %add_rsqrt_fusion, f32[256]{0:T(256)S(1)} %broadcast_multiply_fusion), kind=kLoop, calls=%fused_computation.7 | loop fusion | flops 3932160 | bytes 3160064 | tf_op jit(solution)/shard_map/input_norm/convert_element_type | solution.py:233
  30.7 0.0 copy-start
  30.7 0.0 copy-start.1
  30.7 0.0 copy-start.2
  30.8 0.5 maximum_maximum_fusion.x_ref
  31.3 0.0 collective-permute-done.other_ref
  31.3 0.2 copy-done
  31.6 0.0 copy-done.1
  31.6 0.0 copy-done.2
  31.6 4.2 %head.1 = (bf16[256,128]{1,0:T(8,128)(2,1)}, bf16[256,384]{1,0:T(8,128)(2,1)S(1)}, bf16[4,1552,128]{2,1,0:T(8,128)(2,1)}, f32[8,128]{1,0:T(8,128)S(1)}) custom-call(s32[1]{0:T(128)} %bitcast.core_ref, bf16[272,3072]{1,0:T(8,128)(2,1)S(1)} %maximum_maximum_fusion.x_ref, bf16[8,192,384]{2,1,0:T(8,128)(2,1)S(1)} %all-to-all-done.own_ref, ...), custom_call_target="tpu_custom_call" | custom-call | flops 1400000000 | bytes 9000000 | tf_op jit(solution)/shard_map/head/pallas_call | solution.py:128
  35.7 5.1 %all-to-all-start.1 = ((bf16[4,1552,128]{2,1,0:T(8,128)(2,1)}), bf16[4,1552,128]{2,1,0:T(8,128)(2,1)S(1)}, u32[]{:S(2)}, u32[]{:S(2)}) async-start(bf16[4,1552,128]{2,1,0:T(8,128)(2,1)} %get-tuple-element.13), calls=%async_computation.1 | async-start | bytes 3178496 | tf_op jit(solution)/shard_map/input_gradient_near/all_to_all | solution.py:246
  40.8 1.0 convolution_convert_fusion
  41.8 0.0 copy-start.3
  41.8 0.1 select_bitcast_fusion
  42.0 1.3 %copy-done.3 = bf16[3072,384]{1,0:T(8,128)(2,1)} copy-done((bf16[3072,384]{1,0:T(8,128)(2,1)}, bf16[3072,384]{1,0:T(8,128)(2,1)S(1)}, u32[]{:S(2)}) %copy-start.3) | copy-done | bytes 2359320
  43.3 2.5 %collective-permute-start.1 = (bf16[8,192,384]{2,1,0:T(8,128)(2,1)S(1)}, bf16[8,192,384]{2,1,0:T(8,128)(2,1)}, u32[]{:S(2)}, u32[]{:S(2)}) collective-permute-start(bf16[8,192,384]{2,1,0:T(8,128)(2,1)S(1)} %select_bitcast_fusion), channel_id=1, source_target_pairs={{0,32},{32,0},{64,96},{96,64},{128,160},{160,128},{192,224},{224,1... | collective-permute-start | bytes 3538952 | tf_op jit(solution)/shard_map/w_grad/ppermute | solution.py:252
  45.8 2.5 %collective-permute-done.1 = bf16[8,192,384]{2,1,0:T(8,128)(2,1)} collective-permute-done((bf16[8,192,384]{2,1,0:T(8,128)(2,1)S(1)}, bf16[8,192,384]{2,1,0:T(8,128)(2,1)}, u32[]{:S(2)}, u32[]{:S(2)}) %collective-permute-start.1) | collective-permute-done | bytes 1179680 | tf_op jit(solution)/shard_map/w_grad/ppermute | solution.py:252
  48.3 2.4 %fusion.5 = bf16[8,192,384]{2,1,0:T(8,128)(2,1)S(1)} fusion(bf16[8,192,384]{2,1,0:T(8,128)(2,1)} %collective-permute-done.1, pred[]{:T(512)S(6)} %eq.14, bf16[8,2,192,384]{3,2,1,0:T(8,128)(2,1)} %bitcast.47), kind=kLoop, calls=%fused_computation.9 | loop fusion | flops 2949120 | bytes 4718593 | tf_op jit(solution)/shard_map/w_grad/convert_element_type | solution.py:253
  50.8 0.8 dynamic-slice_bitcast_fusion
  51.6 1.9 %collective-permute-start.2 = (bf16[2,192,384]{2,1,0:T(8,128)(2,1)S(1)}, bf16[2,192,384]{2,1,0:T(8,128)(2,1)S(1)}, u32[]{:S(2)}, u32[]{:S(2)}) collective-permute-start(bf16[2,192,384]{2,1,0:T(8,128)(2,1)S(1)} %get-tuple-element.22), channel_id=1, source_target_pairs={{0,128},{32,160},{64,192},{96,224},{128,256},{160,288},{192,320},{... | collective-permute-start | bytes 884744 | tf_op jit(solution)/shard_map/w_grad/ppermute | solution.py:257
  53.5 4.6 %collective-permute-start.3 = (bf16[2,192,384]{2,1,0:T(8,128)(2,1)S(1)}, bf16[2,192,384]{2,1,0:T(8,128)(2,1)S(1)}, u32[]{:S(2)}, u32[]{:S(2)}) collective-permute-start(bf16[2,192,384]{2,1,0:T(8,128)(2,1)S(1)} %get-tuple-element.21), channel_id=1, source_target_pairs={{0,384},{32,416},{64,448},{96,480},{128,0},{160,32},{192,64},{224,... | collective-permute-start | bytes 884744 | tf_op jit(solution)/shard_map/w_grad/ppermute | solution.py:257
  58.1 4.8 %collective-permute-done.2.refs_0_ = bf16[2,192,384]{2,1,0:T(8,128)(2,1)S(1)} collective-permute-done((bf16[2,192,384]{2,1,0:T(8,128)(2,1)S(1)}, bf16[2,192,384]{2,1,0:T(8,128)(2,1)S(1)}, u32[]{:S(2)}, u32[]{:S(2)}) %collective-permute-start.2) | collective-permute-done | bytes 294944 | tf_op jit(solution)/shard_map/w_grad/ppermute | solution.py:257
  62.9 0.9 collective-permute-done.3.refs_1_
  63.8 0.0 all-to-all-done.1.near_ref
  63.8 1.0 sum_over_near.1
  64.7 13.9 %all-to-all-start.2 = ((bf16[8,208,128]{2,1,0:T(8,128)(2,1)}), bf16[8,208,128]{2,1,0:T(8,128)(2,1)S(1)}, u32[]{:S(2)}, u32[]{:S(2)}) async-start(bf16[8,208,128]{2,1,0:T(8,128)(2,1)} %sum_over_near.1), calls=%async_computation.2 | async-start | bytes 851968 | tf_op jit(solution)/shard_map/sum_over_near/all_to_all | solution.py:265
  78.6 4.1 %collective-permute-start.4 = (bf16[2,192,384]{2,1,0:T(8,128)(2,1)}, bf16[2,192,384]{2,1,0:T(8,128)(2,1)S(1)}, u32[]{:S(2)}, u32[]{:S(2)}) collective-permute-start(bf16[2,192,384]{2,1,0:T(8,128)(2,1)} %get-tuple-element.20), channel_id=1, source_target_pairs={{0,256},{32,288},{64,320},{96,352},{128,384},{160,416},{192,448},{... | collective-permute-start | bytes 884744 | tf_op jit(solution)/shard_map/w_grad/ppermute | solution.py:257
  82.8 1.0 constant_dynamic-slice_fusion
  83.8 0.1 copy.18
  83.9 0.1 dynamic-slice_bitcast_fusion.3
  84.0 0.1 copy.15.gain_ref
  84.1 4.8 %collective-permute-done.4 = bf16[2,192,384]{2,1,0:T(8,128)(2,1)S(1)} collective-permute-done((bf16[2,192,384]{2,1,0:T(8,128)(2,1)}, bf16[2,192,384]{2,1,0:T(8,128)(2,1)S(1)}, u32[]{:S(2)}, u32[]{:S(2)}) %collective-permute-start.4) | collective-permute-done | bytes 294944 | tf_op jit(solution)/shard_map/w_grad/ppermute | solution.py:257
  88.9 0.1 convert_add_fusion.1
  89.1 1.9 %collective-permute-start.5 = (bf16[192,384]{1,0:T(8,128)(2,1)S(1)}, bf16[192,384]{1,0:T(8,128)(2,1)S(1)}, u32[]{:S(2)}, u32[]{:S(2)}) collective-permute-start(bf16[192,384]{1,0:T(8,128)(2,1)S(1)} %fusion.7), channel_id=1, source_target_pairs={{0,64},{32,96},{64,0},{96,32},{128,192},{160,224},{192,128},{224,1... | collective-permute-start | bytes 442376 | tf_op jit(solution)/shard_map/w_grad_y/ppermute | solution.py:271
  91.1 11.3 %all-to-all-done.2.far_ref = bf16[8,208,128]{2,1,0:T(8,128)(2,1)S(1)} async-done(((bf16[8,208,128]{2,1,0:T(8,128)(2,1)}), bf16[8,208,128]{2,1,0:T(8,128)(2,1)S(1)}, u32[]{:S(2)}, u32[]{:S(2)}) %all-to-all-start.2) | async-done | bytes 426016 | tf_op jit(solution)/shard_map/sum_over_near/all_to_all | solution.py:265
  102.3 0.8 input_gradient.1
  103.1 8.8 %all-to-all-start.3 = ((f32[16,8,128]{2,1,0:T(8,128)}), f32[16,8,128]{2,1,0:T(8,128)S(1)}, u32[]{:S(2)}, u32[]{:S(2)}) async-start(f32[16,8,128]{2,1,0:T(8,128)} %get-tuple-element.17), calls=%async_computation.3 | async-start | bytes 131072 | tf_op jit(solution)/shard_map/gain_gradients/all_to_all | solution.py:283
  111.9 0.0 collective-permute-done.5
  111.9 0.7 fusion.6
  112.6 5.2 %all-to-all-done.3 = f32[16,8,128]{2,1,0:T(8,128)S(1)} async-done(((f32[16,8,128]{2,1,0:T(8,128)}), f32[16,8,128]{2,1,0:T(8,128)S(1)}, u32[]{:S(2)}, u32[]{:S(2)}) %all-to-all-start.3) | async-done | bytes 65568 | tf_op jit(solution)/shard_map/gain_gradients/all_to_all | solution.py:283
  117.8 0.5 fusion.8
  118.3 0.5 slice_bitcast_fusion.2
  (9 shorter events, 0.1 us)
Async XLA Ops:
  0.6 7.2 %copy-start.5 = (f32[3072]{0:T(1024)S(1)}, f32[3072]{0:T(1024)}, u32[]{:S(2)}) copy-start(f32[3072]{0:T(1024)} %param.7) | copy-start | bytes 36868
  0.6 7.4 %copy-start.4 = (bf16[256,3072]{1,0:T(8,128)(2,1)S(1)}, bf16[256,3072]{1,0:T(8,128)(2,1)}, u32[]{:S(2)}) copy-start(bf16[256,3072]{1,0:T(8,128)(2,1)} %param.6) | copy-start | bytes 4718596
  2.8 22.3 %all-to-all-start = ((bf16[8,192,384]{2,1,0:T(8,128)(2,1)}), bf16[8,192,384]{2,1,0:T(8,128)(2,1)S(1)}, u32[]{:S(2)}, u32[]{:S(2)}) async-start(bf16[8,192,384]{2,1,0:T(8,128)(2,1)} %broadcast_in_dim.7), calls=%async_computation | async-start | bytes 2359296 | tf_op jit(solution)/shard_map/gather_w/all_to_all | solution.py:225
  25.1 6.2 %collective-permute-start = (bf16[8,192,384]{2,1,0:T(8,128)(2,1)S(1)}, bf16[8,192,384]{2,1,0:T(8,128)(2,1)S(1)}, u32[]{:S(2)}, u32[]{:S(2)}) collective-permute-start(bf16[8,192,384]{2,1,0:T(8,128)(2,1)S(1)} %all-to-all-done.own_ref), channel_id=1, source_target_pairs={{0,32},{32,0},{64,96},{96,64},{128,160},{160,128},{192,224},{224,1... | collective-permute-start | bytes 3538952 | tf_op jit(solution)/shard_map/gather_w/ppermute | solution.py:226
  30.7 0.8 copy-start
  30.7 0.8 copy-start.1
  30.7 0.8 copy-start.2
  35.7 28.0 %all-to-all-start.1 = ((bf16[4,1552,128]{2,1,0:T(8,128)(2,1)}), bf16[4,1552,128]{2,1,0:T(8,128)(2,1)S(1)}, u32[]{:S(2)}, u32[]{:S(2)}) async-start(bf16[4,1552,128]{2,1,0:T(8,128)(2,1)} %get-tuple-element.13), calls=%async_computation.1 | async-start | bytes 3178496 | tf_op jit(solution)/shard_map/input_gradient_near/all_to_all | solution.py:246
  41.8 1.4 %copy-start.3 = (bf16[3072,384]{1,0:T(8,128)(2,1)}, bf16[3072,384]{1,0:T(8,128)(2,1)S(1)}, u32[]{:S(2)}) copy-start(bf16[3072,384]{1,0:T(8,128)(2,1)S(1)} %convolution_convert_fusion) | copy-start | bytes 7077892
  43.3 5.1 %collective-permute-start.1 = (bf16[8,192,384]{2,1,0:T(8,128)(2,1)S(1)}, bf16[8,192,384]{2,1,0:T(8,128)(2,1)}, u32[]{:S(2)}, u32[]{:S(2)}) collective-permute-start(bf16[8,192,384]{2,1,0:T(8,128)(2,1)S(1)} %select_bitcast_fusion), channel_id=1, source_target_pairs={{0,32},{32,0},{64,96},{96,64},{128,160},{160,128},{192,224},{224,1... | collective-permute-start | bytes 3538952 | tf_op jit(solution)/shard_map/w_grad/ppermute | solution.py:252
  51.6 11.3 %collective-permute-start.2 = (bf16[2,192,384]{2,1,0:T(8,128)(2,1)S(1)}, bf16[2,192,384]{2,1,0:T(8,128)(2,1)S(1)}, u32[]{:S(2)}, u32[]{:S(2)}) collective-permute-start(bf16[2,192,384]{2,1,0:T(8,128)(2,1)S(1)} %get-tuple-element.22), channel_id=1, source_target_pairs={{0,128},{32,160},{64,192},{96,224},{128,256},{160,288},{192,320},{... | collective-permute-start | bytes 884744 | tf_op jit(solution)/shard_map/w_grad/ppermute | solution.py:257
  53.5 10.3 %collective-permute-start.3 = (bf16[2,192,384]{2,1,0:T(8,128)(2,1)S(1)}, bf16[2,192,384]{2,1,0:T(8,128)(2,1)S(1)}, u32[]{:S(2)}, u32[]{:S(2)}) collective-permute-start(bf16[2,192,384]{2,1,0:T(8,128)(2,1)S(1)} %get-tuple-element.21), channel_id=1, source_target_pairs={{0,384},{32,416},{64,448},{96,480},{128,0},{160,32},{192,64},{224,... | collective-permute-start | bytes 884744 | tf_op jit(solution)/shard_map/w_grad/ppermute | solution.py:257
  64.7 37.6 %all-to-all-start.2 = ((bf16[8,208,128]{2,1,0:T(8,128)(2,1)}), bf16[8,208,128]{2,1,0:T(8,128)(2,1)S(1)}, u32[]{:S(2)}, u32[]{:S(2)}) async-start(bf16[8,208,128]{2,1,0:T(8,128)(2,1)} %sum_over_near.1), calls=%async_computation.2 | async-start | bytes 851968 | tf_op jit(solution)/shard_map/sum_over_near/all_to_all | solution.py:265
  78.6 10.3 %collective-permute-start.4 = (bf16[2,192,384]{2,1,0:T(8,128)(2,1)}, bf16[2,192,384]{2,1,0:T(8,128)(2,1)S(1)}, u32[]{:S(2)}, u32[]{:S(2)}) collective-permute-start(bf16[2,192,384]{2,1,0:T(8,128)(2,1)} %get-tuple-element.20), channel_id=1, source_target_pairs={{0,256},{32,288},{64,320},{96,352},{128,384},{160,416},{192,448},{... | collective-permute-start | bytes 884744 | tf_op jit(solution)/shard_map/w_grad/ppermute | solution.py:257
  89.1 22.8 %collective-permute-start.5 = (bf16[192,384]{1,0:T(8,128)(2,1)S(1)}, bf16[192,384]{1,0:T(8,128)(2,1)S(1)}, u32[]{:S(2)}, u32[]{:S(2)}) collective-permute-start(bf16[192,384]{1,0:T(8,128)(2,1)S(1)} %fusion.7), channel_id=1, source_target_pairs={{0,64},{32,96},{64,0},{96,32},{128,192},{160,224},{192,128},{224,1... | collective-permute-start | bytes 442376 | tf_op jit(solution)/shard_map/w_grad_y/ppermute | solution.py:271
  103.1 14.7 %all-to-all-start.3 = ((f32[16,8,128]{2,1,0:T(8,128)}), f32[16,8,128]{2,1,0:T(8,128)S(1)}, u32[]{:S(2)}, u32[]{:S(2)}) async-start(f32[16,8,128]{2,1,0:T(8,128)} %get-tuple-element.17), calls=%async_computation.3 | async-start | bytes 131072 | tf_op jit(solution)/shard_map/gain_gradients/all_to_all | solution.py:283

commit v8 on v7

--- a/solution.py
+++ b/solution.py
@@ -136,11 +136,56 @@
             jax.ShapeDtypeStruct((8, hd), F32),
         ],
         scratch_shapes=[pltpu.VMEM((2 * blocks, w_rows, columns), BF)],
-        compiler_params=pltpu.CompilerParams(vmem_limit_bytes=48 * 2**20),
+        compiler_params=pltpu.CompilerParams(vmem_limit_bytes=20 * 2**20),
         cost_estimate=pl.CostEstimate(
             flops=1_400_000_000, bytes_accessed=9_000_000, transcendentals=65536
         ),
     )(core.reshape(1), x, own, other, grad, q_gain, k_gain)
+
+
+def term_of(x_ref, dqkv, at, w_rows):
+    columns = pl.ds(pl.multiple_of(2 * w_rows * at, 128), 2 * w_rows)
+    term = dot(x_ref[:, columns], dqkv, 0, 0)
+    return term[:w_rows], term[w_rows:]
+
+
+def send_kernel(core_ref, x_ref, dqkv_ref, send_ref):
+    dqkv = dqkv_ref[...]
+    for at in range(send_ref.shape[0]):
+        zero, one = term_of(x_ref, dqkv, at, send_ref.shape[1])
+        send_ref[at] = jnp.where(core_ref[0] == 0, one, zero).astype(BF)
+
+
+def chip_kernel(core_ref, x_at_ref, x_ref, dqkv_ref, got_ref, *out_refs):
+    dqkv = dqkv_ref[...]
+    for step, out_ref in enumerate(out_refs):
+        first = lax.rem(x_at_ref[0] + step, NX) * NYL
+        for y in range(NYL):
+            zero, one = term_of(x_ref, dqkv, first + y, out_ref.shape[1])
+            own = jnp.where(core_ref[0] == 0, zero, one)
+            out_ref[y] = (own + got_ref[first + y].astype(F32)).astype(BF)
+
+
+def w_grad_send(core, x, dqkv, shape):
+    vmem, smem = (pl.BlockSpec(memory_space=space) for space in (pltpu.VMEM, pltpu.SMEM))
+    return pl.pallas_call(
+        send_kernel,
+        in_specs=[smem, vmem, vmem],
+        out_specs=vmem,
+        out_shape=jax.ShapeDtypeStruct(shape, BF),
+        compiler_params=pltpu.CompilerParams(vmem_limit_bytes=12 * 2**20),
+    )(core.reshape(1), x, dqkv)
+
+
+def chip_sum(core, x_at, x, dqkv, got):
+    vmem, smem = (pl.BlockSpec(memory_space=space) for space in (pltpu.VMEM, pltpu.SMEM))
+    return pl.pallas_call(
+        chip_kernel,
+        in_specs=[smem, smem, vmem, vmem, vmem],
+        out_specs=[vmem] * NX,
+        out_shape=[jax.ShapeDtypeStruct((NYL,) + got.shape[1:], BF)] * NX,
+        compiler_params=pltpu.CompilerParams(vmem_limit_bytes=12 * 2**20),
+    )(core.reshape(1), x_at.reshape(1), x, dqkv, got)
 
 
 def near_kernel(near_ref, *refs):
@@ -167,7 +212,7 @@
         in_specs=[vmem] + [pl.BlockSpec(memory_space=pl.ANY)] * len(order),
         out_specs=vmem,
         out_shape=jax.ShapeDtypeStruct((blocks, chunk + 16, near.shape[2]), BF),
-        compiler_params=pltpu.CompilerParams(vmem_limit_bytes=24 * 2**20),
+        compiler_params=pltpu.CompilerParams(vmem_limit_bytes=8 * 2**20),
     )(near, *order)
 
 
@@ -206,7 +251,7 @@
             jax.ShapeDtypeStruct(xhat.shape, BF),
             jax.ShapeDtypeStruct((NX * NYL * NC,) + head_gains.shape, F32),
         ],
-        compiler_params=pltpu.CompilerParams(vmem_limit_bytes=24 * 2**20),
+        compiler_params=pltpu.CompilerParams(vmem_limit_bytes=8 * 2**20),
     )(far, xhat, gain, inverse, head_gains)
 
 
@@ -246,26 +291,17 @@
         near = lax.all_to_all(part, MP, 0, 0, axis_index_groups=NEAR, tiled=True)
 
     with jax.named_scope("w_grad"):
-        term = dot(normed, dqkv, 0, 0).astype(BF).reshape(NX * NYL, NC, w_rows, columns)
-        term_keep = jnp.where(core == 0, term[:, 0], term[:, 1])
-        term_send = jnp.where(core == 0, term[:, 1], term[:, 0])
-        term_got = lax.ppermute(term_send, DP, CORE_SWAP)
-        chip = (term_keep.astype(F32) + term_got.astype(F32)).astype(BF)
-        chip = chip.reshape(NX, NYL, w_rows, columns)
-        x_term = lax.dynamic_index_in_dim(chip, x_at, 0, False).astype(F32)
-        x_got = [
-            lax.ppermute(
-                lax.dynamic_index_in_dim(chip, (x_at + step) % NX, 0, False), DP, pairs
-            )
-            for step, pairs in enumerate(X_STEPS, 1)
-        ]
+        send = w_grad_send(core, normed, dqkv, (NX * NYL, w_rows, columns))
+        got = lax.ppermute(send, DP, CORE_SWAP)
+        x_term, *leaves = chip_sum(core, x_at, normed, dqkv, got)
+        x_got = [lax.ppermute(leaf, DP, pairs) for leaf, pairs in zip(leaves, X_STEPS)]
 
     with jax.named_scope("sum_over_near"):
         pair = sum_near(near, [x_got[0], x_got[2]])
         far = lax.all_to_all(pair, MP, 0, 0, axis_index_groups=FAR, tiled=True)
 
     with jax.named_scope("w_grad_y"):
-        x_term = x_term + sum(got.astype(F32) for got in x_got)
+        x_term = sum(got.astype(F32) for got in [x_term, *x_got])
         leaves = jnp.where(y_lo == 0, x_term[1], x_term[0]).astype(BF)
         stays = jnp.where(y_lo == 0, x_term[0], x_term[1])
         w_grad = (stays + lax.ppermute(leaves, DP, YLO_SWAP).astype(F32)).astype(BF)

time: 120 us -> 120 us (level)
  Pallas kernels: 5.9 us -> 9.03 us
  other arithmetic: 6.99 us -> 4.41 us
    pallas_call x0 -> x2, Pallas kernels: none -> 4.35 us  [the longest x1 2.3 us: chip_sum(): pl.pallas_call(chip_kernel, in_specs=[smem, smem, vmem, vmem, vmem], out_...]
    convert_element_type x1 -> x0, other arithmetic: 2.44 us -> none  [per_device(): chip = (term_keep.astype(F32) + term_got.astype(F32)).astype(BF)]
    unnamed x13 -> x21, local copies, waits for them, and re-layouts: 1.66 us -> 2.97 us
    pallas_call x1, Pallas kernels: 4.16 us -> 2.95 us  [run_head(): pl.pallas_call(head_kernel, in_specs=[pl.BlockSpec(memory_space=pltpu.SME...]
  transfers between devices with their start and end apart: 10 -> 10, of which waited for: 7 -> 7; matrix products, arithmetic and copies ran while one was open for 9% -> 5% of each run, Pallas kernels for 1% -> 4%
where the time goes in v8:
time: 120 us; the launch traced here: 119 us
  starting transfers between devices  51.4 us (43%)
  waiting for transfers between devices  46 us (38%)
  Pallas kernels  9.03 us (8%)
  local copies, waits for them, and re-layouts  7.47 us (6%)
  other arithmetic  4.41 us (4%)
    all_to_all x1, waiting for transfers between devices, per_device(): lax.all_to_all(copies, DP, 0, 0, axis_index_groups=SAME_CORE, tiled=True)  16.2 us
    all_to_all x1, starting transfers between devices, per_device(): far = lax.all_to_all(pair, MP, 0, 0, axis_index_groups=FAR, tiled=True)  13.9 us
    all_to_all x1, waiting for transfers between devices, per_device(): far = lax.all_to_all(pair, MP, 0, 0, axis_index_groups=FAR, tiled=True)  11.5 us
    ppermute x3, starting transfers between devices, per_device(): lax.ppermute(leaf, DP, pairs)  10.8 us
    ppermute x3, waiting for transfers between devices, per_device(): lax.ppermute(leaf, DP, pairs)  10.3 us
    all_to_all x1, starting transfers between devices, per_device(): summed = jnp.sum(lax.all_to_all(copies, DP, 0, 0, tiled=True), axis=0)  8.73 us
    all_to_all x1, waiting for transfers between devices, per_device(): summed = jnp.sum(lax.all_to_all(copies, DP, 0, 0, tiled=True), axis=0)  5.16 us
    all_to_all x1, starting transfers between devices, per_device(): near = lax.all_to_all(part, MP, 0, 0, axis_index_groups=NEAR, tiled=True)  5.07 us
  transfers between devices with their start and end apart: 10, of which 7 were waited for; matrix products, arithmetic and copies ran while one was open for 5% of the time, Pallas kernels for 4%

profile of v8, /device:TPU:33, one launch (start us, length us, event | category | flops | bytes accessed | tf_op | source)
XLA Modules:
  0.0 119.3 jit_solution(2070513029928686402)
XLA Ops:
  0.6 0.0 copy-start.9
  0.6 0.0 copy-start.8
  0.7 2.2 %broadcast_in_dim.7 = bf16[8,192,384]{2,1,0:T(8,128)(2,1)} broadcast(bf16[192,384]{1,0:T(8,128)(2,1)} %param.8), dimensions={1,2} | broadcast | bytes 1327104 | tf_op jit(solution)/shard_map/gather_w/broadcast_in_dim | solution.py:269
  2.8 5.0 %all-to-all-start = ((bf16[8,192,384]{2,1,0:T(8,128)(2,1)}), bf16[8,192,384]{2,1,0:T(8,128)(2,1)S(1)}, u32[]{:S(2)}, u32[]{:S(2)}) async-start(bf16[8,192,384]{2,1,0:T(8,128)(2,1)} %broadcast_in_dim.7), calls=%async_computation | async-start | bytes 2359296 | tf_op jit(solution)/shard_map/gather_w/all_to_all | solution.py:270
  7.9 0.0 copy-done.9
  7.9 0.1 pad.3.clone
  8.0 0.0 copy-done.8
  8.0 0.3 convert_reduce_fusion
  8.3 0.6 fusion.2
  8.9 16.2 %all-to-all-done.own_ref = bf16[8,192,384]{2,1,0:T(8,128)(2,1)S(1)} async-done(((bf16[8,192,384]{2,1,0:T(8,128)(2,1)}), bf16[8,192,384]{2,1,0:T(8,128)(2,1)S(1)}, u32[]{:S(2)}, u32[]{:S(2)}) %all-to-all-start) | async-done | bytes 1179680 | tf_op jit(solution)/shard_map/gather_w/all_to_all | solution.py:270
  25.1 3.5 %collective-permute-start = (bf16[8,192,384]{2,1,0:T(8,128)(2,1)S(1)}, bf16[8,192,384]{2,1,0:T(8,128)(2,1)S(1)}, u32[]{:S(2)}, u32[]{:S(2)}) collective-permute-start(bf16[8,192,384]{2,1,0:T(8,128)(2,1)S(1)} %all-to-all-done.own_ref), channel_id=1, source_target_pairs={{0,32},{32,0},{64,96},{96,64},{128,160},{160,128},{192,224},{224,1... | collective-permute-start | bytes 3538952 | tf_op jit(solution)/shard_map/gather_w/ppermute | solution.py:271
  28.6 2.1 %fusion.4.x_ref = bf16[256,3072]{1,0:T(8,128)(2,1)S(1)} fusion(bf16[256,3072]{1,0:T(8,128)(2,1)} %param.6, f32[3072]{0:T(1024)S(1)} %copy-done.9, f32[256]{0:T(256)S(1)} %add_rsqrt_fusion, f32[256]{0:T(256)S(1)} %broadcast_multiply_fusion), kind=kLoop, calls=%fused_computation.6 | loop fusion | flops 3932160 | bytes 3160064 | tf_op jit(solution)/shard_map/input_norm/convert_element_type | solution.py:278
  30.7 0.0 copy-start.5
  30.8 0.0 copy-start.6
  30.8 0.0 copy-start.7
  30.8 0.5 maximum_maximum_fusion.x_ref
  31.3 0.0 collective-permute-done.other_ref
  31.3 0.3 copy-done.5
  31.6 0.0 copy-done.6
  31.6 0.0 copy-done.7
  31.6 3.0 %head.1 = (bf16[256,128]{1,0:T(8,128)(2,1)}, bf16[256,384]{1,0:T(8,128)(2,1)S(1)}, bf16[4,1552,128]{2,1,0:T(8,128)(2,1)S(1)}, f32[8,128]{1,0:T(8,128)S(1)}) custom-call(s32[1]{0:T(128)} %bitcast.core_ref, bf16[272,3072]{1,0:T(8,128)(2,1)S(1)} %maximum_maximum_fusion.x_ref, bf16[8,192,384]{2,1,0:T(8,128)(2,1)S(1)} %all-to-all-done.own_ref, ...), custom_call_target="tpu_custom_call" | custom-call | flops 1400000000 | bytes 9000000 | tf_op jit(solution)/shard_map/head/pallas_call | solution.py:128
  34.5 0.0 copy-start
  34.5 1.2 copy-done
  35.7 5.1 %all-to-all-start.1 = ((bf16[4,1552,128]{2,1,0:T(8,128)(2,1)}), bf16[4,1552,128]{2,1,0:T(8,128)(2,1)S(1)}, u32[]{:S(2)}, u32[]{:S(2)}) async-start(bf16[4,1552,128]{2,1,0:T(8,128)(2,1)} %copy-done), calls=%async_computation.1 | async-start | bytes 3178496 | tf_op jit(solution)/shard_map/input_gradient_near/all_to_all | solution.py:291
  40.8 2.1 %w_grad.2 = bf16[8,192,384]{2,1,0:T(8,128)(2,1)} custom-call(s32[1]{0:T(128)} %bitcast.core_ref, bf16[256,3072]{1,0:T(8,128)(2,1)S(1)} %fusion.4.x_ref, bf16[256,384]{1,0:T(8,128)(2,1)S(1)} %get-tuple-element.18.dqkv_ref), custom_call_target="tpu_custom_call" | custom-call | tf_op jit(solution)/shard_map/w_grad/pallas_call | solution.py:171
  42.8 2.5 %collective-permute-start.1 = (bf16[8,192,384]{2,1,0:T(8,128)(2,1)}, bf16[8,192,384]{2,1,0:T(8,128)(2,1)}, u32[]{:S(2)}, u32[]{:S(2)}) collective-permute-start(bf16[8,192,384]{2,1,0:T(8,128)(2,1)} %w_grad.2), channel_id=1, source_target_pairs={{0,32},{32,0},{64,96},{96,64},{128,160},{160,128},{192,224},{224,1... | collective-permute-start | bytes 3538952 | tf_op jit(solution)/shard_map/w_grad/ppermute | solution.py:295
  45.3 2.8 %collective-permute-done.1.got_ref = bf16[8,192,384]{2,1,0:T(8,128)(2,1)} collective-permute-done((bf16[8,192,384]{2,1,0:T(8,128)(2,1)}, bf16[8,192,384]{2,1,0:T(8,128)(2,1)}, u32[]{:S(2)}, u32[]{:S(2)}) %collective-permute-start.1) | collective-permute-done | bytes 1179680 | tf_op jit(solution)/shard_map/w_grad/ppermute | solution.py:295
  48.1 2.3 %w_grad.3 = (bf16[2,192,384]{2,1,0:T(8,128)(2,1)S(1)}, bf16[2,192,384]{2,1,0:T(8,128)(2,1)S(1)}, bf16[2,192,384]{2,1,0:T(8,128)(2,1)S(1)}, bf16[2,192,384]{2,1,0:T(8,128)(2,1)S(1)}) custom-call(s32[1]{0:T(128)} %bitcast.core_ref, s32[1]{0:T(128)} %bitcast.1.x_at_ref, bf16[256,3072]{1,0:T(8,128)(2,1)S(1)} %fusion.4.x_ref, ...), custom_call_target="tpu_custom_call" | custom-call | tf_op jit(solution)/shard_map/w_grad/pallas_call | solution.py:182
  50.4 0.0 copy-start.1
  50.4 0.7 copy-done.1
  51.1 0.0 copy-start.3
  51.1 0.7 copy-done.3
  51.8 1.9 %collective-permute-start.2 = (bf16[2,192,384]{2,1,0:T(8,128)(2,1)S(1)}, bf16[2,192,384]{2,1,0:T(8,128)(2,1)S(1)}, u32[]{:S(2)}, u32[]{:S(2)}) collective-permute-start(bf16[2,192,384]{2,1,0:T(8,128)(2,1)S(1)} %get-tuple-element.19), channel_id=1, source_target_pairs={{0,128},{32,160},{64,192},{96,224},{128,256},{160,288},{192,320},{... | collective-permute-start | bytes 884744 | tf_op jit(solution)/shard_map/w_grad/ppermute | solution.py:297
  53.8 0.0 copy-start.4
  53.8 0.0 copy-start.2
  53.8 4.7 %collective-permute-start.3 = (bf16[2,192,384]{2,1,0:T(8,128)(2,1)S(1)}, bf16[2,192,384]{2,1,0:T(8,128)(2,1)S(1)}, u32[]{:S(2)}, u32[]{:S(2)}) collective-permute-start(bf16[2,192,384]{2,1,0:T(8,128)(2,1)S(1)} %get-tuple-element.20), channel_id=1, source_target_pairs={{0,384},{32,416},{64,448},{96,480},{128,0},{160,32},{192,64},{224,... | collective-permute-start | bytes 884744 | tf_op jit(solution)/shard_map/w_grad/ppermute | solution.py:297
  58.5 4.7 %collective-permute-done.2.refs_0_ = bf16[2,192,384]{2,1,0:T(8,128)(2,1)S(1)} collective-permute-done((bf16[2,192,384]{2,1,0:T(8,128)(2,1)S(1)}, bf16[2,192,384]{2,1,0:T(8,128)(2,1)S(1)}, u32[]{:S(2)}, u32[]{:S(2)}) %collective-permute-start.2) | collective-permute-done | bytes 294944 | tf_op jit(solution)/shard_map/w_grad/ppermute | solution.py:297
  63.2 1.0 collective-permute-done.3.refs_1_
  64.2 0.0 all-to-all-done.1.near_ref
  64.2 1.0 sum_over_near.1
  65.1 13.9 %all-to-all-start.2 = ((bf16[8,208,128]{2,1,0:T(8,128)(2,1)}), bf16[8,208,128]{2,1,0:T(8,128)(2,1)S(1)}, u32[]{:S(2)}, u32[]{:S(2)}) async-start(bf16[8,208,128]{2,1,0:T(8,128)(2,1)} %sum_over_near.1), calls=%async_computation.2 | async-start | bytes 851968 | tf_op jit(solution)/shard_map/sum_over_near/all_to_all | solution.py:301
  79.0 0.0 copy-done.4
  79.1 4.2 %collective-permute-start.4 = (bf16[2,192,384]{2,1,0:T(8,128)(2,1)S(1)}, bf16[2,192,384]{2,1,0:T(8,128)(2,1)S(1)}, u32[]{:S(2)}, u32[]{:S(2)}) collective-permute-start(bf16[2,192,384]{2,1,0:T(8,128)(2,1)S(1)} %copy-done.4), channel_id=1, source_target_pairs={{0,256},{32,288},{64,320},{96,352},{128,384},{160,416},{192,448},{... | collective-permute-start | bytes 884744 | tf_op jit(solution)/shard_map/w_grad/ppermute | solution.py:297
  83.3 1.0 constant_dynamic-slice_fusion
  84.3 0.1 copy.14
  84.4 0.1 dynamic-slice_bitcast_fusion
  84.4 0.1 copy.13.gain_ref
  84.5 4.6 %collective-permute-done.4 = bf16[2,192,384]{2,1,0:T(8,128)(2,1)S(1)} collective-permute-done((bf16[2,192,384]{2,1,0:T(8,128)(2,1)S(1)}, bf16[2,192,384]{2,1,0:T(8,128)(2,1)S(1)}, u32[]{:S(2)}, u32[]{:S(2)}) %collective-permute-start.4) | collective-permute-done | bytes 294944 | tf_op jit(solution)/shard_map/w_grad/ppermute | solution.py:297
  89.2 0.0 copy-done.2
  89.2 0.1 convert_add_fusion
  89.3 1.9 %collective-permute-start.5 = (bf16[192,384]{1,0:T(8,128)(2,1)S(1)}, bf16[192,384]{1,0:T(8,128)(2,1)S(1)}, u32[]{:S(2)}, u32[]{:S(2)}) collective-permute-start(bf16[192,384]{1,0:T(8,128)(2,1)S(1)} %fusion.6), channel_id=1, source_target_pairs={{0,64},{32,96},{64,0},{96,32},{128,192},{160,224},{192,128},{224,1... | collective-permute-start | bytes 442376 | tf_op jit(solution)/shard_map/w_grad_y/ppermute | solution.py:307
  91.3 11.5 %all-to-all-done.2.far_ref = bf16[8,208,128]{2,1,0:T(8,128)(2,1)S(1)} async-done(((bf16[8,208,128]{2,1,0:T(8,128)(2,1)}), bf16[8,208,128]{2,1,0:T(8,128)(2,1)S(1)}, u32[]{:S(2)}, u32[]{:S(2)}) %all-to-all-start.2) | async-done | bytes 426016 | tf_op jit(solution)/shard_map/sum_over_near/all_to_all | solution.py:301
  102.8 0.8 input_gradient.1
  103.6 8.7 %all-to-all-start.3 = ((f32[16,8,128]{2,1,0:T(8,128)}), f32[16,8,128]{2,1,0:T(8,128)S(1)}, u32[]{:S(2)}, u32[]{:S(2)}) async-start(f32[16,8,128]{2,1,0:T(8,128)} %get-tuple-element.23), calls=%async_computation.3 | async-start | bytes 131072 | tf_op jit(solution)/shard_map/gain_gradients/all_to_all | solution.py:319
  112.3 0.0 collective-permute-done.5
  112.3 0.7 fusion.5
  113.0 5.2 %all-to-all-done.3 = f32[16,8,128]{2,1,0:T(8,128)S(1)} async-done(((f32[16,8,128]{2,1,0:T(8,128)}), f32[16,8,128]{2,1,0:T(8,128)S(1)}, u32[]{:S(2)}, u32[]{:S(2)}) %all-to-all-start.3) | async-done | bytes 65568 | tf_op jit(solution)/shard_map/gain_gradients/all_to_all | solution.py:319
  118.2 0.5 fusion.7
  118.7 0.5 slice_bitcast_fusion
  (9 shorter events, 0.1 us)
Async XLA Ops:
  0.6 7.2 %copy-start.9 = (f32[3072]{0:T(1024)S(1)}, f32[3072]{0:T(1024)}, u32[]{:S(2)}) copy-start(f32[3072]{0:T(1024)} %param.7) | copy-start | bytes 36868
  0.6 7.4 %copy-start.8 = (bf16[256,3072]{1,0:T(8,128)(2,1)S(1)}, bf16[256,3072]{1,0:T(8,128)(2,1)}, u32[]{:S(2)}) copy-start(bf16[256,3072]{1,0:T(8,128)(2,1)} %param.6) | copy-start | bytes 4718596
  2.8 22.3 %all-to-all-start = ((bf16[8,192,384]{2,1,0:T(8,128)(2,1)}), bf16[8,192,384]{2,1,0:T(8,128)(2,1)S(1)}, u32[]{:S(2)}, u32[]{:S(2)}) async-start(bf16[8,192,384]{2,1,0:T(8,128)(2,1)} %broadcast_in_dim.7), calls=%async_computation | async-start | bytes 2359296 | tf_op jit(solution)/shard_map/gather_w/all_to_all | solution.py:270
  25.1 6.2 %collective-permute-start = (bf16[8,192,384]{2,1,0:T(8,128)(2,1)S(1)}, bf16[8,192,384]{2,1,0:T(8,128)(2,1)S(1)}, u32[]{:S(2)}, u32[]{:S(2)}) collective-permute-start(bf16[8,192,384]{2,1,0:T(8,128)(2,1)S(1)} %all-to-all-done.own_ref), channel_id=1, source_target_pairs={{0,32},{32,0},{64,96},{96,64},{128,160},{160,128},{192,224},{224,1... | collective-permute-start | bytes 3538952 | tf_op jit(solution)/shard_map/gather_w/ppermute | solution.py:271
  30.7 0.8 copy-start.5
  30.8 0.8 copy-start.6
  30.8 0.8 copy-start.7
  34.5 1.2 copy-start
  35.7 28.5 %all-to-all-start.1 = ((bf16[4,1552,128]{2,1,0:T(8,128)(2,1)}), bf16[4,1552,128]{2,1,0:T(8,128)(2,1)S(1)}, u32[]{:S(2)}, u32[]{:S(2)}) async-start(bf16[4,1552,128]{2,1,0:T(8,128)(2,1)} %copy-done), calls=%async_computation.1 | async-start | bytes 3178496 | tf_op jit(solution)/shard_map/input_gradient_near/all_to_all | solution.py:291
  42.8 5.3 %collective-permute-start.1 = (bf16[8,192,384]{2,1,0:T(8,128)(2,1)}, bf16[8,192,384]{2,1,0:T(8,128)(2,1)}, u32[]{:S(2)}, u32[]{:S(2)}) collective-permute-start(bf16[8,192,384]{2,1,0:T(8,128)(2,1)} %w_grad.2), channel_id=1, source_target_pairs={{0,32},{32,0},{64,96},{96,64},{128,160},{160,128},{192,224},{224,1... | collective-permute-start | bytes 3538952 | tf_op jit(solution)/shard_map/w_grad/ppermute | solution.py:295
  50.4 0.7 copy-start.1
  51.1 0.7 copy-start.3
  51.8 11.3 %collective-permute-start.2 = (bf16[2,192,384]{2,1,0:T(8,128)(2,1)S(1)}, bf16[2,192,384]{2,1,0:T(8,128)(2,1)S(1)}, u32[]{:S(2)}, u32[]{:S(2)}) collective-permute-start(bf16[2,192,384]{2,1,0:T(8,128)(2,1)S(1)} %get-tuple-element.19), channel_id=1, source_target_pairs={{0,128},{32,160},{64,192},{96,224},{128,256},{160,288},{192,320},{... | collective-permute-start | bytes 884744 | tf_op jit(solution)/shard_map/w_grad/ppermute | solution.py:297
  53.8 25.3 %copy-start.4 = (bf16[2,192,384]{2,1,0:T(8,128)(2,1)S(1)}, bf16[2,192,384]{2,1,0:T(8,128)(2,1)}, u32[]{:S(2)}) copy-start(bf16[2,192,384]{2,1,0:T(8,128)(2,1)} %copy-done.3) | copy-start | bytes 884740
  53.8 35.4 %copy-start.2 = (bf16[2,192,384]{2,1,0:T(8,128)(2,1)S(1)}, bf16[2,192,384]{2,1,0:T(8,128)(2,1)}, u32[]{:S(2)}) copy-start(bf16[2,192,384]{2,1,0:T(8,128)(2,1)} %copy-done.1) | copy-start | bytes 884740
  53.8 10.4 %collective-permute-start.3 = (bf16[2,192,384]{2,1,0:T(8,128)(2,1)S(1)}, bf16[2,192,384]{2,1,0:T(8,128)(2,1)S(1)}, u32[]{:S(2)}, u32[]{:S(2)}) collective-permute-start(bf16[2,192,384]{2,1,0:T(8,128)(2,1)S(1)} %get-tuple-element.20), channel_id=1, source_target_pairs={{0,384},{32,416},{64,448},{96,480},{128,0},{160,32},{192,64},{224,... | collective-permute-start | bytes 884744 | tf_op jit(solution)/shard_map/w_grad/ppermute | solution.py:297
  65.1 37.7 %all-to-all-start.2 = ((bf16[8,208,128]{2,1,0:T(8,128)(2,1)}), bf16[8,208,128]{2,1,0:T(8,128)(2,1)S(1)}, u32[]{:S(2)}, u32[]{:S(2)}) async-start(bf16[8,208,128]{2,1,0:T(8,128)(2,1)} %sum_over_near.1), calls=%async_computation.2 | async-start | bytes 851968 | tf_op jit(solution)/shard_map/sum_over_near/all_to_all | solution.py:301
  79.1 10.1 %collective-permute-start.4 = (bf16[2,192,384]{2,1,0:T(8,128)(2,1)S(1)}, bf16[2,192,384]{2,1,0:T(8,128)(2,1)S(1)}, u32[]{:S(2)}, u32[]{:S(2)}) collective-permute-start(bf16[2,192,384]{2,1,0:T(8,128)(2,1)S(1)} %copy-done.4), channel_id=1, source_target_pairs={{0,256},{32,288},{64,320},{96,352},{128,384},{160,416},{192,448},{... | collective-permute-start | bytes 884744 | tf_op jit(solution)/shard_map/w_grad/ppermute | solution.py:297
  89.3 23.0 %collective-permute-start.5 = (bf16[192,384]{1,0:T(8,128)(2,1)S(1)}, bf16[192,384]{1,0:T(8,128)(2,1)S(1)}, u32[]{:S(2)}, u32[]{:S(2)}) collective-permute-start(bf16[192,384]{1,0:T(8,128)(2,1)S(1)} %fusion.6), channel_id=1, source_target_pairs={{0,64},{32,96},{64,0},{96,32},{128,192},{160,224},{192,128},{224,1... | collective-permute-start | bytes 442376 | tf_op jit(solution)/shard_map/w_grad_y/ppermute | solution.py:307
  103.6 14.6 %all-to-all-start.3 = ((f32[16,8,128]{2,1,0:T(8,128)}), f32[16,8,128]{2,1,0:T(8,128)S(1)}, u32[]{:S(2)}, u32[]{:S(2)}) async-start(f32[16,8,128]{2,1,0:T(8,128)} %get-tuple-element.23), calls=%async_computation.3 | async-start | bytes 131072 | tf_op jit(solution)/shard_map/gain_gradients/all_to_all | solution.py:319

commit v9 on v7

--- a/solution.py
+++ b/solution.py
@@ -261,7 +261,7 @@
         ]
 
     with jax.named_scope("sum_over_near"):
-        pair = sum_near(near, [x_got[0], x_got[2]])
+        pair = sum_near(near, [x_got[0]])
         far = lax.all_to_all(pair, MP, 0, 0, axis_index_groups=FAR, tiled=True)
 
     with jax.named_scope("w_grad_y"):

time: 120 us -> 117 us (0.975)
  starting transfers between devices: 51.4 us -> 46 us
  waiting for transfers between devices: 45.7 us -> 47.4 us
    ppermute x3, waiting for transfers between devices: 10.5 us -> 17 us  [per_device(): lax.ppermute(lax.dynamic_index_in_dim(chip, (x_at + step) % NX, 0, False)...]
    all_to_all x1, waiting for transfers between devices: 11.3 us -> 6.36 us  [per_device(): far = lax.all_to_all(pair, MP, 0, 0, axis_index_groups=FAR, tiled=True)]
    ppermute x3, starting transfers between devices: 10.6 us -> 7.02 us  [per_device(): lax.ppermute(lax.dynamic_index_in_dim(chip, (x_at + step) % NX, 0, False)...]
    all_to_all x1, starting transfers between devices: 8.8 us -> 6.88 us  [per_device(): summed = jnp.sum(lax.all_to_all(copies, DP, 0, 0, tiled=True), axis=0)]
  transfers between devices with their start and end apart: 10 -> 10, of which waited for: 7 -> 7; matrix products, arithmetic and copies ran while one was open for 9% -> 10% of each run, Pallas kernels for 1% -> 1%
where the time goes in v9:
time: 117 us; the launch traced here: 116 us
  waiting for transfers between devices  47.4 us (41%)
  starting transfers between devices  46 us (39%)
  other arithmetic  7.97 us (7%)
  local copies, waits for them, and re-layouts  6.96 us (6%)
  Pallas kernels  5.9 us (5%)
    ppermute x3, waiting for transfers between devices, per_device(): lax.ppermute(lax.dynamic_index_in_dim(chip, (x_at + step) % NX, 0, False)...  17 us
    all_to_all x1, waiting for transfers between devices, per_device(): lax.all_to_all(copies, DP, 0, 0, axis_index_groups=SAME_CORE, tiled=True)  16.2 us
    all_to_all x1, starting transfers between devices, per_device(): far = lax.all_to_all(pair, MP, 0, 0, axis_index_groups=FAR, tiled=True)  13.9 us
    ppermute x3, starting transfers between devices, per_device(): lax.ppermute(lax.dynamic_index_in_dim(chip, (x_at + step) % NX, 0, False)...  7.02 us
    all_to_all x1, starting transfers between devices, per_device(): summed = jnp.sum(lax.all_to_all(copies, DP, 0, 0, tiled=True), axis=0)  6.88 us
    all_to_all x1, waiting for transfers between devices, per_device(): far = lax.all_to_all(pair, MP, 0, 0, axis_index_groups=FAR, tiled=True)  6.36 us
    all_to_all x1, waiting for transfers between devices, per_device(): summed = jnp.sum(lax.all_to_all(copies, DP, 0, 0, tiled=True), axis=0)  5.21 us
    all_to_all x1, starting transfers between devices, per_device(): near = lax.all_to_all(part, MP, 0, 0, axis_index_groups=NEAR, tiled=True)  5.07 us
  transfers between devices with their start and end apart: 10, of which 7 were waited for; matrix products, arithmetic and copies ran while one was open for 10% of the time, Pallas kernels for 1%

profile of v9, /device:TPU:33, one launch (start us, length us, event | category | flops | bytes accessed | tf_op | source)
XLA Modules:
  0.0 116.2 jit_solution(3738644056886621547)
XLA Ops:
  0.6 0.0 copy-start.5
  0.6 0.0 copy-start.4
  0.7 2.2 %broadcast_in_dim.7 = bf16[8,192,384]{2,1,0:T(8,128)(2,1)} broadcast(bf16[192,384]{1,0:T(8,128)(2,1)} %param.8), dimensions={1,2} | broadcast | bytes 1327104 | tf_op jit(solution)/shard_map/gather_w/broadcast_in_dim | solution.py:224
  2.8 5.0 %all-to-all-start = ((bf16[8,192,384]{2,1,0:T(8,128)(2,1)}), bf16[8,192,384]{2,1,0:T(8,128)(2,1)S(1)}, u32[]{:S(2)}, u32[]{:S(2)}) async-start(bf16[8,192,384]{2,1,0:T(8,128)(2,1)} %broadcast_in_dim.7), calls=%async_computation | async-start | bytes 2359296 | tf_op jit(solution)/shard_map/gather_w/all_to_all | solution.py:225
  7.8 0.0 copy-done.5
  7.9 0.1 pad.3.clone
  8.0 0.0 copy-done.4
  8.0 0.3 convert_reduce_fusion
  8.3 0.6 fusion.2
  8.9 16.2 %all-to-all-done.own_ref = bf16[8,192,384]{2,1,0:T(8,128)(2,1)S(1)} async-done(((bf16[8,192,384]{2,1,0:T(8,128)(2,1)}), bf16[8,192,384]{2,1,0:T(8,128)(2,1)S(1)}, u32[]{:S(2)}, u32[]{:S(2)}) %all-to-all-start) | async-done | bytes 1179680 | tf_op jit(solution)/shard_map/gather_w/all_to_all | solution.py:225
  25.1 3.5 %collective-permute-start = (bf16[8,192,384]{2,1,0:T(8,128)(2,1)S(1)}, bf16[8,192,384]{2,1,0:T(8,128)(2,1)S(1)}, u32[]{:S(2)}, u32[]{:S(2)}) collective-permute-start(bf16[8,192,384]{2,1,0:T(8,128)(2,1)S(1)} %all-to-all-done.own_ref), channel_id=1, source_target_pairs={{0,32},{32,0},{64,96},{96,64},{128,160},{160,128},{192,224},{224,1... | collective-permute-start | bytes 3538952 | tf_op jit(solution)/shard_map/gather_w/ppermute | solution.py:226
  28.6 2.1 %fusion.4 = bf16[256,3072]{1,0:T(8,128)(2,1)S(1)} fusion(bf16[256,3072]{1,0:T(8,128)(2,1)} %param.6, f32[3072]{0:T(1024)S(1)} %copy-done.5, f32[256]{0:T(256)S(1)} %add_rsqrt_fusion, f32[256]{0:T(256)S(1)} %broadcast_multiply_fusion), kind=kLoop, calls=%fused_computation.7 | loop fusion | flops 3932160 | bytes 3160064 | tf_op jit(solution)/shard_map/input_norm/convert_element_type | solution.py:233
  30.7 0.0 copy-start
  30.7 0.0 copy-start.1
  30.7 0.0 copy-start.2
  30.8 0.5 maximum_maximum_fusion.x_ref
  31.3 0.0 collective-permute-done.other_ref
  31.3 0.2 copy-done
  31.6 0.0 copy-done.1
  31.6 0.0 copy-done.2
  31.6 4.2 %head.1 = (bf16[256,128]{1,0:T(8,128)(2,1)}, bf16[256,384]{1,0:T(8,128)(2,1)S(1)}, bf16[4,1552,128]{2,1,0:T(8,128)(2,1)}, f32[8,128]{1,0:T(8,128)S(1)}) custom-call(s32[1]{0:T(128)} %bitcast.core_ref, bf16[272,3072]{1,0:T(8,128)(2,1)S(1)} %maximum_maximum_fusion.x_ref, bf16[8,192,384]{2,1,0:T(8,128)(2,1)S(1)} %all-to-all-done.own_ref, ...), custom_call_target="tpu_custom_call" | custom-call | flops 1400000000 | bytes 9000000 | tf_op jit(solution)/shard_map/head/pallas_call | solution.py:128
  35.7 5.1 %all-to-all-start.1 = ((bf16[4,1552,128]{2,1,0:T(8,128)(2,1)}), bf16[4,1552,128]{2,1,0:T(8,128)(2,1)S(1)}, u32[]{:S(2)}, u32[]{:S(2)}) async-start(bf16[4,1552,128]{2,1,0:T(8,128)(2,1)} %get-tuple-element.13), calls=%async_computation.1 | async-start | bytes 3178496 | tf_op jit(solution)/shard_map/input_gradient_near/all_to_all | solution.py:246
  40.8 1.0 convolution_convert_fusion
  41.8 0.0 copy-start.3
  41.8 0.1 select_bitcast_fusion
  42.0 1.3 %copy-done.3 = bf16[3072,384]{1,0:T(8,128)(2,1)} copy-done((bf16[3072,384]{1,0:T(8,128)(2,1)}, bf16[3072,384]{1,0:T(8,128)(2,1)S(1)}, u32[]{:S(2)}) %copy-start.3) | copy-done | bytes 2359320
  43.3 2.5 %collective-permute-start.1 = (bf16[8,192,384]{2,1,0:T(8,128)(2,1)S(1)}, bf16[8,192,384]{2,1,0:T(8,128)(2,1)}, u32[]{:S(2)}, u32[]{:S(2)}) collective-permute-start(bf16[8,192,384]{2,1,0:T(8,128)(2,1)S(1)} %select_bitcast_fusion), channel_id=1, source_target_pairs={{0,32},{32,0},{64,96},{96,64},{128,160},{160,128},{192,224},{224,1... | collective-permute-start | bytes 3538952 | tf_op jit(solution)/shard_map/w_grad/ppermute | solution.py:252
  45.8 2.5 %collective-permute-done.1 = bf16[8,192,384]{2,1,0:T(8,128)(2,1)} collective-permute-done((bf16[8,192,384]{2,1,0:T(8,128)(2,1)S(1)}, bf16[8,192,384]{2,1,0:T(8,128)(2,1)}, u32[]{:S(2)}, u32[]{:S(2)}) %collective-permute-start.1) | collective-permute-done | bytes 1179680 | tf_op jit(solution)/shard_map/w_grad/ppermute | solution.py:252
  48.3 2.4 %fusion.5 = bf16[8,192,384]{2,1,0:T(8,128)(2,1)S(1)} fusion(bf16[8,192,384]{2,1,0:T(8,128)(2,1)} %collective-permute-done.1, pred[]{:T(512)S(6)} %eq.14, bf16[8,2,192,384]{3,2,1,0:T(8,128)(2,1)} %bitcast.47), kind=kLoop, calls=%fused_computation.9 | loop fusion | flops 2949120 | bytes 4718593 | tf_op jit(solution)/shard_map/w_grad/convert_element_type | solution.py:253
  50.8 0.8 dynamic-slice_bitcast_fusion.1
  51.6 1.9 %collective-permute-start.2 = (bf16[2,192,384]{2,1,0:T(8,128)(2,1)S(1)}, bf16[2,192,384]{2,1,0:T(8,128)(2,1)S(1)}, u32[]{:S(2)}, u32[]{:S(2)}) collective-permute-start(bf16[2,192,384]{2,1,0:T(8,128)(2,1)S(1)} %get-tuple-element.22), channel_id=1, source_target_pairs={{0,128},{32,160},{64,192},{96,224},{128,256},{160,288},{192,320},{... | collective-permute-start | bytes 884744 | tf_op jit(solution)/shard_map/w_grad/ppermute | solution.py:257
  53.5 9.4 %collective-permute-done.2.refs_0_ = bf16[2,192,384]{2,1,0:T(8,128)(2,1)S(1)} collective-permute-done((bf16[2,192,384]{2,1,0:T(8,128)(2,1)S(1)}, bf16[2,192,384]{2,1,0:T(8,128)(2,1)S(1)}, u32[]{:S(2)}, u32[]{:S(2)}) %collective-permute-start.2) | collective-permute-done | bytes 294944 | tf_op jit(solution)/shard_map/w_grad/ppermute | solution.py:257
  62.9 0.0 all-to-all-done.1.near_ref
  62.9 1.0 sum_over_near.1
  63.9 13.9 %all-to-all-start.2 = ((bf16[8,208,128]{2,1,0:T(8,128)(2,1)}), bf16[8,208,128]{2,1,0:T(8,128)(2,1)S(1)}, u32[]{:S(2)}, u32[]{:S(2)}) async-start(bf16[8,208,128]{2,1,0:T(8,128)(2,1)} %sum_over_near.1), calls=%async_computation.2 | async-start | bytes 851968 | tf_op jit(solution)/shard_map/sum_over_near/all_to_all | solution.py:265
  77.8 1.9 %collective-permute-start.3 = (bf16[2,192,384]{2,1,0:T(8,128)(2,1)}, bf16[2,192,384]{2,1,0:T(8,128)(2,1)S(1)}, u32[]{:S(2)}, u32[]{:S(2)}) collective-permute-start(bf16[2,192,384]{2,1,0:T(8,128)(2,1)} %get-tuple-element.20), channel_id=1, source_target_pairs={{0,256},{32,288},{64,320},{96,352},{128,384},{160,416},{192,448},{... | collective-permute-start | bytes 884744 | tf_op jit(solution)/shard_map/w_grad/ppermute | solution.py:257
  79.7 3.2 %collective-permute-start.4 = (bf16[2,192,384]{2,1,0:T(8,128)(2,1)S(1)}, bf16[2,192,384]{2,1,0:T(8,128)(2,1)}, u32[]{:S(2)}, u32[]{:S(2)}) collective-permute-start(bf16[2,192,384]{2,1,0:T(8,128)(2,1)S(1)} %get-tuple-element.21), channel_id=1, source_target_pairs={{0,384},{32,416},{64,448},{96,480},{128,0},{160,32},{192,64},{224,... | collective-permute-start | bytes 884744 | tf_op jit(solution)/shard_map/w_grad/ppermute | solution.py:257
  82.9 1.0 constant_dynamic-slice_fusion
  83.9 0.1 copy.18
  84.0 0.1 dynamic-slice_bitcast_fusion.3
  84.1 0.1 copy.15.gain_ref
  84.2 4.2 %collective-permute-done.3 = bf16[2,192,384]{2,1,0:T(8,128)(2,1)S(1)} collective-permute-done((bf16[2,192,384]{2,1,0:T(8,128)(2,1)}, bf16[2,192,384]{2,1,0:T(8,128)(2,1)S(1)}, u32[]{:S(2)}, u32[]{:S(2)}) %collective-permute-start.3) | collective-permute-done | bytes 294944 | tf_op jit(solution)/shard_map/w_grad/ppermute | solution.py:257
  88.4 3.5 %collective-permute-done.4 = bf16[2,192,384]{2,1,0:T(8,128)(2,1)} collective-permute-done((bf16[2,192,384]{2,1,0:T(8,128)(2,1)S(1)}, bf16[2,192,384]{2,1,0:T(8,128)(2,1)}, u32[]{:S(2)}, u32[]{:S(2)}) %collective-permute-start.4) | collective-permute-done | bytes 294944 | tf_op jit(solution)/shard_map/w_grad/ppermute | solution.py:257
  91.9 1.1 convert_add_fusion.1
  93.0 2.1 %collective-permute-start.5 = (bf16[192,384]{1,0:T(8,128)(2,1)S(1)}, bf16[192,384]{1,0:T(8,128)(2,1)S(1)}, u32[]{:S(2)}, u32[]{:S(2)}) collective-permute-start(bf16[192,384]{1,0:T(8,128)(2,1)S(1)} %fusion.7), channel_id=1, source_target_pairs={{0,64},{32,96},{64,0},{96,32},{128,192},{160,224},{192,128},{224,1... | collective-permute-start | bytes 442376 | tf_op jit(solution)/shard_map/w_grad_y/ppermute | solution.py:271
  95.2 6.4 %all-to-all-done.2.far_ref = bf16[8,208,128]{2,1,0:T(8,128)(2,1)S(1)} async-done(((bf16[8,208,128]{2,1,0:T(8,128)(2,1)}), bf16[8,208,128]{2,1,0:T(8,128)(2,1)S(1)}, u32[]{:S(2)}, u32[]{:S(2)}) %all-to-all-start.2) | async-done | bytes 426016 | tf_op jit(solution)/shard_map/sum_over_near/all_to_all | solution.py:265
  101.5 0.8 input_gradient.1
  102.3 6.9 %all-to-all-start.3 = ((f32[16,8,128]{2,1,0:T(8,128)}), f32[16,8,128]{2,1,0:T(8,128)S(1)}, u32[]{:S(2)}, u32[]{:S(2)}) async-start(f32[16,8,128]{2,1,0:T(8,128)} %get-tuple-element.17), calls=%async_computation.3 | async-start | bytes 131072 | tf_op jit(solution)/shard_map/gain_gradients/all_to_all | solution.py:283
  109.2 0.0 collective-permute-done.5
  109.2 0.7 fusion.6
  109.9 5.2 %all-to-all-done.3 = f32[16,8,128]{2,1,0:T(8,128)S(1)} async-done(((f32[16,8,128]{2,1,0:T(8,128)}), f32[16,8,128]{2,1,0:T(8,128)S(1)}, u32[]{:S(2)}, u32[]{:S(2)}) %all-to-all-start.3) | async-done | bytes 65568 | tf_op jit(solution)/shard_map/gain_gradients/all_to_all | solution.py:283
  115.1 0.5 fusion.8
  115.7 0.5 slice_bitcast_fusion.2
  (9 shorter events, 0.1 us)
Async XLA Ops:
  0.6 7.2 %copy-start.5 = (f32[3072]{0:T(1024)S(1)}, f32[3072]{0:T(1024)}, u32[]{:S(2)}) copy-start(f32[3072]{0:T(1024)} %param.7) | copy-start | bytes 36868
  0.6 7.4 %copy-start.4 = (bf16[256,3072]{1,0:T(8,128)(2,1)S(1)}, bf16[256,3072]{1,0:T(8,128)(2,1)}, u32[]{:S(2)}) copy-start(bf16[256,3072]{1,0:T(8,128)(2,1)} %param.6) | copy-start | bytes 4718596
  2.8 22.3 %all-to-all-start = ((bf16[8,192,384]{2,1,0:T(8,128)(2,1)}), bf16[8,192,384]{2,1,0:T(8,128)(2,1)S(1)}, u32[]{:S(2)}, u32[]{:S(2)}) async-start(bf16[8,192,384]{2,1,0:T(8,128)(2,1)} %broadcast_in_dim.7), calls=%async_computation | async-start | bytes 2359296 | tf_op jit(solution)/shard_map/gather_w/all_to_all | solution.py:225
  25.1 6.2 %collective-permute-start = (bf16[8,192,384]{2,1,0:T(8,128)(2,1)S(1)}, bf16[8,192,384]{2,1,0:T(8,128)(2,1)S(1)}, u32[]{:S(2)}, u32[]{:S(2)}) collective-permute-start(bf16[8,192,384]{2,1,0:T(8,128)(2,1)S(1)} %all-to-all-done.own_ref), channel_id=1, source_target_pairs={{0,32},{32,0},{64,96},{96,64},{128,160},{160,128},{192,224},{224,1... | collective-permute-start | bytes 3538952 | tf_op jit(solution)/shard_map/gather_w/ppermute | solution.py:226
  30.7 0.8 copy-start
  30.7 0.8 copy-start.1
  30.7 0.8 copy-start.2
  35.7 27.2 %all-to-all-start.1 = ((bf16[4,1552,128]{2,1,0:T(8,128)(2,1)}), bf16[4,1552,128]{2,1,0:T(8,128)(2,1)S(1)}, u32[]{:S(2)}, u32[]{:S(2)}) async-start(bf16[4,1552,128]{2,1,0:T(8,128)(2,1)} %get-tuple-element.13), calls=%async_computation.1 | async-start | bytes 3178496 | tf_op jit(solution)/shard_map/input_gradient_near/all_to_all | solution.py:246
  41.8 1.4 %copy-start.3 = (bf16[3072,384]{1,0:T(8,128)(2,1)}, bf16[3072,384]{1,0:T(8,128)(2,1)S(1)}, u32[]{:S(2)}) copy-start(bf16[3072,384]{1,0:T(8,128)(2,1)S(1)} %convolution_convert_fusion) | copy-start | bytes 7077892
  43.3 5.1 %collective-permute-start.1 = (bf16[8,192,384]{2,1,0:T(8,128)(2,1)S(1)}, bf16[8,192,384]{2,1,0:T(8,128)(2,1)}, u32[]{:S(2)}, u32[]{:S(2)}) collective-permute-start(bf16[8,192,384]{2,1,0:T(8,128)(2,1)S(1)} %select_bitcast_fusion), channel_id=1, source_target_pairs={{0,32},{32,0},{64,96},{96,64},{128,160},{160,128},{192,224},{224,1... | collective-permute-start | bytes 3538952 | tf_op jit(solution)/shard_map/w_grad/ppermute | solution.py:252
  51.6 11.3 %collective-permute-start.2 = (bf16[2,192,384]{2,1,0:T(8,128)(2,1)S(1)}, bf16[2,192,384]{2,1,0:T(8,128)(2,1)S(1)}, u32[]{:S(2)}, u32[]{:S(2)}) collective-permute-start(bf16[2,192,384]{2,1,0:T(8,128)(2,1)S(1)} %get-tuple-element.22), channel_id=1, source_target_pairs={{0,128},{32,160},{64,192},{96,224},{128,256},{160,288},{192,320},{... | collective-permute-start | bytes 884744 | tf_op jit(solution)/shard_map/w_grad/ppermute | solution.py:257
  63.9 37.7 %all-to-all-start.2 = ((bf16[8,208,128]{2,1,0:T(8,128)(2,1)}), bf16[8,208,128]{2,1,0:T(8,128)(2,1)S(1)}, u32[]{:S(2)}, u32[]{:S(2)}) async-start(bf16[8,208,128]{2,1,0:T(8,128)(2,1)} %sum_over_near.1), calls=%async_computation.2 | async-start | bytes 851968 | tf_op jit(solution)/shard_map/sum_over_near/all_to_all | solution.py:265
  77.8 10.6 %collective-permute-start.3 = (bf16[2,192,384]{2,1,0:T(8,128)(2,1)}, bf16[2,192,384]{2,1,0:T(8,128)(2,1)S(1)}, u32[]{:S(2)}, u32[]{:S(2)}) collective-permute-start(bf16[2,192,384]{2,1,0:T(8,128)(2,1)} %get-tuple-element.20), channel_id=1, source_target_pairs={{0,256},{32,288},{64,320},{96,352},{128,384},{160,416},{192,448},{... | collective-permute-start | bytes 884744 | tf_op jit(solution)/shard_map/w_grad/ppermute | solution.py:257
  79.7 12.2 %collective-permute-start.4 = (bf16[2,192,384]{2,1,0:T(8,128)(2,1)S(1)}, bf16[2,192,384]{2,1,0:T(8,128)(2,1)}, u32[]{:S(2)}, u32[]{:S(2)}) collective-permute-start(bf16[2,192,384]{2,1,0:T(8,128)(2,1)S(1)} %get-tuple-element.21), channel_id=1, source_target_pairs={{0,384},{32,416},{64,448},{96,480},{128,0},{160,32},{192,64},{224,... | collective-permute-start | bytes 884744 | tf_op jit(solution)/shard_map/w_grad/ppermute | solution.py:257
  93.0 16.1 %collective-permute-start.5 = (bf16[192,384]{1,0:T(8,128)(2,1)S(1)}, bf16[192,384]{1,0:T(8,128)(2,1)S(1)}, u32[]{:S(2)}, u32[]{:S(2)}) collective-permute-start(bf16[192,384]{1,0:T(8,128)(2,1)S(1)} %fusion.7), channel_id=1, source_target_pairs={{0,64},{32,96},{64,0},{96,32},{128,192},{160,224},{192,128},{224,1... | collective-permute-start | bytes 442376 | tf_op jit(solution)/shard_map/w_grad_y/ppermute | solution.py:271
  102.3 12.8 %all-to-all-start.3 = ((f32[16,8,128]{2,1,0:T(8,128)}), f32[16,8,128]{2,1,0:T(8,128)S(1)}, u32[]{:S(2)}, u32[]{:S(2)}) async-start(f32[16,8,128]{2,1,0:T(8,128)} %get-tuple-element.17), calls=%async_computation.3 | async-start | bytes 131072 | tf_op jit(solution)/shard_map/gain_gradients/all_to_all | solution.py:283

commit v10 on v9

--- a/solution.py
+++ b/solution.py
@@ -261,7 +261,7 @@
         ]
 
     with jax.named_scope("sum_over_near"):
-        pair = sum_near(near, [x_got[0]])
+        pair = sum_near(near, [chip])
         far = lax.all_to_all(pair, MP, 0, 0, axis_index_groups=FAR, tiled=True)
 
     with jax.named_scope("w_grad_y"):

time: 117 us -> 117 us (level)
  waiting for transfers between devices: 47.4 us -> 49.8 us
  other arithmetic: 7.97 us -> 5.98 us
  local copies, waits for them, and re-layouts: 6.96 us -> 5.26 us
    all_to_all x1, waiting for transfers between devices: 0.01 us -> 14.5 us  [per_device(): near = lax.all_to_all(part, MP, 0, 0, axis_index_groups=NEAR, tiled=True)]
    ppermute x3, waiting for transfers between devices: 17 us -> 10.1 us  [per_device(): lax.ppermute(lax.dynamic_index_in_dim(chip, (x_at + step) % NX, 0, False)...]
    all_to_all x1, waiting for transfers between devices: 6.36 us -> 1.36 us  [per_device(): far = lax.all_to_all(pair, MP, 0, 0, axis_index_groups=FAR, tiled=True)]
    convert_element_type x1, other arithmetic: 2.44 us -> 0.47 us  [per_device(): chip = (term_keep.astype(F32) + term_got.astype(F32)).astype(BF)]
    ppermute x3, starting transfers between devices: 7.02 us -> 8.41 us  [per_device(): lax.ppermute(lax.dynamic_index_in_dim(chip, (x_at + step) % NX, 0, False)...]
  transfers between devices with their start and end apart: 10 -> 10, of which waited for: 7 -> 7; matrix products, arithmetic and copies ran while one was open for 10% -> 7% of each run, Pallas kernels for 1% -> 1%
where the time goes in v10:
time: 117 us; the launch traced here: 116 us
  waiting for transfers between devices  49.8 us (43%)
  starting transfers between devices  47 us (40%)
  other arithmetic  5.98 us (5%)
  Pallas kernels  5.87 us (5%)
  local copies, waits for them, and re-layouts  5.26 us (4%)
    all_to_all x1, waiting for transfers between devices, per_device(): lax.all_to_all(copies, DP, 0, 0, axis_index_groups=SAME_CORE, tiled=True)  16.2 us
    all_to_all x1, waiting for transfers between devices, per_device(): near = lax.all_to_all(part, MP, 0, 0, axis_index_groups=NEAR, tiled=True)  14.5 us
    all_to_all x1, starting transfers between devices, per_device(): far = lax.all_to_all(pair, MP, 0, 0, axis_index_groups=FAR, tiled=True)  13.9 us
    ppermute x3, waiting for transfers between devices, per_device(): lax.ppermute(lax.dynamic_index_in_dim(chip, (x_at + step) % NX, 0, False)...  10.1 us
    ppermute x3, starting transfers between devices, per_device(): lax.ppermute(lax.dynamic_index_in_dim(chip, (x_at + step) % NX, 0, False)...  8.41 us
    all_to_all x1, starting transfers between devices, per_device(): summed = jnp.sum(lax.all_to_all(copies, DP, 0, 0, tiled=True), axis=0)  6.55 us
    all_to_all x1, waiting for transfers between devices, per_device(): summed = jnp.sum(lax.all_to_all(copies, DP, 0, 0, tiled=True), axis=0)  5.21 us
    all_to_all x1, starting transfers between devices, per_device(): near = lax.all_to_all(part, MP, 0, 0, axis_index_groups=NEAR, tiled=True)  5.2 us
  transfers between devices with their start and end apart: 10, of which 7 were waited for; matrix products, arithmetic and copies ran while one was open for 7% of the time, Pallas kernels for 1%

profile of v10, /device:TPU:33, one launch (start us, length us, event | category | flops | bytes accessed | tf_op | source)
XLA Modules:
  0.0 115.9 jit_solution(6643370851530813951)
XLA Ops:
  0.6 0.0 copy-start.6
  0.6 0.0 copy-start.5
  0.7 2.2 %broadcast_in_dim.7 = bf16[8,192,384]{2,1,0:T(8,128)(2,1)} broadcast(bf16[192,384]{1,0:T(8,128)(2,1)} %param.8), dimensions={1,2} | broadcast | bytes 1327104 | tf_op jit(solution)/shard_map/gather_w/broadcast_in_dim | solution.py:224
  2.8 5.0 %all-to-all-start = ((bf16[8,192,384]{2,1,0:T(8,128)(2,1)}), bf16[8,192,384]{2,1,0:T(8,128)(2,1)S(1)}, u32[]{:S(2)}, u32[]{:S(2)}) async-start(bf16[8,192,384]{2,1,0:T(8,128)(2,1)} %broadcast_in_dim.7), calls=%async_computation | async-start | bytes 2359296 | tf_op jit(solution)/shard_map/gather_w/all_to_all | solution.py:225
  7.9 0.0 copy-done.6
  7.9 0.1 pad.3.clone
  8.0 0.0 copy-done.5
  8.0 0.3 convert_reduce_fusion
  8.3 0.6 fusion.2
  8.9 16.2 %all-to-all-done.own_ref = bf16[8,192,384]{2,1,0:T(8,128)(2,1)S(1)} async-done(((bf16[8,192,384]{2,1,0:T(8,128)(2,1)}), bf16[8,192,384]{2,1,0:T(8,128)(2,1)S(1)}, u32[]{:S(2)}, u32[]{:S(2)}) %all-to-all-start) | async-done | bytes 1179680 | tf_op jit(solution)/shard_map/gather_w/all_to_all | solution.py:225
  25.1 3.5 %collective-permute-start = (bf16[8,192,384]{2,1,0:T(8,128)(2,1)S(1)}, bf16[8,192,384]{2,1,0:T(8,128)(2,1)S(1)}, u32[]{:S(2)}, u32[]{:S(2)}) collective-permute-start(bf16[8,192,384]{2,1,0:T(8,128)(2,1)S(1)} %all-to-all-done.own_ref), channel_id=1, source_target_pairs={{0,32},{32,0},{64,96},{96,64},{128,160},{160,128},{192,224},{224,1... | collective-permute-start | bytes 3538952 | tf_op jit(solution)/shard_map/gather_w/ppermute | solution.py:226
  28.6 2.1 %fusion.4 = bf16[256,3072]{1,0:T(8,128)(2,1)S(1)} fusion(bf16[256,3072]{1,0:T(8,128)(2,1)} %param.6, f32[3072]{0:T(1024)S(1)} %copy-done.6, f32[256]{0:T(256)S(1)} %add_rsqrt_fusion, f32[256]{0:T(256)S(1)} %broadcast_multiply_fusion), kind=kLoop, calls=%fused_computation.7 | loop fusion | flops 3932160 | bytes 3160064 | tf_op jit(solution)/shard_map/input_norm/convert_element_type | solution.py:233
  30.7 0.0 copy-start.3
  30.7 0.0 copy-start
  30.8 0.0 copy-start.1
  30.8 0.0 copy-start.2
  30.8 0.5 maximum_maximum_fusion.x_ref
  31.3 0.0 collective-permute-done.other_ref
  31.3 0.5 copy-done.3
  31.9 0.0 copy-done
  31.9 0.0 copy-done.1
  31.9 0.0 copy-done.2
  31.9 4.1 %head.1 = (bf16[256,128]{1,0:T(8,128)(2,1)}, bf16[256,384]{1,0:T(8,128)(2,1)S(1)}, bf16[4,1552,128]{2,1,0:T(8,128)(2,1)}, f32[8,128]{1,0:T(8,128)S(1)}) custom-call(s32[1]{0:T(128)} %bitcast.core_ref, bf16[272,3072]{1,0:T(8,128)(2,1)S(1)} %maximum_maximum_fusion.x_ref, bf16[8,192,384]{2,1,0:T(8,128)(2,1)S(1)} %all-to-all-done.own_ref, ...), custom_call_target="tpu_custom_call" | custom-call | flops 1400000000 | bytes 9000000 | tf_op jit(solution)/shard_map/head/pallas_call | solution.py:128
  36.0 0.0 copy-start.4
  36.0 5.2 %all-to-all-start.1 = ((bf16[4,1552,128]{2,1,0:T(8,128)(2,1)}), bf16[4,1552,128]{2,1,0:T(8,128)(2,1)S(1)}, u32[]{:S(2)}, u32[]{:S(2)}) async-start(bf16[4,1552,128]{2,1,0:T(8,128)(2,1)} %get-tuple-element.13), calls=%async_computation.1 | async-start | bytes 3178496 | tf_op jit(solution)/shard_map/input_gradient_near/all_to_all | solution.py:246
  41.2 0.0 copy-done.4
  41.2 1.0 convolution_convert_fusion
  42.2 0.1 select_bitcast_fusion
  42.4 2.5 %collective-permute-start.1 = (bf16[8,192,384]{2,1,0:T(8,128)(2,1)S(1)}, bf16[8,192,384]{2,1,0:T(8,128)(2,1)S(1)}, u32[]{:S(2)}, u32[]{:S(2)}) collective-permute-start(bf16[8,192,384]{2,1,0:T(8,128)(2,1)S(1)} %select_bitcast_fusion), channel_id=1, source_target_pairs={{0,32},{32,0},{64,96},{96,64},{128,160},{160,128},{192,224},{224,1... | collective-permute-start | bytes 3538952 | tf_op jit(solution)/shard_map/w_grad/ppermute | solution.py:252
  44.9 2.5 %collective-permute-done.1 = bf16[8,192,384]{2,1,0:T(8,128)(2,1)S(1)} collective-permute-done((bf16[8,192,384]{2,1,0:T(8,128)(2,1)S(1)}, bf16[8,192,384]{2,1,0:T(8,128)(2,1)S(1)}, u32[]{:S(2)}, u32[]{:S(2)}) %collective-permute-start.1) | collective-permute-done | bytes 1179680 | tf_op jit(solution)/shard_map/w_grad/ppermute | solution.py:252
  47.3 0.5 fusion.5
  47.8 14.5 %all-to-all-done.1.near_ref = bf16[4,1552,128]{2,1,0:T(8,128)(2,1)S(1)} async-done(((bf16[4,1552,128]{2,1,0:T(8,128)(2,1)}), bf16[4,1552,128]{2,1,0:T(8,128)(2,1)S(1)}, u32[]{:S(2)}, u32[]{:S(2)}) %all-to-all-start.1) | async-done | bytes 1589280 | tf_op jit(solution)/shard_map/input_gradient_near/all_to_all | solution.py:246
  62.3 1.0 sum_over_near.1
  63.3 13.9 %all-to-all-start.2 = ((bf16[8,208,128]{2,1,0:T(8,128)(2,1)}), bf16[8,208,128]{2,1,0:T(8,128)(2,1)S(1)}, u32[]{:S(2)}, u32[]{:S(2)}) async-start(bf16[8,208,128]{2,1,0:T(8,128)(2,1)} %sum_over_near.1), calls=%async_computation.2 | async-start | bytes 851968 | tf_op jit(solution)/shard_map/sum_over_near/all_to_all | solution.py:265
  77.2 0.1 dynamic-slice_bitcast_fusion.2
  77.3 1.9 %collective-permute-start.2 = (bf16[2,192,384]{2,1,0:T(8,128)(2,1)S(1)}, bf16[2,192,384]{2,1,0:T(8,128)(2,1)S(1)}, u32[]{:S(2)}, u32[]{:S(2)}) collective-permute-start(bf16[2,192,384]{2,1,0:T(8,128)(2,1)S(1)} %get-tuple-element.20), channel_id=1, source_target_pairs={{0,128},{32,160},{64,192},{96,224},{128,256},{160,288},{192,320},{... | collective-permute-start | bytes 884744 | tf_op jit(solution)/shard_map/w_grad/ppermute | solution.py:257
  79.2 2.7 %collective-permute-start.3 = (bf16[2,192,384]{2,1,0:T(8,128)(2,1)S(1)}, bf16[2,192,384]{2,1,0:T(8,128)(2,1)S(1)}, u32[]{:S(2)}, u32[]{:S(2)}) collective-permute-start(bf16[2,192,384]{2,1,0:T(8,128)(2,1)S(1)} %get-tuple-element.22), channel_id=1, source_target_pairs={{0,256},{32,288},{64,320},{96,352},{128,384},{160,416},{192,448},{... | collective-permute-start | bytes 884744 | tf_op jit(solution)/shard_map/w_grad/ppermute | solution.py:257
  81.9 3.8 %collective-permute-start.4 = (bf16[2,192,384]{2,1,0:T(8,128)(2,1)S(1)}, bf16[2,192,384]{2,1,0:T(8,128)(2,1)}, u32[]{:S(2)}, u32[]{:S(2)}) collective-permute-start(bf16[2,192,384]{2,1,0:T(8,128)(2,1)S(1)} %get-tuple-element.21), channel_id=1, source_target_pairs={{0,384},{32,416},{64,448},{96,480},{128,0},{160,32},{192,64},{224,... | collective-permute-start | bytes 884744 | tf_op jit(solution)/shard_map/w_grad/ppermute | solution.py:257
  85.8 1.0 constant_dynamic-slice_fusion
  86.8 0.1 copy.18
  86.9 0.1 dynamic-slice_bitcast_fusion.3
  86.9 0.1 copy.15.gain_ref
  87.1 7.4 %collective-permute-done.2 = bf16[2,192,384]{2,1,0:T(8,128)(2,1)S(1)} collective-permute-done((bf16[2,192,384]{2,1,0:T(8,128)(2,1)S(1)}, bf16[2,192,384]{2,1,0:T(8,128)(2,1)S(1)}, u32[]{:S(2)}, u32[]{:S(2)}) %collective-permute-start.2) | collective-permute-done | bytes 294944 | tf_op jit(solution)/shard_map/w_grad/ppermute | solution.py:257
  94.5 0.0 collective-permute-done.3
  94.5 2.6 %collective-permute-done.4 = bf16[2,192,384]{2,1,0:T(8,128)(2,1)} collective-permute-done((bf16[2,192,384]{2,1,0:T(8,128)(2,1)S(1)}, bf16[2,192,384]{2,1,0:T(8,128)(2,1)}, u32[]{:S(2)}, u32[]{:S(2)}) %collective-permute-start.4) | collective-permute-done | bytes 294944 | tf_op jit(solution)/shard_map/w_grad/ppermute | solution.py:257
  97.1 1.1 convert_add_fusion.1
  98.2 1.9 %collective-permute-start.5 = (bf16[192,384]{1,0:T(8,128)(2,1)S(1)}, bf16[192,384]{1,0:T(8,128)(2,1)S(1)}, u32[]{:S(2)}, u32[]{:S(2)}) collective-permute-start(bf16[192,384]{1,0:T(8,128)(2,1)S(1)} %fusion.7), channel_id=1, source_target_pairs={{0,64},{32,96},{64,0},{96,32},{128,192},{160,224},{192,128},{224,1... | collective-permute-start | bytes 442376 | tf_op jit(solution)/shard_map/w_grad_y/ppermute | solution.py:271
  100.2 1.4 %all-to-all-done.2.far_ref = bf16[8,208,128]{2,1,0:T(8,128)(2,1)S(1)} async-done(((bf16[8,208,128]{2,1,0:T(8,128)(2,1)}), bf16[8,208,128]{2,1,0:T(8,128)(2,1)S(1)}, u32[]{:S(2)}, u32[]{:S(2)}) %all-to-all-start.2) | async-done | bytes 426016 | tf_op jit(solution)/shard_map/sum_over_near/all_to_all | solution.py:265
  101.6 0.8 input_gradient.1
  102.3 6.6 %all-to-all-start.3 = ((f32[16,8,128]{2,1,0:T(8,128)}), f32[16,8,128]{2,1,0:T(8,128)S(1)}, u32[]{:S(2)}, u32[]{:S(2)}) async-start(f32[16,8,128]{2,1,0:T(8,128)} %get-tuple-element.17), calls=%async_computation.3 | async-start | bytes 131072 | tf_op jit(solution)/shard_map/gain_gradients/all_to_all | solution.py:283
  108.9 0.0 collective-permute-done.5
  108.9 0.7 fusion.6
  109.6 5.2 %all-to-all-done.3 = f32[16,8,128]{2,1,0:T(8,128)S(1)} async-done(((f32[16,8,128]{2,1,0:T(8,128)}), f32[16,8,128]{2,1,0:T(8,128)S(1)}, u32[]{:S(2)}, u32[]{:S(2)}) %all-to-all-start.3) | async-done | bytes 65568 | tf_op jit(solution)/shard_map/gain_gradients/all_to_all | solution.py:283
  114.8 0.5 fusion.8
  115.4 0.5 slice_bitcast_fusion.2
  (9 shorter events, 0.1 us)
Async XLA Ops:
  0.6 7.2 %copy-start.6 = (f32[3072]{0:T(1024)S(1)}, f32[3072]{0:T(1024)}, u32[]{:S(2)}) copy-start(f32[3072]{0:T(1024)} %param.7) | copy-start | bytes 36868
  0.6 7.4 %copy-start.5 = (bf16[256,3072]{1,0:T(8,128)(2,1)S(1)}, bf16[256,3072]{1,0:T(8,128)(2,1)}, u32[]{:S(2)}) copy-start(bf16[256,3072]{1,0:T(8,128)(2,1)} %param.6) | copy-start | bytes 4718596
  2.8 22.3 %all-to-all-start = ((bf16[8,192,384]{2,1,0:T(8,128)(2,1)}), bf16[8,192,384]{2,1,0:T(8,128)(2,1)S(1)}, u32[]{:S(2)}, u32[]{:S(2)}) async-start(bf16[8,192,384]{2,1,0:T(8,128)(2,1)} %broadcast_in_dim.7), calls=%async_computation | async-start | bytes 2359296 | tf_op jit(solution)/shard_map/gather_w/all_to_all | solution.py:225
  25.1 6.2 %collective-permute-start = (bf16[8,192,384]{2,1,0:T(8,128)(2,1)S(1)}, bf16[8,192,384]{2,1,0:T(8,128)(2,1)S(1)}, u32[]{:S(2)}, u32[]{:S(2)}) collective-permute-start(bf16[8,192,384]{2,1,0:T(8,128)(2,1)S(1)} %all-to-all-done.own_ref), channel_id=1, source_target_pairs={{0,32},{32,0},{64,96},{96,64},{128,160},{160,128},{192,224},{224,1... | collective-permute-start | bytes 3538952 | tf_op jit(solution)/shard_map/gather_w/ppermute | solution.py:226
  30.7 1.1 copy-start.3
  30.7 1.1 copy-start
  30.8 1.1 copy-start.1
  30.8 1.1 copy-start.2
  36.0 5.2 %copy-start.4 = (bf16[256,3072]{1,0:T(8,128)(2,1)S(1)}, bf16[256,3072]{1,0:T(8,128)(2,1)}, u32[]{:S(2)}) copy-start(bf16[256,3072]{1,0:T(8,128)(2,1)} %copy-done.3) | copy-start | bytes 4718596
  36.0 26.3 %all-to-all-start.1 = ((bf16[4,1552,128]{2,1,0:T(8,128)(2,1)}), bf16[4,1552,128]{2,1,0:T(8,128)(2,1)S(1)}, u32[]{:S(2)}, u32[]{:S(2)}) async-start(bf16[4,1552,128]{2,1,0:T(8,128)(2,1)} %get-tuple-element.13), calls=%async_computation.1 | async-start | bytes 3178496 | tf_op jit(solution)/shard_map/input_gradient_near/all_to_all | solution.py:246
  42.4 4.9 %collective-permute-start.1 = (bf16[8,192,384]{2,1,0:T(8,128)(2,1)S(1)}, bf16[8,192,384]{2,1,0:T(8,128)(2,1)S(1)}, u32[]{:S(2)}, u32[]{:S(2)}) collective-permute-start(bf16[8,192,384]{2,1,0:T(8,128)(2,1)S(1)} %select_bitcast_fusion), channel_id=1, source_target_pairs={{0,32},{32,0},{64,96},{96,64},{128,160},{160,128},{192,224},{224,1... | collective-permute-start | bytes 3538952 | tf_op jit(solution)/shard_map/w_grad/ppermute | solution.py:252
  63.3 38.3 %all-to-all-start.2 = ((bf16[8,208,128]{2,1,0:T(8,128)(2,1)}), bf16[8,208,128]{2,1,0:T(8,128)(2,1)S(1)}, u32[]{:S(2)}, u32[]{:S(2)}) async-start(bf16[8,208,128]{2,1,0:T(8,128)(2,1)} %sum_over_near.1), calls=%async_computation.2 | async-start | bytes 851968 | tf_op jit(solution)/shard_map/sum_over_near/all_to_all | solution.py:265
  77.3 17.2 %collective-permute-start.2 = (bf16[2,192,384]{2,1,0:T(8,128)(2,1)S(1)}, bf16[2,192,384]{2,1,0:T(8,128)(2,1)S(1)}, u32[]{:S(2)}, u32[]{:S(2)}) collective-permute-start(bf16[2,192,384]{2,1,0:T(8,128)(2,1)S(1)} %get-tuple-element.20), channel_id=1, source_target_pairs={{0,128},{32,160},{64,192},{96,224},{128,256},{160,288},{192,320},{... | collective-permute-start | bytes 884744 | tf_op jit(solution)/shard_map/w_grad/ppermute | solution.py:257
  79.2 15.3 %collective-permute-start.3 = (bf16[2,192,384]{2,1,0:T(8,128)(2,1)S(1)}, bf16[2,192,384]{2,1,0:T(8,128)(2,1)S(1)}, u32[]{:S(2)}, u32[]{:S(2)}) collective-permute-start(bf16[2,192,384]{2,1,0:T(8,128)(2,1)S(1)} %get-tuple-element.22), channel_id=1, source_target_pairs={{0,256},{32,288},{64,320},{96,352},{128,384},{160,416},{192,448},{... | collective-permute-start | bytes 884744 | tf_op jit(solution)/shard_map/w_grad/ppermute | solution.py:257
  81.9 15.2 %collective-permute-start.4 = (bf16[2,192,384]{2,1,0:T(8,128)(2,1)S(1)}, bf16[2,192,384]{2,1,0:T(8,128)(2,1)}, u32[]{:S(2)}, u32[]{:S(2)}) collective-permute-start(bf16[2,192,384]{2,1,0:T(8,128)(2,1)S(1)} %get-tuple-element.21), channel_id=1, source_target_pairs={{0,384},{32,416},{64,448},{96,480},{128,0},{160,32},{192,64},{224,... | collective-permute-start | bytes 884744 | tf_op jit(solution)/shard_map/w_grad/ppermute | solution.py:257
  98.2 10.7 %collective-permute-start.5 = (bf16[192,384]{1,0:T(8,128)(2,1)S(1)}, bf16[192,384]{1,0:T(8,128)(2,1)S(1)}, u32[]{:S(2)}, u32[]{:S(2)}) collective-permute-start(bf16[192,384]{1,0:T(8,128)(2,1)S(1)} %fusion.7), channel_id=1, source_target_pairs={{0,64},{32,96},{64,0},{96,32},{128,192},{160,224},{192,128},{224,1... | collective-permute-start | bytes 442376 | tf_op jit(solution)/shard_map/w_grad_y/ppermute | solution.py:271
  102.3 12.5 %all-to-all-start.3 = ((f32[16,8,128]{2,1,0:T(8,128)}), f32[16,8,128]{2,1,0:T(8,128)S(1)}, u32[]{:S(2)}, u32[]{:S(2)}) async-start(f32[16,8,128]{2,1,0:T(8,128)} %get-tuple-element.17), calls=%async_computation.3 | async-start | bytes 131072 | tf_op jit(solution)/shard_map/gain_gradients/all_to_all | solution.py:283

commit v11 on v10

--- a/solution.py
+++ b/solution.py
@@ -55,7 +55,7 @@
 
 def head_kernel(
     core_ref, x_ref, own_ref, other_ref, grad_ref, q_gain_ref, k_gain_ref,
-    context_ref, dqkv_ref, part_ref, gains_ref, full_ref,
+    context_ref, dqkv_ref, out_ref, gains_ref, full_ref, part_ref, sems,
 ):
     rows, hd = grad_ref.shape
     lane = rows // 2
@@ -99,6 +99,29 @@
     )
     dqkv_ref[...] = dqkv
 
+    row = lax.broadcasted_iota(jnp.int32, (8, columns), 0)
+    w_hi, w_lo = hi_lo(jnp.where(row % 2 == 0, weighted, 0.0))
+    ones = jnp.where(row % 2 == 1, 1.0, 0.0).astype(BF)
+    p_hi, p_lo = hi_lo(dqkv.astype(F32) * raw)
+    sums = (dot(w_hi, dqkv, 1, 1) + dot(w_lo, dqkv, 1, 1)) + (
+        dot(ones, p_hi, 1, 1) + dot(ones, p_lo, 1, 1)
+    )
+    packed = pack(jnp.concatenate([sums[:, :lane], sums[:, lane:]], axis=0))
+    for group in range(4):
+        part_ref[group, 2 * blocks * share :] = packed
+
+    copies = []
+
+    def leave(index, at, size):
+        rows_at = pl.ds(at, size)
+        copy = pltpu.make_async_copy(
+            part_ref.at[:, rows_at], out_ref.at[:, rows_at], sems.at[index]
+        )
+        copy.start()
+        copies.append(copy)
+
+    leave(blocks, 2 * blocks * share, 16)
+
     for k in range(blocks):
         pair = full_ref[2 * k : 2 * k + 2].reshape(2 * w_rows, columns)
         part = dot(pair, dqkv, 1, 1).astype(BF)
@@ -108,17 +131,9 @@
                 part_ref[group, at : at + share] = part[
                     group * share : (group + 1) * share, half * lane : (half + 1) * lane
                 ]
-
-    row = lax.broadcasted_iota(jnp.int32, (8, columns), 0)
-    w_hi, w_lo = hi_lo(jnp.where(row % 2 == 0, weighted, 0.0))
-    ones = jnp.where(row % 2 == 1, 1.0, 0.0).astype(BF)
-    p_hi, p_lo = hi_lo(dqkv.astype(F32) * raw)
-    sums = (dot(w_hi, dqkv, 1, 1) + dot(w_lo, dqkv, 1, 1)) + (
-        dot(ones, p_hi, 1, 1) + dot(ones, p_lo, 1, 1)
-    )
-    packed = pack(jnp.concatenate([sums[:, :lane], sums[:, lane:]], axis=0))
-    for group in range(4):
-        part_ref[group, 2 * blocks * share :] = packed
+        leave(k, 2 * k * share, 2 * share)
+    for copy in copies:
+        copy.wait()
 
 
 def run_head(core, x, own, other, grad, q_gain, k_gain):
@@ -128,14 +143,18 @@
     return pl.pallas_call(
         head_kernel,
         in_specs=[pl.BlockSpec(memory_space=pltpu.SMEM)] + [vmem] * 6,
-        out_specs=[vmem] * 4,
+        out_specs=[vmem, vmem, pl.BlockSpec(memory_space=pl.ANY), vmem],
         out_shape=[
             jax.ShapeDtypeStruct((rows, hd), BF),
             jax.ShapeDtypeStruct((rows, columns), BF),
             jax.ShapeDtypeStruct((4, blocks * w_rows + 16, rows // 2), BF),
             jax.ShapeDtypeStruct((8, hd), F32),
         ],
-        scratch_shapes=[pltpu.VMEM((2 * blocks, w_rows, columns), BF)],
+        scratch_shapes=[
+            pltpu.VMEM((2 * blocks, w_rows, columns), BF),
+            pltpu.VMEM((4, blocks * w_rows + 16, rows // 2), BF),
+            pltpu.SemaphoreType.DMA((blocks + 1,)),
+        ],
         compiler_params=pltpu.CompilerParams(vmem_limit_bytes=48 * 2**20),
         cost_estimate=pl.CostEstimate(
             flops=1_400_000_000, bytes_accessed=9_000_000, transcendentals=65536
@@ -253,15 +272,18 @@
         chip = (term_keep.astype(F32) + term_got.astype(F32)).astype(BF)
         chip = chip.reshape(NX, NYL, w_rows, columns)
         x_term = lax.dynamic_index_in_dim(chip, x_at, 0, False).astype(F32)
-        x_got = [
-            lax.ppermute(
-                lax.dynamic_index_in_dim(chip, (x_at + step) % NX, 0, False), DP, pairs
-            )
-            for step, pairs in enumerate(X_STEPS, 1)
+        leaves = [
+            lax.dynamic_index_in_dim(chip, (x_at + step) % NX, 0, False) for step in range(1, NX)
         ]
+        x_got = [lax.ppermute(leaf, DP, pairs) for leaf, pairs in zip(leaves, X_STEPS)]
 
     with jax.named_scope("sum_over_near"):
-        pair = sum_near(near, [chip])
+        start = mp * share
+        tokens_share = lax.dynamic_slice_in_dim(tokens, start, share, 1).astype(F32)
+        xhat_share = ((tokens_share - mean) * inverse).T
+        gain_share = lax.dynamic_slice_in_dim(layer_norm_gain, start, share, 0)[:, None]
+        inverse_row = inverse.T
+        pair = sum_near(near, leaves + [xhat_share, gain_share, inverse_row])
         far = lax.all_to_all(pair, MP, 0, 0, axis_index_groups=FAR, tiled=True)
 
     with jax.named_scope("w_grad_y"):
@@ -271,13 +293,7 @@
         w_grad = (stays + lax.ppermute(leaves, DP, YLO_SWAP).astype(F32)).astype(BF)
 
     with jax.named_scope("input_gradient"):
-        start = mp * share
-        tokens_share = lax.dynamic_slice_in_dim(tokens, start, share, 1).astype(F32)
-        xhat_share = ((tokens_share - mean) * inverse).T
-        gain_share = lax.dynamic_slice_in_dim(layer_norm_gain, start, share, 0)
-        gradient, copies = finish(
-            width, far, xhat_share, gain_share[:, None], inverse.T, head_gains
-        )
+        gradient, copies = finish(width, far, xhat_share, gain_share, inverse_row, head_gains)
 
     with jax.named_scope("gain_gradients"):
         summed = jnp.sum(lax.all_to_all(copies, DP, 0, 0, tiled=True), axis=0)

time: 117 us -> 117 us (level)
  waiting for transfers between devices: 49.8 us -> 45.3 us
  other arithmetic: 5.98 us -> 8.84 us
  local copies, waits for them, and re-layouts: 5.26 us -> 6.57 us
    all_to_all x1, waiting for transfers between devices: 14.5 us -> 9.78 us  [per_device(): near = lax.all_to_all(part, MP, 0, 0, axis_index_groups=NEAR, tiled=True)]
    convert_element_type x1, other arithmetic: 0.47 us -> 2.2 us  [per_device(): chip = (term_keep.astype(F32) + term_got.astype(F32)).astype(BF)]
    unnamed x15, local copies, waits for them, and re-layouts: 0.67 us -> 1.98 us
    ppermute x3, waiting for transfers between devices: 10.1 us -> 11.4 us  [per_device(): lax.ppermute(leaf, DP, pairs)]
    ppermute x1, waiting for transfers between devices: 2.45 us -> 1.26 us  [per_device(): term_got = lax.ppermute(term_send, DP, CORE_SWAP)]
  transfers between devices with their start and end apart: 10 -> 10, of which waited for: 7 -> 7; matrix products, arithmetic and copies ran while one was open for 7% -> 10% of each run, Pallas kernels for 1% -> 1%
where the time goes in v11:
time: 117 us; the launch traced here: 116 us
  starting transfers between devices  46.9 us (40%)
  waiting for transfers between devices  45.3 us (39%)
  other arithmetic  8.84 us (8%)
  local copies, waits for them, and re-layouts  6.57 us (6%)
  Pallas kernels  6.38 us (5%)
    all_to_all x1, waiting for transfers between devices, per_device(): lax.all_to_all(copies, DP, 0, 0, axis_index_groups=SAME_CORE, tiled=True)  16.2 us
    all_to_all x1, starting transfers between devices, per_device(): far = lax.all_to_all(pair, MP, 0, 0, axis_index_groups=FAR, tiled=True)  13.9 us
    ppermute x3, waiting for transfers between devices, per_device(): lax.ppermute(leaf, DP, pairs)  11.4 us
    all_to_all x1, waiting for transfers between devices, per_device(): near = lax.all_to_all(part, MP, 0, 0, axis_index_groups=NEAR, tiled=True)  9.78 us
    ppermute x3, starting transfers between devices, per_device(): lax.ppermute(leaf, DP, pairs)  8.4 us
    all_to_all x1, starting transfers between devices, per_device(): summed = jnp.sum(lax.all_to_all(copies, DP, 0, 0, tiled=True), axis=0)  6.57 us
    all_to_all x1, waiting for transfers between devices, per_device(): summed = jnp.sum(lax.all_to_all(copies, DP, 0, 0, tiled=True), axis=0)  5.21 us
    all_to_all x1, starting transfers between devices, per_device(): near = lax.all_to_all(part, MP, 0, 0, axis_index_groups=NEAR, tiled=True)  5.08 us
  transfers between devices with their start and end apart: 10, of which 7 were waited for; matrix products, arithmetic and copies ran while one was open for 10% of the time, Pallas kernels for 1%

profile of v11, /device:TPU:33, one launch (start us, length us, event | category | flops | bytes accessed | tf_op | source)
XLA Modules:
  0.0 116.0 jit_solution(8142938378381439525)
XLA Ops:
  0.6 0.0 copy-start.6
  0.6 0.0 copy-start.4
  0.7 2.2 %broadcast_in_dim.7 = bf16[8,192,384]{2,1,0:T(8,128)(2,1)} broadcast(bf16[192,384]{1,0:T(8,128)(2,1)} %param.8), dimensions={1,2} | broadcast | bytes 1327104 | tf_op jit(solution)/shard_map/gather_w/broadcast_in_dim | solution.py:243
  2.8 5.0 %all-to-all-start = ((bf16[8,192,384]{2,1,0:T(8,128)(2,1)}), bf16[8,192,384]{2,1,0:T(8,128)(2,1)S(1)}, u32[]{:S(2)}, u32[]{:S(2)}) async-start(bf16[8,192,384]{2,1,0:T(8,128)(2,1)} %broadcast_in_dim.7), calls=%async_computation | async-start | bytes 2359296 | tf_op jit(solution)/shard_map/gather_w/all_to_all | solution.py:244
  7.9 0.0 copy-done.6
  7.9 0.1 pad.3.clone
  8.0 0.0 copy-done.4
  8.0 0.3 convert_reduce_fusion
  8.3 0.6 fusion.2
  8.9 16.2 %all-to-all-done.own_ref = bf16[8,192,384]{2,1,0:T(8,128)(2,1)S(1)} async-done(((bf16[8,192,384]{2,1,0:T(8,128)(2,1)}), bf16[8,192,384]{2,1,0:T(8,128)(2,1)S(1)}, u32[]{:S(2)}, u32[]{:S(2)}) %all-to-all-start) | async-done | bytes 1179680 | tf_op jit(solution)/shard_map/gather_w/all_to_all | solution.py:244
  25.1 3.5 %collective-permute-start = (bf16[8,192,384]{2,1,0:T(8,128)(2,1)S(1)}, bf16[8,192,384]{2,1,0:T(8,128)(2,1)S(1)}, u32[]{:S(2)}, u32[]{:S(2)}) collective-permute-start(bf16[8,192,384]{2,1,0:T(8,128)(2,1)S(1)} %all-to-all-done.own_ref), channel_id=1, source_target_pairs={{0,32},{32,0},{64,96},{96,64},{128,160},{160,128},{192,224},{224,1... | collective-permute-start | bytes 3538952 | tf_op jit(solution)/shard_map/gather_w/ppermute | solution.py:245
  28.6 2.1 %fusion.4 = bf16[256,3072]{1,0:T(8,128)(2,1)S(1)} fusion(bf16[256,3072]{1,0:T(8,128)(2,1)} %param.6, f32[3072]{0:T(1024)S(1)} %copy-done.6, f32[256]{0:T(256)S(1)} %add_rsqrt_fusion, f32[256]{0:T(256)S(1)} %broadcast_multiply_fusion), kind=kLoop, calls=%fused_computation.7 | loop fusion | flops 3932160 | bytes 3160064 | tf_op jit(solution)/shard_map/input_norm/convert_element_type | solution.py:252
  30.7 0.0 copy-start
  30.7 0.0 copy-start.1
  30.8 0.0 copy-start.2
  30.8 0.5 maximum_maximum_fusion.x_ref
  31.3 0.0 collective-permute-done.other_ref
  31.3 0.2 copy-done
  31.6 0.0 copy-done.1
  31.6 0.0 copy-done.2
  31.6 4.6 %head.1 = (bf16[256,128]{1,0:T(8,128)(2,1)}, bf16[256,384]{1,0:T(8,128)(2,1)S(1)}, bf16[4,1552,128]{2,1,0:T(8,128)(2,1)}, f32[8,128]{1,0:T(8,128)S(1)}) custom-call(s32[1]{0:T(128)} %bitcast.core_ref, bf16[272,3072]{1,0:T(8,128)(2,1)S(1)} %maximum_maximum_fusion.x_ref, bf16[8,192,384]{2,1,0:T(8,128)(2,1)S(1)} %all-to-all-done.own_ref, ...), custom_call_target="tpu_custom_call" | custom-call | flops 1400000000 | bytes 9000000 | tf_op jit(solution)/shard_map/head/pallas_call | solution.py:143
  36.2 5.1 %all-to-all-start.1 = ((bf16[4,1552,128]{2,1,0:T(8,128)(2,1)}), bf16[4,1552,128]{2,1,0:T(8,128)(2,1)S(1)}, u32[]{:S(2)}, u32[]{:S(2)}) async-start(bf16[4,1552,128]{2,1,0:T(8,128)(2,1)} %get-tuple-element.13), calls=%async_computation.1 | async-start | bytes 3178496 | tf_op jit(solution)/shard_map/input_gradient_near/all_to_all | solution.py:265
  41.3 1.0 convolution_convert_fusion
  42.3 0.0 copy-start.3
  42.3 1.2 %select_bitcast_fusion = bf16[8,192,384]{2,1,0:T(8,128)(2,1)} fusion(pred[]{:T(512)S(6)} %eq.14, bf16[8,2,192,384]{3,2,1,0:T(8,128)(2,1)S(1)} %bitcast.47), kind=kLoop, calls=%fused_computation.13 | loop fusion | flops 589824 | bytes 3538945 | tf_op jit(solution)/shard_map/w_grad/jit(_where)/select_n | solution.py:270
  43.6 0.6 copy-done.3
  44.2 2.5 %collective-permute-start.1 = (bf16[8,192,384]{2,1,0:T(8,128)(2,1)}, bf16[8,192,384]{2,1,0:T(8,128)(2,1)S(1)}, u32[]{:S(2)}, u32[]{:S(2)}) collective-permute-start(bf16[8,192,384]{2,1,0:T(8,128)(2,1)} %select_bitcast_fusion), channel_id=1, source_target_pairs={{0,32},{32,0},{64,96},{96,64},{128,160},{160,128},{192,224},{224,1... | collective-permute-start | bytes 3538952 | tf_op jit(solution)/shard_map/w_grad/ppermute | solution.py:271
  46.7 1.0 constant_dynamic-slice_fusion
  47.7 0.1 copy.19
  47.8 0.1 dynamic-slice_bitcast_fusion.3
  47.9 0.1 copy.15.refs_4_.gain_ref
  48.0 1.3 %collective-permute-done.1 = bf16[8,192,384]{2,1,0:T(8,128)(2,1)S(1)} collective-permute-done((bf16[8,192,384]{2,1,0:T(8,128)(2,1)}, bf16[8,192,384]{2,1,0:T(8,128)(2,1)S(1)}, u32[]{:S(2)}, u32[]{:S(2)}) %collective-permute-start.1) | collective-permute-done | bytes 1179680 | tf_op jit(solution)/shard_map/w_grad/ppermute | solution.py:271
  49.3 2.2 %fusion.5 = bf16[8,192,384]{2,1,0:T(8,128)(2,1)S(1)} fusion(bf16[8,192,384]{2,1,0:T(8,128)(2,1)S(1)} %collective-permute-done.1, pred[]{:T(512)S(6)} %eq.14, bf16[8,2,192,384]{3,2,1,0:T(8,128)(2,1)} %bitcast.48), kind=kLoop, calls=%fused_computation.9 | loop fusion | flops 2949120 | bytes 4718593 | tf_op jit(solution)/shard_map/w_grad/convert_element_type | solution.py:272
  51.5 0.0 copy-start.5
  51.5 1.0 copy-done.5
  52.5 0.1 dynamic-slice_bitcast_fusion
  52.6 9.8 %all-to-all-done.1.near_ref = bf16[4,1552,128]{2,1,0:T(8,128)(2,1)S(1)} async-done(((bf16[4,1552,128]{2,1,0:T(8,128)(2,1)}), bf16[4,1552,128]{2,1,0:T(8,128)(2,1)S(1)}, u32[]{:S(2)}, u32[]{:S(2)}) %all-to-all-start.1) | async-done | bytes 1589280 | tf_op jit(solution)/shard_map/input_gradient_near/all_to_all | solution.py:265
  62.4 1.0 sum_over_near.1
  63.4 13.9 %all-to-all-start.2 = ((bf16[8,208,128]{2,1,0:T(8,128)(2,1)}), bf16[8,208,128]{2,1,0:T(8,128)(2,1)S(1)}, u32[]{:S(2)}, u32[]{:S(2)}) async-start(bf16[8,208,128]{2,1,0:T(8,128)(2,1)} %sum_over_near.1), calls=%async_computation.2 | async-start | bytes 851968 | tf_op jit(solution)/shard_map/sum_over_near/all_to_all | solution.py:287
  77.3 1.9 %collective-permute-start.2 = (bf16[2,192,384]{2,1,0:T(8,128)(2,1)S(1)}, bf16[2,192,384]{2,1,0:T(8,128)(2,1)S(1)}, u32[]{:S(2)}, u32[]{:S(2)}) collective-permute-start(bf16[2,192,384]{2,1,0:T(8,128)(2,1)S(1)} %get-tuple-element.22.refs_0_), channel_id=1, source_target_pairs={{0,128},{32,160},{64,192},{96,224},{128,256},{160,288},{192,320},{... | collective-permute-start | bytes 884744 | tf_op jit(solution)/shard_map/w_grad/ppermute | solution.py:278
  79.2 2.7 %collective-permute-start.3 = (bf16[2,192,384]{2,1,0:T(8,128)(2,1)S(1)}, bf16[2,192,384]{2,1,0:T(8,128)(2,1)S(1)}, u32[]{:S(2)}, u32[]{:S(2)}) collective-permute-start(bf16[2,192,384]{2,1,0:T(8,128)(2,1)S(1)} %get-tuple-element.21.refs_1_), channel_id=1, source_target_pairs={{0,256},{32,288},{64,320},{96,352},{128,384},{160,416},{192,448},{... | collective-permute-start | bytes 884744 | tf_op jit(solution)/shard_map/w_grad/ppermute | solution.py:278
  81.9 3.8 %collective-permute-start.4 = (bf16[2,192,384]{2,1,0:T(8,128)(2,1)S(1)}, bf16[2,192,384]{2,1,0:T(8,128)(2,1)S(1)}, u32[]{:S(2)}, u32[]{:S(2)}) collective-permute-start(bf16[2,192,384]{2,1,0:T(8,128)(2,1)S(1)} %get-tuple-element.20.refs_2_), channel_id=1, source_target_pairs={{0,384},{32,416},{64,448},{96,480},{128,0},{160,32},{192,64},{224,... | collective-permute-start | bytes 884744 | tf_op jit(solution)/shard_map/w_grad/ppermute | solution.py:278
  85.7 8.7 %collective-permute-done.2 = bf16[2,192,384]{2,1,0:T(8,128)(2,1)S(1)} collective-permute-done((bf16[2,192,384]{2,1,0:T(8,128)(2,1)S(1)}, bf16[2,192,384]{2,1,0:T(8,128)(2,1)S(1)}, u32[]{:S(2)}, u32[]{:S(2)}) %collective-permute-start.2) | collective-permute-done | bytes 294944 | tf_op jit(solution)/shard_map/w_grad/ppermute | solution.py:278
  94.5 0.0 collective-permute-done.3
  94.5 2.6 %collective-permute-done.4 = bf16[2,192,384]{2,1,0:T(8,128)(2,1)S(1)} collective-permute-done((bf16[2,192,384]{2,1,0:T(8,128)(2,1)S(1)}, bf16[2,192,384]{2,1,0:T(8,128)(2,1)S(1)}, u32[]{:S(2)}, u32[]{:S(2)}) %collective-permute-start.4) | collective-permute-done | bytes 294944 | tf_op jit(solution)/shard_map/w_grad/ppermute | solution.py:278
  97.1 1.1 convert_add_fusion.1
  98.3 1.9 %collective-permute-start.5 = (bf16[192,384]{1,0:T(8,128)(2,1)S(1)}, bf16[192,384]{1,0:T(8,128)(2,1)S(1)}, u32[]{:S(2)}, u32[]{:S(2)}) collective-permute-start(bf16[192,384]{1,0:T(8,128)(2,1)S(1)} %fusion.7), channel_id=1, source_target_pairs={{0,64},{32,96},{64,0},{96,32},{128,192},{160,224},{192,128},{224,1... | collective-permute-start | bytes 442376 | tf_op jit(solution)/shard_map/w_grad_y/ppermute | solution.py:293
  100.2 1.5 %all-to-all-done.2.far_ref = bf16[8,208,128]{2,1,0:T(8,128)(2,1)S(1)} async-done(((bf16[8,208,128]{2,1,0:T(8,128)(2,1)}), bf16[8,208,128]{2,1,0:T(8,128)(2,1)S(1)}, u32[]{:S(2)}, u32[]{:S(2)}) %all-to-all-start.2) | async-done | bytes 426016 | tf_op jit(solution)/shard_map/sum_over_near/all_to_all | solution.py:287
  101.7 0.8 input_gradient.1
  102.4 6.6 %all-to-all-start.3 = ((f32[16,8,128]{2,1,0:T(8,128)}), f32[16,8,128]{2,1,0:T(8,128)S(1)}, u32[]{:S(2)}, u32[]{:S(2)}) async-start(f32[16,8,128]{2,1,0:T(8,128)} %get-tuple-element.17), calls=%async_computation.3 | async-start | bytes 131072 | tf_op jit(solution)/shard_map/gain_gradients/all_to_all | solution.py:299
  109.0 0.0 collective-permute-done.5
  109.0 0.7 fusion.6
  109.7 5.2 %all-to-all-done.3 = f32[16,8,128]{2,1,0:T(8,128)S(1)} async-done(((f32[16,8,128]{2,1,0:T(8,128)}), f32[16,8,128]{2,1,0:T(8,128)S(1)}, u32[]{:S(2)}, u32[]{:S(2)}) %all-to-all-start.3) | async-done | bytes 65568 | tf_op jit(solution)/shard_map/gain_gradients/all_to_all | solution.py:299
  114.9 0.5 fusion.8
  115.5 0.5 slice_bitcast_fusion.2
  (9 shorter events, 0.1 us)
Async XLA Ops:
  0.6 7.2 %copy-start.6 = (f32[3072]{0:T(1024)S(1)}, f32[3072]{0:T(1024)}, u32[]{:S(2)}) copy-start(f32[3072]{0:T(1024)} %param.7) | copy-start | bytes 36868
  0.6 7.4 %copy-start.4 = (bf16[256,3072]{1,0:T(8,128)(2,1)S(1)}, bf16[256,3072]{1,0:T(8,128)(2,1)}, u32[]{:S(2)}) copy-start(bf16[256,3072]{1,0:T(8,128)(2,1)} %param.6) | copy-start | bytes 4718596
  2.8 22.3 %all-to-all-start = ((bf16[8,192,384]{2,1,0:T(8,128)(2,1)}), bf16[8,192,384]{2,1,0:T(8,128)(2,1)S(1)}, u32[]{:S(2)}, u32[]{:S(2)}) async-start(bf16[8,192,384]{2,1,0:T(8,128)(2,1)} %broadcast_in_dim.7), calls=%async_computation | async-start | bytes 2359296 | tf_op jit(solution)/shard_map/gather_w/all_to_all | solution.py:244
  25.1 6.2 %collective-permute-start = (bf16[8,192,384]{2,1,0:T(8,128)(2,1)S(1)}, bf16[8,192,384]{2,1,0:T(8,128)(2,1)S(1)}, u32[]{:S(2)}, u32[]{:S(2)}) collective-permute-start(bf16[8,192,384]{2,1,0:T(8,128)(2,1)S(1)} %all-to-all-done.own_ref), channel_id=1, source_target_pairs={{0,32},{32,0},{64,96},{96,64},{128,160},{160,128},{192,224},{224,1... | collective-permute-start | bytes 3538952 | tf_op jit(solution)/shard_map/gather_w/ppermute | solution.py:245
  30.7 0.8 copy-start
  30.7 0.8 copy-start.1
  30.8 0.8 copy-start.2
  36.2 26.2 %all-to-all-start.1 = ((bf16[4,1552,128]{2,1,0:T(8,128)(2,1)}), bf16[4,1552,128]{2,1,0:T(8,128)(2,1)S(1)}, u32[]{:S(2)}, u32[]{:S(2)}) async-start(bf16[4,1552,128]{2,1,0:T(8,128)(2,1)} %get-tuple-element.13), calls=%async_computation.1 | async-start | bytes 3178496 | tf_op jit(solution)/shard_map/input_gradient_near/all_to_all | solution.py:265
  42.3 1.8 %copy-start.3 = (bf16[3072,384]{1,0:T(8,128)(2,1)}, bf16[3072,384]{1,0:T(8,128)(2,1)S(1)}, u32[]{:S(2)}) copy-start(bf16[3072,384]{1,0:T(8,128)(2,1)S(1)} %convolution_convert_fusion) | copy-start | bytes 7077892
  44.2 5.1 %collective-permute-start.1 = (bf16[8,192,384]{2,1,0:T(8,128)(2,1)}, bf16[8,192,384]{2,1,0:T(8,128)(2,1)S(1)}, u32[]{:S(2)}, u32[]{:S(2)}) collective-permute-start(bf16[8,192,384]{2,1,0:T(8,128)(2,1)} %select_bitcast_fusion), channel_id=1, source_target_pairs={{0,32},{32,0},{64,96},{96,64},{128,160},{160,128},{192,224},{224,1... | collective-permute-start | bytes 3538952 | tf_op jit(solution)/shard_map/w_grad/ppermute | solution.py:271
  51.5 1.0 copy-start.5
  63.4 38.3 %all-to-all-start.2 = ((bf16[8,208,128]{2,1,0:T(8,128)(2,1)}), bf16[8,208,128]{2,1,0:T(8,128)(2,1)S(1)}, u32[]{:S(2)}, u32[]{:S(2)}) async-start(bf16[8,208,128]{2,1,0:T(8,128)(2,1)} %sum_over_near.1), calls=%async_computation.2 | async-start | bytes 851968 | tf_op jit(solution)/shard_map/sum_over_near/all_to_all | solution.py:287
  77.3 17.2 %collective-permute-start.2 = (bf16[2,192,384]{2,1,0:T(8,128)(2,1)S(1)}, bf16[2,192,384]{2,1,0:T(8,128)(2,1)S(1)}, u32[]{:S(2)}, u32[]{:S(2)}) collective-permute-start(bf16[2,192,384]{2,1,0:T(8,128)(2,1)S(1)} %get-tuple-element.22.refs_0_), channel_id=1, source_target_pairs={{0,128},{32,160},{64,192},{96,224},{128,256},{160,288},{192,320},{... | collective-permute-start | bytes 884744 | tf_op jit(solution)/shard_map/w_grad/ppermute | solution.py:278
  79.2 15.3 %collective-permute-start.3 = (bf16[2,192,384]{2,1,0:T(8,128)(2,1)S(1)}, bf16[2,192,384]{2,1,0:T(8,128)(2,1)S(1)}, u32[]{:S(2)}, u32[]{:S(2)}) collective-permute-start(bf16[2,192,384]{2,1,0:T(8,128)(2,1)S(1)} %get-tuple-element.21.refs_1_), channel_id=1, source_target_pairs={{0,256},{32,288},{64,320},{96,352},{128,384},{160,416},{192,448},{... | collective-permute-start | bytes 884744 | tf_op jit(solution)/shard_map/w_grad/ppermute | solution.py:278
  81.9 15.2 %collective-permute-start.4 = (bf16[2,192,384]{2,1,0:T(8,128)(2,1)S(1)}, bf16[2,192,384]{2,1,0:T(8,128)(2,1)S(1)}, u32[]{:S(2)}, u32[]{:S(2)}) collective-permute-start(bf16[2,192,384]{2,1,0:T(8,128)(2,1)S(1)} %get-tuple-element.20.refs_2_), channel_id=1, source_target_pairs={{0,384},{32,416},{64,448},{96,480},{128,0},{160,32},{192,64},{224,... | collective-permute-start | bytes 884744 | tf_op jit(solution)/shard_map/w_grad/ppermute | solution.py:278
  98.3 10.7 %collective-permute-start.5 = (bf16[192,384]{1,0:T(8,128)(2,1)S(1)}, bf16[192,384]{1,0:T(8,128)(2,1)S(1)}, u32[]{:S(2)}, u32[]{:S(2)}) collective-permute-start(bf16[192,384]{1,0:T(8,128)(2,1)S(1)} %fusion.7), channel_id=1, source_target_pairs={{0,64},{32,96},{64,0},{96,32},{128,192},{160,224},{192,128},{224,1... | collective-permute-start | bytes 442376 | tf_op jit(solution)/shard_map/w_grad_y/ppermute | solution.py:293
  102.4 12.5 %all-to-all-start.3 = ((f32[16,8,128]{2,1,0:T(8,128)}), f32[16,8,128]{2,1,0:T(8,128)S(1)}, u32[]{:S(2)}, u32[]{:S(2)}) async-start(f32[16,8,128]{2,1,0:T(8,128)} %get-tuple-element.17), calls=%async_computation.3 | async-start | bytes 131072 | tf_op jit(solution)/shard_map/gain_gradients/all_to_all | solution.py:299
